TPU v7x, 32 devices: a whole 2x2x4 slice. The times are simulated.
32 devices in a mesh: dp: 8 (over z, x), tensor: 4 (over y, core).
Axes of the slice: x: 2, y: 2, z: 4, core: 2. Of those that a mesh axis runs over, the one named last changes fastest.
Arguments:
- tokens: bfloat16 [16384, 1024], P(('dp', 'tensor')), may hold values from -6 to 6
- lengths: int32 [16], P('dp'), may hold values from 256 to 1024, as said below
- routes: int32 [16384, 8], P('dp'), may hold values from 0 to 31, all different within a row; in each aligned block of 512 rows (0 to 511, 512 to 1023, ...) at most 136 rows name the same one
- gain_attn: float32 [1024], replicated, may hold values from 0.5 to 1.5
- w_query: bfloat16 [1024, 1024], P('dp', 'tensor'), may hold values from -0.1875 to 0.1875
- w_keyvalue: bfloat16 [1024, 2, 512], P('dp', None, 'tensor'), may hold values from -0.1875 to 0.1875
- w_out: bfloat16 [1024, 1024], P('dp', 'tensor'), may hold values from -3 to 3
- gain_mixer: float32 [1024], replicated, may hold values from 0.5 to 1.5
- w_router: bfloat16 [1024, 32], replicated, may hold values from -0.09375 to 0.09375
- w_gate: bfloat16 [1024, 32, 512], P('dp', None, 'tensor'), may hold values from -0.1875 to 0.1875
- w_up: bfloat16 [1024, 32, 512], P('dp', None, 'tensor'), may hold values from -0.1875 to 0.1875
- w_down: bfloat16 [1024, 32, 512], P('dp', None, 'tensor'), may hold values from -1 to 1
- out_grad: bfloat16 [16384, 1024], P(('dp', 'tensor')), may hold values from -6 to 6
Outputs:
- mixed: bfloat16 [16384, 1024], P(('dp', 'tensor'))
- grad_tokens: bfloat16 [16384, 1024], P(('dp', 'tensor'))
- grad_gain_attn: float32 [1024], replicated
- grad_w_query: float32 [1024, 1024], P('dp', 'tensor')
- grad_w_keyvalue: float32 [1024, 2, 512], P('dp', None, 'tensor')
- grad_w_out: float32 [1024, 1024], P('dp', 'tensor')
- grad_gain_mixer: float32 [1024], replicated
- grad_w_router: float32 [1024, 32], replicated
- grad_w_gate: float32 [1024, 32, 512], P('dp', None, 'tensor')
- grad_w_up: float32 [1024, 32, 512], P('dp', None, 'tensor')
- grad_w_down: float32 [1024, 32, 512], P('dp', None, 'tensor')
Inputs may be any that keep to these rules, and one draw needn't show every extreme that they name: `lengths`: every sequence has at least 256 live tokens; in every draw some sequence is full and some has exactly 256. `routes`: each row names 8 different experts; within each aligned block of 512 rows (the token slots of one device) no expert is named by more than 136 rows, and in every draw some expert reaches 136 in some block.
All inputs are finite; a program needn't handle non-finite values.
Results may differ from a plain program's by a relative error of at most 0.023.
Values may be sent and summed in bfloat16 or wider, within the bound.
A program may use at most 576 MiB of HBM per device.

v0:
```python
import math

import jax
import jax.numpy as jnp
from jax import lax
from jax.sharding import PartitionSpec as P

HD = 64


epsilon = 1e-06
rope_base = 10000.0
highest = lax.Precision.HIGHEST


def rotary_tables(positions, head_size):
    half_size = head_size // 2
    exponent = 2.0 * jnp.arange(half_size, dtype=jnp.float32) / head_size
    frequency = jnp.exp(-math.log(rope_base) * exponent)
    angles = positions.astype(jnp.float32)[:, None] * frequency[None, :]
    return (jnp.cos(angles), jnp.sin(angles))


def rotate(vectors, cosine_table, sine_table):
    half_size = vectors.shape[-1] // 2
    first_half = vectors[..., :half_size]
    second_half = vectors[..., half_size:]
    cos_rows = cosine_table[:, None, :]
    sin_rows = sine_table[:, None, :]
    return jnp.concatenate(
        [
            first_half * cos_rows - second_half * sin_rows,
            second_half * cos_rows + first_half * sin_rows,
        ],
        axis=-1,
    )


def unrotate(grad_rows, cosine_table, sine_table):
    half_size = grad_rows.shape[-1] // 2
    first_half = grad_rows[..., :half_size]
    second_half = grad_rows[..., half_size:]
    cos_rows = cosine_table[:, None, :]
    sin_rows = sine_table[:, None, :]
    return jnp.concatenate(
        [
            first_half * cos_rows + second_half * sin_rows,
            second_half * cos_rows - first_half * sin_rows,
        ],
        axis=-1,
    )


def masked_scores(query_blk, keys_blk, block_start, seq_length):
    raw_scores = jnp.einsum(
        "qgrd,kgd->grqk", query_blk, keys_blk, preferred_element_type=jnp.float32
    )
    scaled = raw_scores * (1.0 / math.sqrt(query_blk.shape[-1]))
    query_pos = block_start + jnp.arange(query_blk.shape[0], dtype=jnp.int32)
    key_pos = jnp.arange(keys_blk.shape[0], dtype=jnp.int32)
    allowed = (key_pos[None, :] <= query_pos[:, None]) & (key_pos[None, :] < seq_length)
    return jnp.where(allowed[None, None], scaled, -1e30)


def attend_sequence(operands):
    query_seq, keys_seq, values_seq, seq_length = operands
    seq_len = query_seq.shape[0]
    block_len = min(512, seq_len)
    outputs = []
    log_sums = []
    for block_id in range(seq_len // block_len):
        block_start = block_id * block_len
        block_stop = block_start + block_len
        scores = masked_scores(
            query_seq[block_start:block_stop], keys_seq[:block_stop], block_start, seq_length
        )
        row_peak = jnp.max(scores, axis=-1, keepdims=True)
        exp_scores = jnp.exp(scores - row_peak)
        totals = jnp.sum(exp_scores, axis=-1, keepdims=True)
        attn_weights = (exp_scores / totals).astype(jnp.bfloat16)
        context = jnp.einsum(
            "grqk,kgd->qgrd",
            attn_weights,
            values_seq[:block_stop],
            preferred_element_type=jnp.float32,
        )
        outputs.append(context.astype(jnp.bfloat16))
        log_sums.append(row_peak[..., 0] + jnp.log(totals[..., 0]))
    return (jnp.concatenate(outputs, axis=0), jnp.concatenate(log_sums, axis=2))


def sequence_backward(operands):
    query_seq, keys_seq, values_seq, grad_ctx, log_sums, seq_length = operands
    seq_len = query_seq.shape[0]
    block_len = min(512, seq_len)
    scale = 1.0 / math.sqrt(query_seq.shape[-1])
    grad_keys = jnp.zeros(keys_seq.shape, jnp.float32)
    grad_values = jnp.zeros(values_seq.shape, jnp.float32)
    query_parts = []
    for block_id in range(seq_len // block_len):
        block_start = block_id * block_len
        block_stop = block_start + block_len
        query_blk = query_seq[block_start:block_stop]
        keys_blk = keys_seq[:block_stop]
        values_blk = values_seq[:block_stop]
        grad_blk = grad_ctx[block_start:block_stop]
        scores = masked_scores(query_blk, keys_blk, block_start, seq_length)
        attn_weights = jnp.exp(scores - log_sums[:, :, block_start:block_stop, None])
        grad_weights = jnp.einsum(
            "qgrd,kgd->grqk", grad_blk, values_blk, preferred_element_type=jnp.float32
        )
        value_terms = jnp.einsum(
            "grqk,qgrd->kgd",
            attn_weights.astype(jnp.bfloat16),
            grad_blk,
            preferred_element_type=jnp.float32,
        )
        grad_values = grad_values.at[:block_stop].add(value_terms)
        centre = jnp.sum(attn_weights * grad_weights, axis=-1, keepdims=True)
        grad_scores = (attn_weights * (grad_weights - centre) * scale).astype(jnp.bfloat16)
        query_parts.append(
            jnp.einsum("grqk,kgd->qgrd", grad_scores, keys_blk, preferred_element_type=jnp.float32)
        )
        key_terms = jnp.einsum(
            "grqk,qgrd->kgd", grad_scores, query_blk, preferred_element_type=jnp.float32
        )
        grad_keys = grad_keys.at[:block_stop].add(key_terms)
    return (jnp.concatenate(query_parts, axis=0), grad_keys, grad_values)


def norm_backward(grad_normed, source, inverse, gain):
    weighted = grad_normed * gain[None, :]
    grad_gain = jnp.sum(grad_normed * source * inverse, axis=0)
    grad_source = inverse * weighted - source * inverse * inverse * inverse * jnp.mean(
        source * weighted, axis=1, keepdims=True
    )
    return (grad_source, grad_gain)


def combine_routes(slot_rows, slot_index, top_count):
    combined = slot_rows[slot_index[:, 0]]
    for route_k in range(1, top_count):
        combined = combined + slot_rows[slot_index[:, route_k]]
    return combined


def shards(
    tokens,
    lengths,
    routes,
    gain_attn,
    w_query,
    w_keyvalue,
    w_out,
    gain_mixer,
    w_router,
    w_gate,
    w_up,
    w_down,
    out_grad,
):
    tok_rows, model_width = tokens.shape
    group_rows = routes.shape[0]
    top_count = routes.shape[1]
    seq_count = lengths.shape[0]
    seq_len = group_rows // seq_count
    parts = lax.axis_size("tensor")
    own_start = lax.axis_index("tensor") * tok_rows
    head_size = HD
    q_local = w_query.shape[1] // head_size
    kv_local = w_keyvalue.shape[2] // head_size
    repeat_count = q_local // kv_local
    experts = w_router.shape[1]
    capacity = (tok_rows * top_count * 17 + experts * 16 - 1) // (experts * 16)
    per_expert = parts * capacity
    turns = experts // 2
    rows_all = jnp.arange(group_rows, dtype=jnp.int32)
    positions = rows_all % seq_len
    seq_ids = rows_all // seq_len
    row_length = jnp.sum(
        jnp.where(
            seq_ids[:, None] == jnp.arange(seq_count, dtype=jnp.int32)[None, :], lengths[None, :], 0
        ),
        axis=1,
    )
    live = (positions < row_length).astype(jnp.float32)
    live_own = lax.dynamic_slice_in_dim(live, own_start, tok_rows, 0)
    tokens_f = tokens.astype(jnp.float32)
    inverse_attn = lax.rsqrt(jnp.mean(tokens_f * tokens_f, axis=1, keepdims=True) + epsilon)
    normed_attn = (tokens_f * inverse_attn * gain_attn[None, :]).astype(jnp.bfloat16)
    query_w, keyval_w, out_w = (
        lax.all_gather(w_query, "dp", axis=0, tiled=True),
        lax.all_gather(w_keyvalue, "dp", axis=0, tiled=True),
        lax.all_gather(w_out, "dp", axis=0, tiled=True),
    )
    rows_attn = lax.all_gather(normed_attn, "tensor", axis=0, tiled=True)
    query_pre = jnp.dot(rows_attn, query_w, preferred_element_type=jnp.float32)
    keyval_pre = jnp.einsum("rd,dsk->rsk", rows_attn, keyval_w, preferred_element_type=jnp.float32)
    cosine_table, sine_table = rotary_tables(positions, head_size)
    query_rot = rotate(
        query_pre.reshape(group_rows, q_local, head_size), cosine_table, sine_table
    ).astype(jnp.bfloat16)
    keys_rot = rotate(
        keyval_pre[:, 0].reshape(group_rows, kv_local, head_size), cosine_table, sine_table
    ).astype(jnp.bfloat16)
    values_rows = keyval_pre[:, 1].reshape(group_rows, kv_local, head_size).astype(jnp.bfloat16)
    query_seqs = query_rot.reshape(seq_count, seq_len, kv_local, repeat_count, head_size)
    keys_seqs = keys_rot.reshape(seq_count, seq_len, kv_local, head_size)
    values_seqs = values_rows.reshape(seq_count, seq_len, kv_local, head_size)
    context_seqs, log_sums = lax.map(attend_sequence, (query_seqs, keys_seqs, values_seqs, lengths))
    context_rows = context_seqs.reshape(group_rows, q_local * head_size)
    attn_part = (
        jnp.einsum("rh,dh->rd", context_rows, out_w, preferred_element_type=jnp.float32)
        * live[:, None]
    )
    attn_own = lax.psum_scatter(
        attn_part.astype(jnp.bfloat16), "tensor", scatter_dimension=0, tiled=True
    ).astype(jnp.float32)
    hidden_own = tokens_f + attn_own
    inverse_mix = lax.rsqrt(jnp.mean(hidden_own * hidden_own, axis=1, keepdims=True) + epsilon)
    normed_mix = (hidden_own * inverse_mix * gain_mixer[None, :]).astype(jnp.bfloat16)
    rows_mix, grad_out_rows = (
        lax.all_gather(normed_mix, "tensor", axis=0, tiled=True),
        lax.all_gather(out_grad, "tensor", axis=0, tiled=True),
    )
    logits = jnp.dot(rows_mix, w_router, preferred_element_type=jnp.float32)
    expert_ids = jnp.arange(experts, dtype=jnp.int32)
    picks = routes[:, :, None] == expert_ids[None, None, :]
    chosen = jnp.sum(jnp.where(picks, logits[:, None, :], 0.0), axis=2)
    shares = jax.nn.softmax(chosen, axis=1)
    gates = shares * live[:, None]
    row_hits = jnp.any(picks, axis=1).astype(jnp.bfloat16).reshape(parts, tok_rows, experts)
    local_ids = jnp.arange(tok_rows, dtype=jnp.int32)
    strictly_lower = (local_ids[:, None] > local_ids[None, :]).astype(jnp.bfloat16)
    earlier_rows = jnp.einsum(
        "ij,bje->bie", strictly_lower, row_hits, preferred_element_type=jnp.float32
    ).reshape(group_rows, experts)
    rank_pair = jnp.sum(jnp.where(picks, earlier_rows[:, None, :], 0.0), axis=2).astype(jnp.int32)
    block_of_row = rows_all // tok_rows
    slot_index = routes * per_expert + block_of_row[:, None] * capacity + rank_pair
    local_slot = (routes * capacity + rank_pair).reshape(parts, tok_rows * top_count)
    gates_blocks = gates.reshape(parts, tok_rows * top_count)
    slot_ids = jnp.arange(experts * capacity, dtype=jnp.int32)
    entry_row = jnp.arange(tok_rows * top_count, dtype=jnp.int32) // top_count

    def block_slots(operands):
        slots_blk, gates_blk, block_id = operands
        match = slots_blk[None, :] == slot_ids[:, None]
        owners = jnp.sum(jnp.where(match, entry_row[None, :], 0), axis=1) + block_id * tok_rows
        slot_gates = jnp.sum(jnp.where(match, gates_blk[None, :], 0.0), axis=1)
        return (owners, slot_gates)

    owner_blocks, gate_blocks = lax.map(
        block_slots, (local_slot, gates_blocks, jnp.arange(parts, dtype=jnp.int32))
    )
    owner_turns = jnp.transpose(owner_blocks.reshape(parts, experts, capacity), (1, 0, 2)).reshape(
        turns, 2, per_expert
    )
    gate_turns = jnp.transpose(gate_blocks.reshape(parts, experts, capacity), (1, 0, 2)).reshape(
        turns, 2, per_expert
    )
    turn_ids = jnp.arange(turns, dtype=jnp.int32)
    slots_total = experts * per_expert
    gate_all, up_all, down_all = (
        lax.all_gather(w_gate, "dp", axis=0, tiled=True),
        lax.all_gather(w_up, "dp", axis=0, tiled=True),
        lax.all_gather(w_down, "dp", axis=0, tiled=True),
    )

    def expert_forward(carry, operands):
        owners, slot_gates, turn_id = operands
        rows_in = rows_mix[owners]
        gate_pair = lax.dynamic_slice_in_dim(gate_all, 2 * turn_id, 2, 1)
        up_pair = lax.dynamic_slice_in_dim(up_all, 2 * turn_id, 2, 1)
        down_pair = lax.dynamic_slice_in_dim(down_all, 2 * turn_id, 2, 1)
        gate_lin = jnp.einsum(
            "erd,def->erf", rows_in, gate_pair, preferred_element_type=jnp.float32
        )
        up_lin = jnp.einsum("erd,def->erf", rows_in, up_pair, preferred_element_type=jnp.float32)
        scaled_hidden = (slot_gates[:, :, None] * jax.nn.silu(gate_lin) * up_lin).astype(
            jnp.bfloat16
        )
        expert_out = jnp.einsum(
            "erf,def->erd", scaled_hidden, down_pair, preferred_element_type=jnp.float32
        )
        return (carry, (gate_lin, up_lin, expert_out))

    _, (gate_lins, up_lins, expert_outs) = lax.scan(
        expert_forward, jnp.zeros((), jnp.float32), (owner_turns, gate_turns, turn_ids)
    )
    moe_part = combine_routes(expert_outs.reshape(slots_total, model_width), slot_index, top_count)
    moe_own = lax.psum_scatter(
        moe_part.astype(jnp.bfloat16), "tensor", scatter_dimension=0, tiled=True
    ).astype(jnp.float32)
    mixed = (hidden_own + moe_own).astype(jnp.bfloat16)
    gate_back, up_back, down_back = (
        lax.all_gather(w_gate, "dp", axis=0, tiled=True),
        lax.all_gather(w_up, "dp", axis=0, tiled=True),
        lax.all_gather(w_down, "dp", axis=0, tiled=True),
    )

    def expert_backward(carry, operands):
        grad_gate_w, grad_up_w, grad_down_w = carry
        owners, slot_gates, gate_lin, up_lin, turn_id = operands
        rows_in = rows_mix[owners]
        grad_in = grad_out_rows[owners]
        gate_pair = lax.dynamic_slice_in_dim(gate_back, 2 * turn_id, 2, 1)
        up_pair = lax.dynamic_slice_in_dim(up_back, 2 * turn_id, 2, 1)
        down_pair = lax.dynamic_slice_in_dim(down_back, 2 * turn_id, 2, 1)
        sigmoid_gate = jax.nn.sigmoid(gate_lin)
        silu_gate = jax.nn.silu(gate_lin)
        scaled_hidden = (slot_gates[:, :, None] * silu_gate * up_lin).astype(jnp.bfloat16)
        grad_scaled = jnp.einsum(
            "erd,def->erf", grad_in, down_pair, preferred_element_type=jnp.float32
        )
        slot_grads = jnp.sum(grad_scaled * silu_gate * up_lin, axis=2)
        grad_act = slot_gates[:, :, None] * grad_scaled
        grad_gate_lin = (
            grad_act * up_lin * sigmoid_gate * (1.0 + gate_lin * (1.0 - sigmoid_gate))
        ).astype(jnp.bfloat16)
        grad_up_lin = (grad_act * silu_gate).astype(jnp.bfloat16)
        down_terms = jnp.einsum(
            "erd,erf->def", grad_in, scaled_hidden, preferred_element_type=jnp.float32
        )
        gate_terms = jnp.einsum(
            "erd,erf->def", rows_in, grad_gate_lin, preferred_element_type=jnp.float32
        )
        up_terms = jnp.einsum(
            "erd,erf->def", rows_in, grad_up_lin, preferred_element_type=jnp.float32
        )
        grad_down_w = lax.dynamic_update_slice_in_dim(grad_down_w, down_terms, 2 * turn_id, 1)
        grad_gate_w = lax.dynamic_update_slice_in_dim(grad_gate_w, gate_terms, 2 * turn_id, 1)
        grad_up_w = lax.dynamic_update_slice_in_dim(grad_up_w, up_terms, 2 * turn_id, 1)
        rows_grad = jnp.einsum(
            "erf,def->erd", grad_gate_lin, gate_pair, preferred_element_type=jnp.float32
        )
        rows_grad = rows_grad + jnp.einsum(
            "erf,def->erd", grad_up_lin, up_pair, preferred_element_type=jnp.float32
        )
        return ((grad_gate_w, grad_up_w, grad_down_w), (slot_grads, rows_grad))

    weight_zeros = jnp.zeros(gate_all.shape, jnp.float32)
    start_carry = (weight_zeros, weight_zeros, weight_zeros)
    back_carry, (slot_grad_turns, rows_grad_turns) = lax.scan(
        expert_backward, start_carry, (owner_turns, gate_turns, gate_lins, up_lins, turn_ids)
    )
    grad_gate_w, grad_up_w, grad_down_w = back_carry
    acc_rows = combine_routes(
        rows_grad_turns.reshape(slots_total, model_width), slot_index, top_count
    )
    gate_grad_part = slot_grad_turns.reshape(-1)[slot_index]
    grad_experts_own, gate_grad_own = (
        lax.psum_scatter(
            acc_rows.astype(jnp.bfloat16), "tensor", scatter_dimension=0, tiled=True
        ).astype(jnp.float32),
        lax.psum_scatter(
            gate_grad_part.astype(jnp.bfloat16), "tensor", scatter_dimension=0, tiled=True
        ).astype(jnp.float32),
    )
    grad_gate_out, grad_up_out, grad_down_out = (
        lax.psum_scatter(grad_gate_w, "dp", scatter_dimension=0, tiled=True),
        lax.psum_scatter(grad_up_w, "dp", scatter_dimension=0, tiled=True),
        lax.psum_scatter(grad_down_w, "dp", scatter_dimension=0, tiled=True),
    )
    shares_own = lax.dynamic_slice_in_dim(shares, own_start, tok_rows, 0)
    picks_own = lax.dynamic_slice_in_dim(picks, own_start, tok_rows, 0)
    grad_shares = gate_grad_own * live_own[:, None]
    grad_chosen = shares_own * (
        grad_shares - jnp.sum(shares_own * grad_shares, axis=1, keepdims=True)
    )
    grad_logits = jnp.sum(jnp.where(picks_own, grad_chosen[:, :, None], 0.0), axis=1)
    grad_router_part = jnp.einsum(
        "rd,re->de", normed_mix.astype(jnp.float32), grad_logits, precision=highest
    )
    grad_mix = grad_experts_own + jnp.einsum(
        "re,de->rd", grad_logits, w_router.astype(jnp.float32), precision=highest
    )
    grad_from_mix, grad_gain_mix_part = norm_backward(grad_mix, hidden_own, inverse_mix, gain_mixer)
    grad_hidden_own = out_grad.astype(jnp.float32) + grad_from_mix
    grad_branch_own = (grad_hidden_own * live_own[:, None]).astype(jnp.bfloat16)
    grad_branch_rows = lax.all_gather(grad_branch_own, "tensor", axis=0, tiled=True)
    query_back, keyval_back, out_back = (
        lax.all_gather(w_query, "dp", axis=0, tiled=True),
        lax.all_gather(w_keyvalue, "dp", axis=0, tiled=True),
        lax.all_gather(w_out, "dp", axis=0, tiled=True),
    )
    grad_context = jnp.einsum(
        "rd,dh->rh", grad_branch_rows, out_back, preferred_element_type=jnp.float32
    ).astype(jnp.bfloat16)
    grad_out_w = jnp.einsum(
        "rd,rh->dh", grad_branch_rows, context_rows, preferred_element_type=jnp.float32
    )
    grad_ctx_seqs = grad_context.reshape(seq_count, seq_len, kv_local, repeat_count, head_size)
    grad_query_seqs, grad_keys_seqs, grad_values_seqs = lax.map(
        sequence_backward, (query_seqs, keys_seqs, values_seqs, grad_ctx_seqs, log_sums, lengths)
    )
    grad_query_pre = (
        unrotate(grad_query_seqs.reshape(group_rows, q_local, head_size), cosine_table, sine_table)
        .reshape(group_rows, q_local * head_size)
        .astype(jnp.bfloat16)
    )
    grad_key_pre = unrotate(
        grad_keys_seqs.reshape(group_rows, kv_local, head_size), cosine_table, sine_table
    ).reshape(group_rows, kv_local * head_size)
    grad_value_pre = grad_values_seqs.reshape(group_rows, kv_local * head_size)
    grad_keyval = jnp.stack([grad_key_pre, grad_value_pre], axis=1).astype(jnp.bfloat16)
    grad_query_w = jnp.einsum(
        "rd,rh->dh", rows_attn, grad_query_pre, preferred_element_type=jnp.float32
    )
    grad_keyval_w = jnp.einsum(
        "rd,rsk->dsk", rows_attn, grad_keyval, preferred_element_type=jnp.float32
    )
    grad_normed_part = jnp.einsum(
        "rh,dh->rd", grad_query_pre, query_back, preferred_element_type=jnp.float32
    )
    grad_normed_part = grad_normed_part + jnp.einsum(
        "rsk,dsk->rd", grad_keyval, keyval_back, preferred_element_type=jnp.float32
    )
    grad_normed_own = lax.psum_scatter(
        grad_normed_part.astype(jnp.bfloat16), "tensor", scatter_dimension=0, tiled=True
    ).astype(jnp.float32)
    grad_query_out, grad_keyval_out, grad_out_out = (
        lax.psum_scatter(grad_query_w, "dp", scatter_dimension=0, tiled=True),
        lax.psum_scatter(grad_keyval_w, "dp", scatter_dimension=0, tiled=True),
        lax.psum_scatter(grad_out_w, "dp", scatter_dimension=0, tiled=True),
    )
    grad_from_attn, grad_gain_attn_part = norm_backward(
        grad_normed_own, tokens_f, inverse_attn, gain_attn
    )
    grad_tokens = (grad_hidden_own + grad_from_attn).astype(jnp.bfloat16)
    grad_gain_attn, grad_gain_mixer, grad_router = lax.psum(
        (grad_gain_attn_part, grad_gain_mix_part, grad_router_part), ("dp", "tensor")
    )
    return (
        mixed,
        grad_tokens,
        grad_gain_attn,
        grad_query_out,
        grad_keyval_out,
        grad_out_out,
        grad_gain_mixer,
        grad_router,
        grad_gate_out,
        grad_up_out,
        grad_down_out,
    )


def solution(mesh):
    placed = (
        P(("dp", "tensor"), None),
        P("dp"),
        P("dp", None),
        P(),
        P("dp", "tensor"),
        P("dp", None, "tensor"),
        P("dp", "tensor"),
        P(),
        P(),
        P("dp", None, "tensor"),
        P("dp", None, "tensor"),
        P("dp", None, "tensor"),
        P(("dp", "tensor"), None),
    )
    return jax.shard_map(
        shards,
        mesh=mesh,
        in_specs=placed,
        out_specs=(
            P(("dp", "tensor"), None),
            P(("dp", "tensor"), None),
            P(),
            P("dp", "tensor"),
            P("dp", None, "tensor"),
            P("dp", "tensor"),
            P(),
            P(),
            P("dp", None, "tensor"),
            P("dp", None, "tensor"),
            P("dp", None, "tensor"),
        ),
        check_vma=False,
    )
```

profile of v0, /device:TPU:0, one launch (start us, length us, event | category | flops | bytes accessed | tf_op | source)
XLA Modules:
  0.0 3995.2 jit_solution(4288880722890021635)
XLA Ops:
  12.3 29.6 all_gather.37
  41.9 31.6 all_gather.38
  73.5 33.4 all_gather.39
  123.6 31.4 while.80
  161.1 43.8 %reduce-scatter.12.cloned.1.call-done = bf16[512,1024]{1,0:T(8,128)(2,1)} async-done(((bf16[2048,1024]{1,0:T(8,128)(2,1)}), bf16[512,1024]{1,0:T(8,128)(2,1)}) %reduce-scatter.12.cloned.1.call-update) | async-done | bytes 1048592 | tf_op jit(solution)/shard_map/reduce_scatter | solution.py:216
  217.3 26.7 all-gather.10.cloned.1.call-done
  252.5 91.1 %while.84 = (s32[]{:T(128)}, s32[4,4352]{1,0:T(4,128)S(1)}, f32[4,4352]{1,0:T(4,128)S(1)}, s32[4,4096]{1,0:T(4,128)S(1)}, s32[4]{0:T(128)S(1)}, /*index=5*/f32[4...) while((s32[]{:T(128)}, s32[4,4352]{1,0:T(4,128)S(1)}, f32[4,4352]{1,0:T(4,128)S(1)}, ...), condition=%wide.region_18.19_spmd.clone, body=%wide.region_15.18_spmd.clone.sunk | while | flops 106983168 | bytes 356497 | solution.py:253
  344.5 27.3 all-gather.12.cloned.1.call-done
  371.8 126.0 %all-gather.14.cloned.1.call-done = bf16[1024,32,128]{2,0,1:T(8,128)(2,1)} async-done(((bf16[128,32,128]{2,0,1:T(8,128)(2,1)}), bf16[1024,32,128]{2,0,1:T(8,128)(2,1)}) %all-gather.14.cloned.1.call-update) | async-done | bytes 8388624 | tf_op jit(solution)/shard_map/all_gather | solution.py:266
  497.7 126.0 %all-gather.16.cloned.1.call-done = bf16[1024,32,128]{2,0,1:T(8,128)(2,1)} async-done(((bf16[128,32,128]{2,0,1:T(8,128)(2,1)}), bf16[1024,32,128]{2,0,1:T(8,128)(2,1)}) %all-gather.16.cloned.1.call-update) | async-done | bytes 8388624 | tf_op jit(solution)/shard_map/all_gather | solution.py:267
  623.7 23.7 broadcast.591.clone
  647.4 310.3 %while.81 = (s32[]{:T(128)}, f32[16,2,544,128]{3,2,1,0:T(8,128)}, f32[16,2,544,128]{3,2,1,0:T(8,128)}, f32[16,2,544,1024]{3,2,1,0:T(8,128)}, s32[16,2,544]{2,1,0...) while((s32[]{:T(128)}, f32[16,2,544,128]{3,2,1,0:T(8,128)}, ...), condition=%wide.region_20.21_spmd, body=%wide.region_19.20_spmd.sunk | while | flops 856618176 | bytes 18332144 | solution.py:288
  987.8 22.8 broadcast.591
  1010.5 730.3 %while.82 = (s32[]{:T(128)}, f32[1024,32,128]{2,1,0:T(8,128)}, f32[1024,32,128]{2,1,0:T(8,128)}, f32[1024,32,128]{2,1,0:T(8,128)}, bf16[16,2,544]{2,1,0:T(2,128)...) while((s32[]{:T(128)}, f32[1024,32,128]{2,1,0:T(8,128)}, ...), condition=%wide.region_24.25_spmd, body=%wide.region_22.24_spmd.sunk | while | flops 1715736704 | bytes 63043856 | solution.py:344
  1741.0 100.9 %gather_fusion.19 = bf16[16384]{0:T(1024)(128)(2,1)S(1)} fusion(bf16[17408]{0:T(1024)(128)(2,1)S(1)} %reshape.637, s32[16384]{0:T(1024)S(1)} %copy-done.8), kind=kCustom, calls=%fused_computation.19 | custom fusion | bytes 131072 | tf_op jit(solution)/shard_map/gather | solution.py:351
  1843.4 39.3 gather_fusion.18
  1882.8 38.9 gather_fusion.17
  1921.7 38.9 gather_fusion.16
  1960.6 38.9 gather_fusion.15
  1999.5 38.8 gather_fusion.14
  2038.3 38.8 gather_fusion.13
  2077.1 38.8 gather_fusion.12
  2115.9 38.9 gather_fusion.11
  2154.7 24.8 add_convert_fusion
  2183.8 38.6 reduce-scatter.16.cloned.1.call-done
  2229.5 34.6 all-gather.20.cloned.1.call-done
  2271.3 192.8 %while.83 = (s32[]{:T(128)}, f32[2,1024,2,2,64]{1,0,4,3,2:T(2,128)}, f32[2,1024,2,64]{1,0,3,2:T(2,128)}, bf16[2,1024,2,64]{1,3,2,0:T(8,128)(2,1)}, bf16[2,1024,2...) while((s32[]{:T(128)}, ...), condition=%wide.region_33.34_spmd, body=%wide.region_30.33_spmd.sunk | while | flops 2097165312 | bytes 212629296 | solution.py:394
  2310.2 13.6 fusion.344
  2323.8 13.4 fusion.338
  2348.9 18.8 dynamic_update_slice.103
  2406.3 13.6 fusion.344
  2445.0 18.8 dynamic_update_slice.103
  2484.2 39.2 gather_fusion.10
  2523.4 39.5 gather_fusion.9
  2562.9 39.0 gather_fusion.8
  2601.9 38.8 gather_fusion.7
  2640.8 38.8 gather_fusion.6
  2679.6 38.8 gather_fusion.5
  2718.4 38.8 gather_fusion.4
  2757.2 38.8 gather_fusion.3
  2796.0 24.7 add_convert_fusion.1
  2839.7 39.9 all-reduce.2
  2884.2 111.0 %all-reduce.5.cloned.1.call-done = f32[1024,32]{0,1:T(8,128)} async-done(((f32[1024,32]{0,1:T(8,128)}), f32[1024,32]{0,1:T(8,128)}) %all-reduce.5.cloned.1.call-update) | async-done | bytes 131088 | tf_op jit(solution)/shard_map/psum | solution.py:431
  2995.2 66.4 %reduce-scatter.26.cloned.1.call-done = f32[128,256]{1,0:T(8,128)} async-done(((f32[1024,256]{1,0:T(8,128)}), f32[128,256]{1,0:T(8,128)}) %reduce-scatter.26.cloned.1.call-update) | async-done | bytes 131088 | tf_op jit(solution)/shard_map/reduce_scatter | solution.py:425
  3061.6 66.7 %reduce-scatter.22.cloned.1.call-done = f32[128,256]{1,0:T(8,128)} async-done(((f32[1024,256]{1,0:T(8,128)}), f32[128,256]{1,0:T(8,128)}) %reduce-scatter.22.cloned.1.call-update) | async-done | bytes 131088 | tf_op jit(solution)/shard_map/reduce_scatter | solution.py:423
  3128.3 285.9 %reduce-scatter.28.cloned.1.call-done = f32[128,32,128]{2,1,0:T(8,128)} async-done(((f32[1024,32,128]{2,1,0:T(8,128)}), f32[128,32,128]{2,1,0:T(8,128)}) %reduce-scatter.28.cloned.1.call-update) | async-done | bytes 2097168 | tf_op jit(solution)/shard_map/reduce_scatter | solution.py:361
  3414.3 286.5 %reduce-scatter.30.cloned.1.call-done = f32[128,32,128]{2,1,0:T(8,128)} async-done(((f32[1024,32,128]{2,1,0:T(8,128)}), f32[128,32,128]{2,1,0:T(8,128)}) %reduce-scatter.30.cloned.1.call-update) | async-done | bytes 2097168 | tf_op jit(solution)/shard_map/reduce_scatter | solution.py:362
  3700.8 286.1 %reduce-scatter.32.cloned.1.call-done = f32[128,32,128]{2,1,0:T(8,128)} async-done(((f32[1024,32,128]{2,1,0:T(8,128)}), f32[128,32,128]{2,1,0:T(8,128)}) %reduce-scatter.32.cloned.1.call-update) | async-done | bytes 2097168 | tf_op jit(solution)/shard_map/reduce_scatter | solution.py:363
  (1022 shorter events, 1394.4 us)
Async XLA Ops:
  7.2 236.8 %copy-start = (bf16[1024,32]{0,1:T(8,128)(2,1)S(1)}, bf16[1024,32]{0,1:T(8,128)(2,1)}, u32[]{:S(2)}) copy-start(bf16[1024,32]{0,1:T(8,128)(2,1)} %param.43) | copy-start | bytes 196612
  7.2 66.2 %copy-start.61 = (bf16[128,256]{1,0:T(8,128)(2,1)S(1)}, bf16[128,256]{1,0:T(8,128)(2,1)}, u32[]{:S(2)}) copy-start(bf16[128,256]{1,0:T(8,128)(2,1)} %param.41) | copy-start | bytes 196612
  7.2 100.6 %all-gather.8.cloned.1.call-start = ((), (), s32[]{:S(2)}) async-start(), calls=%async_computation.11 | async-start | bytes 5242880 | tf_op jit(solution)/shard_map/all_gather | solution.py:196
  12.0 193.0 %reduce-scatter.12.cloned.1.call-start = ((), (), s32[]{:S(2)}) async-start(), calls=%async_computation.12 | async-start | bytes 5242880 | tf_op jit(solution)/shard_map/reduce_scatter | solution.py:216
  12.3 144.1 %copy-start.75 = (f32[2048]{0:T(1024)}, f32[2048]{0:T(1024)S(1)}, u32[]{:S(2)}) copy-start(f32[2048]{0:T(1024)S(1)} %fusion.211) | copy-start | bytes 24580
  41.9 69.7 %copy-start.21 = (bf16[1024,2,128]{0,2,1:T(8,128)(2,1)}, bf16[1024,2,128]{0,2,1:T(8,128)(2,1)S(1)}, u32[]{:S(2)}) copy-start(bf16[1024,2,128]{0,2,1:T(8,128)(2,1)S(1)} %all_gather.37) | copy-start | bytes 1572868
  161.0 43.9 %copy-start.4 = (bf16[512,1024]{1,0:T(8,128)(2,1)S(1)}, bf16[512,1024]{1,0:T(8,128)(2,1)}, u32[]{:S(2)}) copy-start(bf16[512,1024]{1,0:T(8,128)(2,1)} %param.35) | copy-start | bytes 3145732
  161.0 45.6 %copy-start.65 = (f32[1024]{0:T(1024)S(1)}, f32[1024]{0:T(1024)}, u32[]{:S(2)}) copy-start(f32[1024]{0:T(1024)} %param.42) | copy-start | bytes 12292
  161.1 48.3 %copy-start.27 = (bf16[128,32,128]{2,1,0:T(8,128)(2,1)S(1)}, bf16[128,32,128]{2,1,0:T(8,128)(2,1)}, u32[]{:S(2)}) copy-start(bf16[128,32,128]{2,1,0:T(8,128)(2,1)} %param.44) | copy-start | bytes 3145732
  161.1 82.9 %all-gather.10.cloned.1.call-start = ((), (), s32[]{:S(2)}) async-start(), calls=%async_computation.13 | async-start | bytes 5242880 | tf_op jit(solution)/shard_map/all_gather | solution.py:223
  209.3 162.4 %all-gather.12.cloned.1.call-start = ((), (), s32[]{:S(2)}) async-start(), calls=%async_computation.14 | async-start | bytes 9437184 | tf_op jit(solution)/shard_map/all_gather | solution.py:265
  210.8 286.9 %all-gather.14.cloned.1.call-start = ((), (), s32[]{:S(2)}) async-start(), calls=%async_computation.15 | async-start | bytes 9437184 | tf_op jit(solution)/shard_map/all_gather | solution.py:266
  212.5 411.2 %all-gather.16.cloned.1.call-start = ((), (), s32[]{:S(2)}) async-start(), calls=%async_computation.16 | async-start | bytes 9437184 | tf_op jit(solution)/shard_map/all_gather | solution.py:267
  213.9 750.1 %all-gather.18.cloned.1.call-start = ((), (), s32[]{:S(2)}) async-start(), calls=%async_computation.18 | async-start | bytes 5242880 | tf_op jit(solution)/shard_map/all_gather | solution.py:224
  214.7 1966.7 %reduce-scatter.18.cloned.1.call-start = ((), (), s32[]{:S(2)}) async-start(), calls=%async_computation.20 | async-start | bytes 40960 | tf_op jit(solution)/shard_map/reduce_scatter | solution.py:356
  1010.5 730.4 %copy-start.8 = (s32[16384]{0:T(1024)S(1)}, s32[16384]{0:T(1024)}, u32[]{:S(2)}) copy-start(s32[16384]{0:T(1024)} %broadcast_clamp_fusion) | copy-start | bytes 196612
  1741.0 102.4 %copy-start.48 = (s32[2048]{0:T(1024)S(1)}, s32[2048]{0:T(1024)}, u32[]{:S(2)}) copy-start(s32[2048]{0:T(1024)} %broadcast_clamp_fusion.1) | copy-start | bytes 24580
  1843.4 379.1 %reduce-scatter.16.cloned.1.call-start = ((), (), s32[]{:S(2)}) async-start(), calls=%async_computation.19 | async-start | bytes 5242880 | tf_op jit(solution)/shard_map/reduce_scatter | solution.py:353
  1843.4 39.3 copy-start.50
  1882.8 38.9 copy-start.52
  1921.7 38.9 copy-start.54
  1960.6 38.9 copy-start.56
  1999.5 38.8 copy-start.58
  2179.5 42.9 %copy-start.5 = (bf16[512,1024]{1,0:T(8,128)(2,1)S(1)}, bf16[512,1024]{1,0:T(8,128)(2,1)}, u32[]{:S(2)}) copy-start(bf16[512,1024]{1,0:T(8,128)(2,1)} %param.35) | copy-start | bytes 3145732
  2179.5 42.9 %copy-start.9 = (bf16[512,1024]{1,0:T(8,128)(2,1)S(1)}, bf16[512,1024]{1,0:T(8,128)(2,1)}, u32[]{:S(2)}) copy-start(bf16[512,1024]{1,0:T(8,128)(2,1)} %reduce-scatter.12.cloned.1.call-done) | copy-start | bytes 3145732
  2179.6 42.9 %copy-start.66 = (f32[1024]{0:T(1024)S(1)}, f32[1024]{0:T(1024)}, u32[]{:S(2)}) copy-start(f32[1024]{0:T(1024)} %param.42) | copy-start | bytes 12292
  2179.6 42.9 %copy-start.71 = (f32[512]{0:T(512)S(1)}, f32[512]{0:T(512)}, u32[]{:S(2)}) copy-start(f32[512]{0:T(512)} %copy-done.70) | copy-start | bytes 6148
  2179.6 47.9 %copy-start.11 = (bf16[512,1024]{1,0:T(8,128)(2,1)S(1)}, bf16[512,1024]{1,0:T(8,128)(2,1)}, u32[]{:S(2)}) copy-start(bf16[512,1024]{1,0:T(8,128)(2,1)} %param.47) | copy-start | bytes 3145732
  2179.6 84.5 %all-gather.20.cloned.1.call-start = ((), (), s32[]{:S(2)}) async-start(), calls=%async_computation.21 | async-start | bytes 5242880 | tf_op jit(solution)/shard_map/all_gather | solution.py:381
  2183.8 45.6 %copy-start.37 = (f32[512,32]{0,1:T(8,128)}, f32[512,32]{0,1:T(8,128)S(1)}, u32[]{:S(2)}) copy-start(f32[512,32]{0,1:T(8,128)S(1)} %select_reduce_fusion.2) | copy-start | bytes 196612
  2229.4 606.2 %reduce-scatter.24.cloned.1.call-start = ((), (), s32[]{:S(2)}) async-start(), calls=%async_computation.24 | async-start | bytes 1179648 | tf_op jit(solution)/shard_map/reduce_scatter | solution.py:424
  2474.4 363.2 %reduce-scatter.20.cloned.1.call-start = ((), (), s32[]{:S(2)}) async-start(), calls=%async_computation.22 | async-start | bytes 5242880 | tf_op jit(solution)/shard_map/reduce_scatter | solution.py:419
  2483.5 396.1 %reduce-scatter.14.cloned.1.call-start = ((), (), s32[]{:S(2)}) async-start(), calls=%async_computation.17 | async-start | bytes 5242880 | tf_op jit(solution)/shard_map/reduce_scatter | solution.py:292
  2484.2 39.2 copy-start.51
  2523.4 39.5 copy-start.53
  2562.9 39.0 copy-start.55
  2601.9 38.8 copy-start.57
  2820.8 174.4 %all-reduce.5.cloned.1.call-start = ((), (), s32[]{:S(2)}) async-start(), calls=%async_computation.26 | async-start | bytes 262144 | tf_op jit(solution)/shard_map/psum | solution.py:431
  2823.3 238.3 %reduce-scatter.26.cloned.1.call-start = ((), (), s32[]{:S(2)}) async-start(), calls=%async_computation.25 | async-start | bytes 1179648 | tf_op jit(solution)/shard_map/reduce_scatter | solution.py:425
  2828.0 300.4 %reduce-scatter.22.cloned.1.call-start = ((), (), s32[]{:S(2)}) async-start(), calls=%async_computation.23 | async-start | bytes 1179648 | tf_op jit(solution)/shard_map/reduce_scatter | solution.py:423
  2833.7 580.5 %reduce-scatter.28.cloned.1.call-start = ((), (), s32[]{:S(2)}) async-start(), calls=%async_computation.27 | async-start | bytes 18874368 | tf_op jit(solution)/shard_map/reduce_scatter | solution.py:361
  2834.3 866.5 %reduce-scatter.30.cloned.1.call-start = ((), (), s32[]{:S(2)}) async-start(), calls=%async_computation.28 | async-start | bytes 18874368 | tf_op jit(solution)/shard_map/reduce_scatter | solution.py:362
  2834.9 1152.0 %reduce-scatter.32.cloned.1.call-start = ((), (), s32[]{:S(2)}) async-start(), calls=%async_computation.29 | async-start | bytes 18874368 | tf_op jit(solution)/shard_map/reduce_scatter | solution.py:363
  2835.0 44.6 %copy-start.10 = (bf16[512,1024]{1,0:T(8,128)(2,1)S(1)}, bf16[512,1024]{1,0:T(8,128)(2,1)}, u32[]{:S(2)}) copy-start(bf16[512,1024]{1,0:T(8,128)(2,1)} %reduce-scatter.12.cloned.1.call-done) | copy-start | bytes 3145732
  2835.0 44.6 %copy-start.12 = (bf16[512,1024]{1,0:T(8,128)(2,1)S(1)}, bf16[512,1024]{1,0:T(8,128)(2,1)}, u32[]{:S(2)}) copy-start(bf16[512,1024]{1,0:T(8,128)(2,1)} %param.47) | copy-start | bytes 3145732
  2835.0 44.6 %copy-start.67 = (f32[1024]{0:T(1024)S(1)}, f32[1024]{0:T(1024)}, u32[]{:S(2)}) copy-start(f32[1024]{0:T(1024)} %param.42) | copy-start | bytes 12292
  2835.0 44.6 %copy-start.72 = (f32[512]{0:T(512)S(1)}, f32[512]{0:T(512)}, u32[]{:S(2)}) copy-start(f32[512]{0:T(512)} %copy-done.70) | copy-start | bytes 6148
  2835.0 44.6 %copy-start.74 = (f32[512]{0:T(512)S(1)}, f32[512]{0:T(512)}, u32[]{:S(2)}) copy-start(f32[512]{0:T(512)} %copy-done.73) | copy-start | bytes 6148
  (115 other events, 765.7 us)
Sparse Core Ops, SparseCore 0:
  12.1 37.1 all-gather.7
  161.2 43.7 reduce-scatter.11
  209.4 34.4 all-gather.9
  246.8 124.9 all-gather.11
  374.6 123.0 all-gather.13
  500.6 123.0 all-gather.15
  625.3 32.6 all-gather.17
  1843.5 17.6 reduce-scatter.17
  2179.7 42.6 reduce-scatter.15
  2229.5 34.4 all-gather.19
  2474.5 63.3 reduce-scatter.23
  2540.2 43.4 reduce-scatter.19
  2820.9 45.8 reduce-scatter.13
  2872.8 122.3 all-reduce.4
  2999.0 62.5 reduce-scatter.25
  3065.8 62.4 reduce-scatter.21
  3132.5 281.6 reduce-scatter.27
  3418.9 281.7 reduce-scatter.29
  3705.1 281.7 reduce-scatter.31
where the time goes:
time: 4020 us; the launch traced here: 4000 us
  waiting for transfers between devices  1530 us (38%)
  local copies, waits for them, and re-layouts  1500 us (37%)
  matrix products  612 us (15%)
  other arithmetic  180 us (4%)
  blocking collectives  134 us (3%)
    gather x14, local copies, waits for them, and re-layouts, combine_routes(): combined = combined + slot_rows[slot_index[:, route_k]]  545 us
    reduce_scatter x1, waiting for transfers between devices, shards(): lax.psum_scatter(grad_up_w, 'dp', scatter_dimension=0, tiled=True)  287 us
    reduce_scatter x1, waiting for transfers between devices, shards(): lax.psum_scatter(grad_down_w, 'dp', scatter_dimension=0, tiled=True)  286 us
    reduce_scatter x1, waiting for transfers between devices, shards(): lax.psum_scatter(grad_gate_w, 'dp', scatter_dimension=0, tiled=True)  286 us
    gather x16, local copies, waits for them, and re-layouts, expert_backward(): grad_in = grad_out_rows[owners]  149 us
    gather x16, local copies, waits for them, and re-layouts, expert_forward(): rows_in = rows_mix[owners]  142 us
    gather x16, local copies, waits for them, and re-layouts, expert_backward(): rows_in = rows_mix[owners]  142 us
    all_gather x1, waiting for transfers between devices, shards(): lax.all_gather(w_down, 'dp', axis=0, tiled=True)  126 us
  transfers between devices with their start and end apart: 19, of which 13 were waited for; matrix products, arithmetic and copies ran while one was open for 29% of the time, Pallas kernels for 0%

commit v1 on v0

v1 whole, which is shorter than its diff:
```python
import functools
import math

import jax
import jax.numpy as jnp
from jax import lax
from jax.experimental import pallas as pl
from jax.experimental.pallas import tpu as pltpu
from jax.sharding import PartitionSpec as P

HD = 64
LANES = 128
epsilon = 1e-06
rope_base = 10000.0
bf16 = jnp.bfloat16
f32 = jnp.float32
BOTH = ("dp", "tensor")
VMEM_LIMIT = 60 * 1024 * 1024
QBLK = 256


def dot(a, b, ca, cb):
    return lax.dot_general(a, b, (((ca,), (cb,)), ((), ())), preferred_element_type=f32)


def call(kernel, out_shape, flops, nbytes, **kw):
    return pl.pallas_call(
        kernel,
        out_shape=out_shape,
        compiler_params=pltpu.CompilerParams(vmem_limit_bytes=VMEM_LIMIT),
        cost_estimate=pl.CostEstimate(flops=flops, bytes_accessed=nbytes, transcendentals=0),
        **kw,
    )


def sds(shape, dtype):
    return jax.ShapeDtypeStruct(shape, dtype)


VM = pl.BlockSpec(memory_space=pltpu.VMEM)
SM = pl.BlockSpec(memory_space=pltpu.SMEM)


def hop(x, dp_bit, t_bits):
    nd, nt = lax.axis_size("dp"), lax.axis_size("tensor")
    pairs = [
        (d * nt + t, (d ^ dp_bit) * nt + (t ^ t_bits)) for d in range(nd) for t in range(nt)
    ]
    return lax.ppermute(x, BOTH, pairs)


def hop_c(x):
    return hop(x, 0, 1)


def hop_y(x):
    return hop(x, 0, 2)


def hop_x(x):
    return hop(x, 1, 0)


def gather_plane(x):
    half = x.shape[0] // 2
    from_y, from_x = hop_y(x), hop_x(x)
    diag_a, diag_b = hop_x(from_y[:half]), hop_y(from_x[half:])
    near = (x, from_y, from_x, diag_a, diag_b)
    far = tuple(hop_c(item) for item in near)
    return near + far


def add16(a, b):
    return (a.astype(f32) + b.astype(f32)).astype(bf16)


def scatter_plane(send, keep):
    total = add16(keep, hop_c(send))
    half = total.shape[1] // 2
    x_a, y_b = total[2, :half], total[1, half:]
    got_xa, got_yb = hop_x(x_a), hop_y(y_b)
    got_da, got_db = hop_x(total[3, :half]), hop_y(total[3, half:])
    got_ya = hop_y(add16(total[1, :half], got_da))
    got_xb = hop_x(add16(total[2, half:], got_db))
    return total[0], jnp.concatenate([got_xa, got_xb]), jnp.concatenate([got_ya, got_yb])


def swap_halves(v):
    lane = lax.broadcasted_iota(jnp.int32, v.shape, 1)
    left = pltpu.roll(v, LANES - HD // 2, 1)
    right = pltpu.roll(v, HD // 2, 1)
    return jnp.where(lane % HD < HD // 2, left, right)


def in_head(tile, h):
    lane = lax.broadcasted_iota(jnp.int32, tile.shape, 1)
    return (lane < HD) if h == 0 else (lane >= HD)


def only_head(tile, h):
    return jnp.where(in_head(tile, h), tile, jnp.zeros_like(tile))


def spread_head(tile, h):
    wide = tile.astype(f32)
    return jnp.where(in_head(wide, h), wide, pltpu.roll(wide, HD, 1)).astype(tile.dtype)


def stacked(tile):
    return jnp.concatenate([only_head(tile, 0), only_head(tile, 1)], axis=0)


def key_limit(start, rows, length):
    column = lax.broadcasted_iota(jnp.int32, (1, 2 * rows), 1)
    position = start + jnp.where(column >= rows, column - rows, column)
    return jnp.minimum(position, length - 1)


def scores_t(kd, qm, limit):
    raw = dot(kd, qm, 1, 1) * (1.0 / math.sqrt(HD))
    key = lax.broadcasted_iota(jnp.int32, raw.shape, 0)
    return jnp.where(key <= limit, raw, -1e30)


def attend_kernel(
    where_ref, own, peer, w, wo, cos, sin,
    q_ref, k_ref, v_ref, ctx_ref, lse_ref, keep_ref, send_ref,
    rows_ref,
):
    core, length = where_ref[0], where_ref[1]
    half = own.shape[0]
    seq = 2 * half
    qw, kw = q_ref.shape[1], k_ref.shape[1]
    rows_ref[pl.ds(pl.multiple_of(core * half, half), half)] = own[...]
    rows_ref[pl.ds(pl.multiple_of((1 - core) * half, half), half)] = peer[...]
    for blk in range(seq // QBLK):
        sl = slice(blk * QBLK, (blk + 1) * QBLK)
        pre = dot(rows_ref[sl], w[...], 1, 0)
        c, s = cos[sl], sin[sl]
        for tile in range((qw + kw) // LANES):
            col = pre[:, tile * LANES:(tile + 1) * LANES]
            turned = (col * c + swap_halves(col) * s).astype(bf16)
            if tile * LANES < qw:
                q_ref[sl, tile * LANES:(tile + 1) * LANES] = turned
            else:
                at = tile * LANES - qw
                k_ref[sl, at:at + LANES] = turned
        v_ref[sl] = pre[:, qw + kw:].astype(bf16)
    for g in range(qw // LANES):
        kv = slice(g // 2 * LANES, (g // 2 + 1) * LANES)
        cols = slice(g * LANES, (g + 1) * LANES)
        kd = spread_head(k_ref[:, kv], g % 2)
        vd_t = spread_head(v_ref[:, kv], g % 2).T
        for blk in range(seq // QBLK):
            top = (blk + 1) * QBLK
            sl = slice(blk * QBLK, top)
            s = scores_t(kd[:top], stacked(q_ref[sl, cols]), key_limit(blk * QBLK, QBLK, length))
            peak = jnp.max(s, axis=0, keepdims=True)
            e = jnp.exp(s - peak)
            total = jnp.sum(e, axis=0, keepdims=True)
            p = (e * (1.0 / total)).astype(bf16)
            ctx = dot(vd_t[:, :top], p, 1, 0).T
            tile = jnp.where(in_head(ctx[:QBLK], 0), ctx[:QBLK], ctx[QBLK:])
            ctx_ref[sl, cols] = tile.astype(bf16)
            lse = peak + jnp.log(total)
            lse_ref[2 * g:2 * g + 1, sl] = lse[:, :QBLK]
            lse_ref[2 * g + 1:2 * g + 2, sl] = lse[:, QBLK:]
    mine = ctx_ref[pl.ds(pl.multiple_of(core * half, half), half)]
    other = ctx_ref[pl.ds(pl.multiple_of((1 - core) * half, half), half)]
    send_ref[...] = dot(other, wo[...], 1, 1).astype(bf16)
    keep_ref[...] = dot(mine, wo[...], 1, 1).astype(bf16)


def attend_back_kernel(
    where_ref, own, peer, gb_own, gb_peer, w, wo, cos, sin, q_ref, k_ref, v_ref, ctx_ref, lse_ref,
    dw_ref, dwo_ref, keep_ref, send_ref,
    rows_ref, gb_ref, gc_ref, dqkv_ref, dk_ref, dv_ref,
):
    core, length = where_ref[0], where_ref[1]
    half = own.shape[0]
    seq = 2 * half
    qw, kw = q_ref.shape[1], k_ref.shape[1]
    at_own = pl.ds(pl.multiple_of(core * half, half), half)
    at_peer = pl.ds(pl.multiple_of((1 - core) * half, half), half)
    rows_ref[at_own] = own[...]
    rows_ref[at_peer] = peer[...]
    gb_ref[at_own] = gb_own[...]
    gb_ref[at_peer] = gb_peer[...]
    gc_ref[...] = dot(gb_ref[...], wo[...], 1, 0).astype(bf16)
    dwo_ref[...] = dot(gb_ref[...], ctx_ref[...], 0, 0).astype(bf16)
    scale = 1.0 / math.sqrt(HD)
    folded = {}
    for g in range(qw // LANES):
        kv = slice(g // 2 * LANES, (g // 2 + 1) * LANES)
        cols = slice(g * LANES, (g + 1) * LANES)
        kd = spread_head(k_ref[:, kv], g % 2)
        kd_t = kd.T
        vd = spread_head(v_ref[:, kv], g % 2)
        for blk in reversed(range(seq // QBLK)):
            top = (blk + 1) * QBLK
            sl = slice(blk * QBLK, top)
            qm = stacked(q_ref[sl, cols])
            gm = stacked(gc_ref[sl, cols])
            s = scores_t(kd[:top], qm, key_limit(blk * QBLK, QBLK, length))
            lse = jnp.concatenate([lse_ref[2 * g:2 * g + 1, sl], lse_ref[2 * g + 1:2 * g + 2, sl]], axis=1)
            p = jnp.exp(s - lse)
            gw = dot(vd[:top], gm, 1, 1)
            centre = jnp.sum(p * gw, axis=0, keepdims=True)
            ds = (p * (gw - centre) * scale).astype(bf16)
            dv = dot(p.astype(bf16), gm, 1, 0)
            dk = dot(ds, qm, 1, 0)
            dq = dot(kd_t[:, :top], ds, 1, 0).T
            if top == seq:
                dk_ref[...] = dk
                dv_ref[...] = dv
            else:
                dk_ref[:top] += dk
                dv_ref[:top] += dv
            tile = jnp.where(in_head(dq[:QBLK], 0), dq[:QBLK], dq[QBLK:])
            back = tile * cos[sl] - swap_halves(tile) * sin[sl]
            dqkv_ref[sl, cols] = back.astype(bf16)
        dk_all = dk_ref[...] + pltpu.roll(dk_ref[...], HD, 1)
        dv_all = dv_ref[...] + pltpu.roll(dv_ref[...], HD, 1)
        if g % 2 == 0:
            folded = (dk_all, dv_all)
        else:
            dk_pair = jnp.where(in_head(dk_all, 0), folded[0], dk_all)
            dv_pair = jnp.where(in_head(dv_all, 0), folded[1], dv_all)
            at = qw + g // 2 * LANES
            back = dk_pair * cos[...] - swap_halves(dk_pair) * sin[...]
            dqkv_ref[:, at:at + LANES] = back.astype(bf16)
            dqkv_ref[:, at + kw:at + kw + LANES] = dv_pair.astype(bf16)
    send_ref[...] = dot(dqkv_ref[at_peer], w[...], 1, 1).astype(bf16)
    keep_ref[...] = dot(dqkv_ref[at_own], w[...], 1, 1).astype(bf16)
    dw_ref[...] = dot(rows_ref[...], dqkv_ref[...], 0, 0).astype(bf16)


def mix_norm_kernel(tokens, keep, got, live, gain, hidden_ref, normed_ref, inv_ref):
    branch = keep[...].astype(f32) + got[...].astype(f32)
    hidden = tokens[...].astype(f32) + live[...] * branch
    inverse = lax.rsqrt(jnp.mean(hidden * hidden, axis=1, keepdims=True) + epsilon)
    hidden_ref[...] = hidden
    inv_ref[...] = inverse
    normed_ref[...] = (hidden * inverse * gain[...]).astype(bf16)


def masked_shares(logits, hit, axis):
    peak = jnp.max(jnp.where(hit, logits, -1e30), axis=axis, keepdims=True)
    e = jnp.where(hit, jnp.exp(jnp.where(hit, logits - peak, 0.0)), 0.0)
    total = jnp.sum(e, axis=axis, keepdims=True)
    return e / jnp.where(total > 0.0, total, 1.0)


def split16(v):
    high = v.astype(bf16)
    return high, (v - high.astype(f32)).astype(bf16)


def mix_back_kernel(
    normed, hidden_in, inv, part_a, part_b, part_c, out_grad, router, hits, live, gain,
    grad_hidden_ref, branch_ref, router_grad_ref, gain_grad_ref,
):
    width = normed.shape[1]
    summed = part_a[...].astype(f32) + part_b[...].astype(f32) + part_c[...].astype(f32)
    grad_experts, grad_gates = summed[:, :width], summed[:, width:]
    hit = hits[...] > 0.0
    shares = masked_shares(dot(normed[...], router[...], 1, 0), hit, 1)
    grad_shares = jnp.where(hit, grad_gates, 0.0)
    grad_chosen = shares * (grad_shares - jnp.sum(shares * grad_shares, axis=1, keepdims=True))
    high, low = split16(grad_chosen)
    experts = router_grad_ref.shape[0]
    router_grad_ref[...] = (dot(high, normed[...], 0, 0) + dot(low, normed[...], 0, 0))[:experts]
    grad_mix = grad_experts + dot(high, router[...], 1, 1) + dot(low, router[...], 1, 1)
    hidden, inverse = hidden_in[...], inv[...]
    gain_grad_ref[...] = jnp.sum(grad_mix * hidden * inverse, axis=0, keepdims=True)
    weighted = grad_mix * gain[...]
    centre = jnp.mean(hidden * weighted, axis=1, keepdims=True)
    grad_hidden = out_grad[...].astype(f32) + inverse * weighted - hidden * (inverse * inverse * inverse * centre)
    grad_hidden_ref[...] = grad_hidden
    branch_ref[...] = (live[...] * grad_hidden).astype(bf16)


def token_back_kernel(tokens, keep, got, grad_hidden, gain, out_ref, gain_grad_ref):
    source = tokens[...].astype(f32)
    inverse = lax.rsqrt(jnp.mean(source * source, axis=1, keepdims=True) + epsilon)
    grad = keep[...].astype(f32) + got[...].astype(f32)
    gain_grad_ref[...] = jnp.sum(grad * source * inverse, axis=0, keepdims=True)
    weighted = grad * gain[...]
    centre = jnp.mean(source * weighted, axis=1, keepdims=True)
    total = grad_hidden[...] + inverse * weighted - source * (inverse * inverse * inverse * centre)
    out_ref[...] = total.astype(bf16)


def placing(ranks, cap):
    slot = lax.broadcasted_iota(jnp.int32, (cap, ranks.shape[1]), 0).astype(f32)
    return [(slot == ranks[e:e + 1]).astype(f32) for e in range(ranks.shape[0])]


def pick_block(refs, block_ref):
    step = pl.program_id(0)
    near, far = refs[:5], refs[5:]
    half = near[0].shape[0] // 2
    for j in range(8):
        part = near if j % 2 == 0 else far

        @pl.when(step == j)
        def _():
            if j // 2 < 3:
                block_ref[...] = part[j // 2][...]
            else:
                block_ref[:half] = part[3][...]
                block_ref[half:] = part[4][...]


def dispatch_kernel(local, cap, where_ref, *refs):
    rows, (ranks, out_ref, block_ref) = refs[:10], refs[10:]
    pick_block(rows, block_ref)
    first = pl.multiple_of(where_ref[1] * 8, 8)
    mine = ranks[0, 0, pl.ds(first, 8)].astype(f32)[:local]
    matrix = jnp.concatenate([m.astype(bf16) for m in placing(mine, cap)], axis=0)
    placed = dot(matrix, block_ref[...], 1, 0).astype(bf16)
    out_ref[...] = placed.reshape(out_ref.shape)


def dispatch_gates_kernel(local, cap, where_ref, *refs):
    rows, (ranks, router_t, out_ref, gates_ref, block_ref, shares_ref) = refs[:10], refs[10:]
    pick_block(rows, block_ref)
    all_ranks = ranks[0, 0].astype(f32)
    logits = dot(router_t[...], block_ref[...], 1, 1)
    shares_ref[...] = masked_shares(logits, all_ranks >= 0.0, 0)
    first = pl.multiple_of(where_ref[1] * 8, 8)
    mine = ranks[0, 0, pl.ds(first, 8)].astype(f32)[:local]
    shares = shares_ref[pl.ds(first, 8)]
    places = placing(mine, cap)
    for e in range(local):
        gates_ref[e, 0] = jnp.sum(places[e] * shares[e:e + 1], axis=1, keepdims=True)
    matrix = jnp.concatenate([m.astype(bf16) for m in places], axis=0)
    placed = dot(matrix, block_ref[...], 1, 0).astype(bf16)
    out_ref[...] = placed.reshape(out_ref.shape)


def combine_kernel(local, cap, groups, where_ref, *refs):
    values, (ranks, out_ref) = refs[:groups], refs[groups:]
    first = pl.multiple_of(where_ref[1] * 8, 8)
    mine = ranks[0, 0, pl.ds(first, 8)].astype(f32)[:local]
    matrix = jnp.concatenate([m.astype(bf16) for m in placing(mine, cap)], axis=0)
    rows = jnp.concatenate([v[:, 0].reshape(-1, v.shape[-1]) for v in values], axis=0)
    out_ref[0] = dot(matrix, rows, 0, 0).astype(bf16)


def expert_kernel(base, where_ref, x_ref, g_ref, gates_ref, w_ref, y_ref, dx_ref, dw_ref):
    slots, width = x_ref.shape[1] * x_ref.shape[2], x_ref.shape[3]
    hidden = w_ref.shape[-1]
    x = x_ref[0].reshape(slots, width)
    g = g_ref[0].reshape(slots, width)
    gates = gates_ref[0].reshape(slots, 1)
    w_gate, w_up, w_down = (w_ref[:, 0, i].reshape(width, hidden) for i in range(3))
    gate_lin = dot(x, w_gate, 1, 0)
    up_lin = dot(x, w_up, 1, 0)
    grad_scaled = dot(g, w_down, 1, 0)
    sigmoid = 1.0 / (1.0 + jnp.exp(-gate_lin))
    silu = gate_lin * sigmoid
    grad_gates = jnp.sum(grad_scaled * silu * up_lin, axis=1, keepdims=True)
    scaled_hidden = (gates * silu * up_lin).astype(bf16)
    grad_act = gates * grad_scaled
    grad_gate_lin = (grad_act * up_lin * sigmoid * (1.0 + gate_lin * (1.0 - sigmoid))).astype(bf16)
    grad_up_lin = (grad_act * silu).astype(bf16)
    y_ref[0] = dot(scaled_hidden, w_down, 1, 1).astype(bf16).reshape(y_ref.shape[1:])
    dx = dot(grad_gate_lin, w_gate, 1, 1) + dot(grad_up_lin, w_up, 1, 1)
    dx_ref[0, :, :, :width] = dx.astype(bf16).reshape(dx_ref.shape[1:3] + (width,))
    lane = lax.broadcasted_iota(jnp.int32, (slots, LANES), 1)
    number = where_ref[2] + base + pl.program_id(0)
    tail = jnp.where(lane == number, grad_gates, 0.0).astype(bf16)
    dx_ref[0, :, :, width:] = tail.reshape(dx_ref.shape[1:3] + (LANES,))
    planes, _, _, _, deep, _, = dw_ref.shape[0], 0, 0, 0, dw_ref.shape[4], 0
    quarter = dw_ref.shape[5]
    for i, (left, right) in enumerate(((x, grad_gate_lin), (x, grad_up_lin), (g, scaled_hidden))):
        grad = dot(left, right, 0, 0).astype(bf16)
        for z in range(planes):
            for q in range(8):
                row = (z * 2 + q // 4) * deep
                col = q % 4 * quarter
                dw_ref[z, q, 0, i] = grad[row:row + deep, col:col + quarter]


def shards(
    tokens,
    lengths,
    routes,
    gain_attn,
    w_query,
    w_keyvalue,
    w_out,
    gain_mixer,
    w_router,
    w_gate,
    w_up,
    w_down,
    out_grad,
):
    nd, nt = lax.axis_size("dp"), lax.axis_size("tensor")
    dp_id, t_id = lax.axis_index("dp"), lax.axis_index("tensor")
    rows, width = tokens.shape
    group_rows, top_count = routes.shape
    seq_count = lengths.shape[0]
    seq_len = group_rows // seq_count
    experts = w_router.shape[1]
    local = experts // 8
    planes = nd // 2
    deep = width // nd
    hidden = w_gate.shape[2] * nt
    capacity = (rows * top_count * 17 + experts * 16 - 1) // (experts * 16)
    cap = -(-capacity // 16) * 16
    plane_id = (dp_id % 2) * nt + t_id
    core = t_id % 2
    z_groups = [[x + 2 * z for z in range(planes)] for x in range(2)]
    plane_groups = [[(z * 2 + x) * nt + t for x in range(2) for t in range(nt)] for z in range(planes)]

    q_cols, kv_cols = w_query.shape[1], w_keyvalue.shape[2]
    w_mine = jnp.concatenate([w_query, w_keyvalue[:, 0], w_keyvalue[:, 1], w_out], axis=1)
    w_other = hop_y(w_mine)
    cuts = [0, q_cols, q_cols + kv_cols, q_cols + 2 * kv_cols, 2 * q_cols + 2 * kv_cols]
    w_pairs = []
    for lo, hi in zip(cuts[:-1], cuts[1:]):
        w_pairs += [w_mine[:, lo:hi], w_other[:, lo:hi]]
    w_attn = lax.all_gather(jnp.concatenate(w_pairs, axis=1), "dp", axis=0, tiled=True)
    w_qkv, wo = w_attn[:, : 2 * q_cols + 4 * kv_cols], w_attn[:, 2 * q_cols + 4 * kv_cols:]

    tokens_f = tokens.astype(f32)
    inverse_attn = lax.rsqrt(jnp.mean(tokens_f * tokens_f, axis=1, keepdims=True) + epsilon)
    normed_attn = (tokens_f * inverse_attn * gain_attn[None, :]).astype(bf16)
    normed_peer = hop_c(normed_attn)

    positions = jnp.arange(group_rows, dtype=jnp.int32) % seq_len
    row_length = jnp.repeat(lengths, seq_len)
    live = positions < row_length
    ids = jnp.arange(experts, dtype=jnp.int32)
    hits_t = jnp.any(routes.T[:, None, :] == ids[None, :, None], axis=0) & live[None, :]
    order = jnp.arange(rows, dtype=jnp.int32)
    before = (order[:, None] < order[None, :]).astype(bf16)
    hits_blocks = hits_t.reshape(experts, nt, rows)
    earlier = jnp.einsum("ebr,rs->ebs", hits_blocks.astype(bf16), before, preferred_element_type=f32)
    ranks = jnp.where(hits_blocks, earlier, -1.0).astype(bf16)
    ranks = jnp.transpose(ranks.reshape(8, local, nt, rows), (2, 0, 1, 3))
    ranks = jnp.pad(ranks, ((0, 0), (0, 0), (0, 8 - local), (0, 0)), constant_values=-1.0)
    ranks = ranks.reshape(nt, 64, rows)
    ranks = jnp.stack([ranks, hop_x(ranks)])
    own_start = t_id * rows
    live_own = lax.dynamic_slice_in_dim(live, own_start, rows, 0).astype(f32)[:, None]
    routes_own = lax.dynamic_slice_in_dim(routes, own_start, rows, 0)
    lane_ids = jnp.arange(LANES, dtype=jnp.int32)
    hits_own = jnp.any(routes_own[:, :, None] == lane_ids[None, None, :], axis=1).astype(f32) * live_own
    router = jnp.pad(w_router, ((0, 0), (0, LANES - experts)))
    router_t = jnp.pad(w_router.T.reshape(8, local, width), ((0, 0), (0, 8 - local), (0, 0))).reshape(64, width)

    def for_plane(w):
        return jnp.transpose(w.reshape(deep, 8, local, hidden // nt), (1, 2, 0, 3))

    w_send = jnp.stack([for_plane(w_gate), for_plane(w_up), for_plane(w_down)], axis=2)
    groups = 2
    per = local // groups
    w_groups = []
    for i in range(groups):
        piece = lax.all_to_all(
            w_send[:, i * per:(i + 1) * per], BOTH, 0, 0, tiled=True, axis_index_groups=plane_groups
        )
        piece = piece.reshape(2, nt, per, 3, deep, hidden // nt)
        piece = jnp.transpose(piece, (2, 3, 0, 4, 1, 5)).reshape(per, 3, 2 * deep, hidden)
        w_groups.append(lax.all_gather(piece, "dp", axis_index_groups=z_groups))

    half_head = HD // 2
    exponent = 2.0 * jnp.arange(half_head, dtype=f32) / HD
    angles = jnp.arange(seq_len, dtype=f32)[:, None] * jnp.exp(-math.log(rope_base) * exponent)[None, :]
    cosine, sine = jnp.cos(angles), jnp.sin(angles)
    cos_table = jnp.concatenate([cosine] * 4, axis=1)
    sin_table = jnp.concatenate([-sine, sine] * 2, axis=1)

    place = jnp.stack(
        [core, plane_id, plane_id * local, t_id]
    ).astype(jnp.int32)
    length = lax.dynamic_slice_in_dim(lengths, own_start // seq_len, 1, 0)[0]
    where_attn = jnp.stack([core, length]).astype(jnp.int32)

    q_width, k_width = 2 * q_cols, 2 * kv_cols
    heads = q_width // HD
    q, k, v, ctx, lse, keep, send = call(
        attend_kernel,
        [
            sds((seq_len, q_width), bf16), sds((seq_len, k_width), bf16), sds((seq_len, k_width), bf16),
            sds((seq_len, q_width), bf16), sds((heads, seq_len), f32),
            sds((rows, width), bf16), sds((rows, width), bf16),
        ],
        12 * 10**9, 16 * 2**20,
        in_specs=[SM] + [VM] * 6, out_specs=[VM] * 7,
        scratch_shapes=[pltpu.VMEM((seq_len, width), bf16)],
    )(where_attn, normed_attn, normed_peer, w_qkv, wo, cos_table, sin_table)
    got = hop_c(send)
    hidden_own, normed_mix, inverse_mix = call(
        mix_norm_kernel,
        [sds((rows, width), f32), sds((rows, width), bf16), sds((rows, 1), f32)],
        10**7, 8 * 2**20,
        in_specs=[VM] * 5, out_specs=[VM] * 3,
    )(tokens, keep, got, live_own, gain_mixer[None, :])

    slots_shape = (local, 8, cap, width)

    def ranks_spec(stride, start):
        def index(i, where):
            j = stride * i + start
            return (j // 4, lax.bitwise_xor(where[3], j % 4), 0, 0)
        return pl.BlockSpec((1, 1, 64, rows), index)

    def whole(a):
        return pl.BlockSpec(a.shape, lambda i, where: (0,) * a.ndim)

    def dispatch(blocks, gated):
        out_specs = [pl.BlockSpec((local, 1, cap, width), lambda i, where: (0, i, 0, 0))]
        out_shape = [sds(slots_shape, bf16)]
        scratch = [pltpu.VMEM((rows, width), bf16)]
        extra = []
        if gated:
            extra = [router_t]
            out_specs.append(pl.BlockSpec((local, 1, cap, 1), lambda i, where: (0, i, 0, 0)))
            out_shape.append(sds((local, 8, cap, 1), f32))
            scratch.append(pltpu.VMEM((64, rows), f32))
        return call(
            functools.partial(dispatch_gates_kernel if gated else dispatch_kernel, local, cap),
            out_shape, 5 * 10**9, 20 * 2**20,
            grid_spec=pltpu.PrefetchScalarGridSpec(
                num_scalar_prefetch=1, grid=(8,),
                in_specs=[whole(b) for b in blocks] + [ranks_spec(1, 0)] + [whole(e) for e in extra],
                out_specs=out_specs, scratch_shapes=scratch,
            ),
        )(place, *blocks, ranks, *extra)

    (grads_in,) = dispatch(gather_plane(out_grad), False)
    rows_in, gates_in = dispatch(gather_plane(normed_mix), True)

    ys, dxs, dws = [], [], []
    for i in range(groups):
        def slot_spec(last):
            return pl.BlockSpec((1, 8, cap, last), lambda e, where, i=i: (i * per + e, 0, 0, 0))
        def out_spec(last):
            return pl.BlockSpec((1, 8, cap, last), lambda e, where: (e, 0, 0, 0))
        y, dx, dw = call(
            functools.partial(expert_kernel, i * per),
            [
                sds((per, 8, cap, width), bf16), sds((per, 8, cap, width + LANES), bf16),
                sds((planes, 8, per, 3, deep, hidden // nt), bf16),
            ],
            per * 18 * 8 * cap * width * hidden, per * 20 * 2**20,
            grid_spec=pltpu.PrefetchScalarGridSpec(
                num_scalar_prefetch=1, grid=(per,),
                in_specs=[
                    slot_spec(width), slot_spec(width), slot_spec(1),
                    pl.BlockSpec((planes, 1, 3, 2 * deep, hidden), lambda e, where: (0, e, 0, 0, 0)),
                ],
                out_specs=[
                    out_spec(width), out_spec(width + LANES),
                    pl.BlockSpec((planes, 8, 1, 3, deep, hidden // nt), lambda e, where: (0, 0, e, 0, 0, 0)),
                ],
            ),
        )(place, rows_in, grads_in, gates_in, w_groups[i])
        ys.append(y)
        dxs.append(dx)
        dws.append(dw)

    def combine(values, start):
        last = values[0].shape[-1]
        return call(
            functools.partial(combine_kernel, local, cap, groups),
            sds((4, rows, last), bf16), 25 * 10**8, 12 * 2**20,
            grid_spec=pltpu.PrefetchScalarGridSpec(
                num_scalar_prefetch=1, grid=(4,),
                in_specs=[
                    pl.BlockSpec((per, 1, cap, last), lambda i, where: (0, 2 * i + start, 0, 0)) for _ in values
                ] + [ranks_spec(2, start)],
                out_specs=pl.BlockSpec((1, rows, last), lambda i, where: (i, 0, 0)),
            ),
        )(place, *values, ranks)

    grad_terms = scatter_plane(combine(dxs, 1), combine(dxs, 0))
    grad_hidden, grad_branch, router_grad, gain_mix_grad = call(
        mix_back_kernel,
        [
            sds((rows, width), f32), sds((rows, width), bf16), sds((experts, width), f32), sds((1, width), f32),
        ],
        10**8, 12 * 2**20,
        in_specs=[VM] * 11, out_specs=[VM] * 4,
    )(
        normed_mix, hidden_own, inverse_mix, *grad_terms, out_grad, router, hits_own, live_own,
        gain_mixer[None, :],
    )
    branch_peer = hop_c(grad_branch)

    out_terms = scatter_plane(combine(ys, 1), combine(ys, 0))
    mixed = (hidden_own + sum(term.astype(f32) for term in out_terms)).astype(bf16)

    dw_qkv, dwo, keep_back, send_back = call(
        attend_back_kernel,
        [
            sds((width, q_width + 2 * k_width), bf16), sds((width, q_width), bf16),
            sds((rows, width), bf16), sds((rows, width), bf16),
        ],
        25 * 10**9, 24 * 2**20,
        in_specs=[SM] + [VM] * 13, out_specs=[VM] * 4,
        scratch_shapes=[
            pltpu.VMEM((seq_len, width), bf16), pltpu.VMEM((seq_len, width), bf16),
            pltpu.VMEM((seq_len, q_width), bf16), pltpu.VMEM((seq_len, q_width + 2 * k_width), bf16),
            pltpu.VMEM((seq_len, LANES), f32), pltpu.VMEM((seq_len, LANES), f32),
        ],
    )(
        where_attn, normed_attn, normed_peer, grad_branch, branch_peer, w_qkv, wo, cos_table, sin_table,
        q, k, v, ctx, lse,
    )
    got_back = hop_c(send_back)
    grad_tokens, gain_attn_grad = call(
        token_back_kernel,
        [sds((rows, width), bf16), sds((1, width), f32)],
        10**7, 8 * 2**20,
        in_specs=[VM] * 5, out_specs=[VM] * 2,
    )(tokens, keep_back, got_back, grad_hidden, gain_attn[None, :])

    grad_pieces = []
    for dw in dws:
        mine = lax.psum_scatter(dw, "dp", scatter_dimension=0, axis_index_groups=z_groups)
        grad_pieces.append(
            lax.all_to_all(mine, BOTH, 0, 0, tiled=True, axis_index_groups=plane_groups)
        )

    def to_owner(which):
        parts = [piece[:, :, which].astype(f32) for piece in grad_pieces]
        whole_grad = jnp.concatenate(parts, axis=1).reshape(experts, deep, hidden // nt)
        return jnp.transpose(whole_grad, (1, 0, 2))

    def halves(grad, start, cols):
        return grad[:, start:start + cols], grad[:, start + cols:start + 2 * cols]

    pieces = [
        halves(dw_qkv, 0, q_cols), halves(dw_qkv, q_width, kv_cols),
        halves(dw_qkv, q_width + k_width, kv_cols), halves(dwo, 0, q_cols),
    ]
    mine = jnp.concatenate([a for a, _ in pieces], axis=1)
    other = jnp.concatenate([b for _, b in pieces], axis=1)
    attn_grad = add16(mine, hop_y(other))
    attn_grad = lax.psum_scatter(attn_grad, "dp", scatter_dimension=0, tiled=True).astype(f32)
    grad_query = attn_grad[:, cuts[0]:cuts[1]]
    grad_keyval = jnp.stack([attn_grad[:, cuts[1]:cuts[2]], attn_grad[:, cuts[2]:cuts[3]]], axis=1)
    grad_out = attn_grad[:, cuts[3]:cuts[4]]

    small = lax.psum(jnp.concatenate([router_grad, gain_mix_grad, gain_attn_grad], axis=0), BOTH)
    return (
        mixed,
        grad_tokens,
        small[experts + 1],
        grad_query,
        grad_keyval,
        grad_out,
        small[experts],
        small[:experts].T,
        to_owner(0),
        to_owner(1),
        to_owner(2),
    )


def solution(mesh):
    placed = (
        P(("dp", "tensor"), None),
        P("dp"),
        P("dp", None),
        P(),
        P("dp", "tensor"),
        P("dp", None, "tensor"),
        P("dp", "tensor"),
        P(),
        P(),
        P("dp", None, "tensor"),
        P("dp", None, "tensor"),
        P("dp", None, "tensor"),
        P(("dp", "tensor"), None),
    )
    return jax.shard_map(
        shards,
        mesh=mesh,
        in_specs=placed,
        out_specs=(
            P(("dp", "tensor"), None),
            P(("dp", "tensor"), None),
            P(),
            P("dp", "tensor"),
            P("dp", None, "tensor"),
            P("dp", "tensor"),
            P(),
            P(),
            P("dp", None, "tensor"),
            P("dp", None, "tensor"),
            P("dp", None, "tensor"),
        ),
        check_vma=False,
    )
```

time: 4020 us -> 781 us (0.19)
  local copies, waits for them, and re-layouts: 1500 us -> 62 us
  waiting for transfers between devices: 1530 us -> 360 us
  matrix products: 612 us -> 0.24 us
  Pallas kernels: 0 us -> 191 us
  other arithmetic: 180 us -> 42.8 us
  blocking collectives: 134 us -> 64.2 us
    gather x65 -> x0, local copies, waits for them, and re-layouts: 1160 us -> none  [the longest x14 545 us: combine_routes(): combined = combined + slot_rows[slot_index[:, route_k]]]
    reduce_scatter x11 -> x3, waiting for transfers between devices: 1070 us -> 67.9 us  [the longest x1 67.9 us: shards(): lax.psum_scatter(attn_grad, 'dp', scatter_dimension=0, tiled=True)]
    dot_general x184 -> x1, matrix products: 609 us -> 0.24 us  [shards(): jnp.einsum('ebr,rs->ebs', hits_blocks.astype(bf16), before, preferred_ele...]
    all_gather x7 -> x3, waiting for transfers between devices: 340 us -> 71.6 us  [the longest x2 71.6 us: shards(): w_groups.append(lax.all_gather(piece, 'dp', axis_index_groups=z_groups))]
    dynamic_update_slice x112 -> x0, local copies, waits for them, and re-layouts: 194 us -> none  [the longest x8 60.8 us: shards(): lax.map(sequence_backward, (query_seqs, keys_seqs, values_seqs, grad_ctx_...]
    pallas_call x0 -> x13, Pallas kernels: none -> 191 us  [the longest x2 61.4 us: shards(): call(functools.partial(expert_kernel, i * per), [sds((per, 8, cap, width)...]
    ppermute x0 -> x39, waiting for transfers between devices: none -> 140 us  [hop(): return lax.ppermute(x, BOTH, pairs)]
    reduce_sum x19 -> x0, other arithmetic: 95.2 us -> none  [the longest x4 41.4 us: block_slots(): slot_gates = jnp.sum(jnp.where(match, gates_blk[None, :], 0.0), axis=1)]
  transfers between devices with their start and end apart: 19 -> 48, of which waited for: 13 -> 18; matrix products, arithmetic and copies ran while one was open for 29% -> 11% of each run, Pallas kernels for 0% -> 25%
where the time goes in v1:
time: 781 us; the launch traced here: 774 us
  waiting for transfers between devices  360 us (46%)
  Pallas kernels  191 us (24%)
  blocking collectives  64.2 us (8%)
  local copies, waits for them, and re-layouts  62 us (8%)
  other arithmetic  42.8 us (5%)
  starting transfers between devices  38.7 us (5%)
  between operations  15.1 us (2%)
    ppermute x39, waiting for transfers between devices, hop(): return lax.ppermute(x, BOTH, pairs)  140 us
    psum x1, waiting for transfers between devices, shards(): lax.psum(jnp.concatenate([router_grad, gain_mix_grad, gain_attn_grad], ax...  81 us
    all_gather x2, waiting for transfers between devices, shards(): w_groups.append(lax.all_gather(piece, 'dp', axis_index_groups=z_groups))  71.6 us
    reduce_scatter x1, waiting for transfers between devices, shards(): lax.psum_scatter(attn_grad, 'dp', scatter_dimension=0, tiled=True)  67.9 us
    all_to_all x2, blocking collectives, shards(): lax.all_to_all(w_send[:, i * per:(i + 1) * per], BOTH, 0, 0, tiled=True,...  64.2 us
    pallas_call x2, Pallas kernels, shards(): call(functools.partial(expert_kernel, i * per), [sds((per, 8, cap, width)...  61.4 us
    pallas_call x4, Pallas kernels, combine(): call(functools.partial(combine_kernel, local, cap, groups), sds((4, rows,...  33.5 us
    ppermute x39, starting transfers between devices, hop(): return lax.ppermute(x, BOTH, pairs)  29.4 us
  transfers between devices with their start and end apart: 48, of which 18 were waited for; matrix products, arithmetic and copies ran while one was open for 11% of the time, Pallas kernels for 25%

profile of v1, /device:TPU:0, one launch (start us, length us, event | category | flops | bytes accessed | tf_op | source)
XLA Modules:
  0.0 774.3 jit_solution(16797630354048545184)
XLA Ops:
  9.3 3.0 collective-permute-start.1
  13.2 4.1 collective-permute-done.1
  21.2 28.1 %all_to_all.20 = bf16[8,2,3,128,128]{4,3,2,1,0:T(8,128)(2,1)S(1)} all-to-all(bf16[8,2,3,128,128]{4,3,2,1,0:T(8,128)(2,1)S(1)} %get-tuple-element.134), channel_id=1, replica_groups={{0,1,2,3,4,5,6,7},{8,9,10,11,12,13,14,15},{16,17,18,19,20,21,22,23},{24..., dimensions={0} | all-to-all | bytes 3145728 | tf_op jit(solution)/shard_map/all_to_all | solution.py:464
  50.5 2.0 all_gather_reshape.7
  52.6 36.1 %all_to_all.21 = bf16[8,2,3,128,128]{4,3,2,1,0:T(8,128)(2,1)S(1)} all-to-all(bf16[8,2,3,128,128]{4,3,2,1,0:T(8,128)(2,1)S(1)} %get-tuple-element.135), channel_id=1, replica_groups={{0,1,2,3,4,5,6,7},{8,9,10,11,12,13,14,15},{16,17,18,19,20,21,22,23},{24..., dimensions={0} | all-to-all | bytes 3145728 | tf_op jit(solution)/shard_map/all_to_all | solution.py:464
  100.9 3.1 slice.200.w
  104.0 2.4 slice.201.wo
  107.4 21.1 %shard_map.212 = (bf16[1024,512]{1,0:T(8,128)(2,1)}, bf16[1024,256]{1,0:T(8,128)(2,1)}, bf16[1024,256]{1,0:T(8,128)(2,1)}, bf16[1024,512]{1,0:T(8,128)(2,1)}, f3...) custom-call(s32[2]{0:T(128)} %pad_add_fusion.where_ref, bf16[512,1024]{1,0:T(8,128)(2,1)} %copy-done.4, ...), custom_call_target="tpu_custom_call" | custom-call | flops 12000000000 | bytes 16777216 | tf_op jit(solution)/shard_map/pallas_call | solution.py:486
  136.2 4.2 shard_map.213
  144.2 29.3 %collective-permute-done.12 = bf16[4,64,512]{2,1,0:T(8,128)(2,1)S(1)} collective-permute-done((bf16[4,64,512]{2,1,0:T(8,128)(2,1)S(1)}, bf16[4,64,512]{2,1,0:T(8,128)(2,1)S(1)}, u32[]{:S(2)}, u32[]{:S(2)}) %collective-permute-start.12) | collective-permute-done | bytes 262176 | tf_op jit(solution)/shard_map/ppermute | solution.py:49
  184.1 8.2 %collective-permute-done.5.refs_3_ = bf16[256,1024]{1,0:T(8,128)(2,1)} collective-permute-done((bf16[256,1024]{1,0:T(8,128)(2,1)}, bf16[256,1024]{1,0:T(8,128)(2,1)}, u32[]{:S(2)}, u32[]{:S(2)}) %collective-permute-start.5) | collective-permute-done | bytes 524320 | tf_op jit(solution)/shard_map/ppermute | solution.py:49
  195.0 12.9 %shard_map.215.g_ref = bf16[4,8,144,1024]{3,2,1,0:T(8,128)(2,1)} custom-call(s32[4]{0:T(128)} %pad_add_fusion.1.where_ref, bf16[512,1024]{1,0:T(8,128)(2,1)} %out_grad.1, bf16[512,1024]{1,0:T(8,128)(2,1)} %collective-permute-done.13.refs_1_, bf16[512,1024]{1,0:T(8,128)(2,1)} %collective-permute-done.14.refs_2_, ...), custom_call_target="tpu_custom_call" | custom-call | flops 5000000000 | bytes 20971520 | tf_op jit(solution)/shard_map/pallas_call | solution.py:526
  209.8 16.1 %shard_map.214 = (bf16[4,8,144,1024]{3,2,1,0:T(8,128)(2,1)}, f32[4,8,144,1]{3,2,1,0:T(8,128)}) custom-call(s32[4]{0:T(128)} %pad_add_fusion.1.where_ref, bf16[512,1024]{1,0:T(8,128)(2,1)} %get-tuple-element.42.refs_0_.normed, bf16[512,1024]{1,0:T(8,128)(2,1)} %collective-permute-done.3.refs_1_, bf16[512,1024]{1,0:T(8,128)(2,1)} %collective-permute-done.4.refs_2_, ...), custom_call_target="tpu_custom_call" | custom-call | flops 5000000000 | bytes 20971520 | tf_op jit(solution)/shard_map/pallas_call | solution.py:526
  225.9 30.6 %shard_map.217 = (bf16[2,8,144,1024]{3,2,1,0:T(8,128)(2,1)}, bf16[2,8,144,1152]{3,2,1,0:T(8,128)(2,1)}, bf16[4,8,2,3,128,128]{5,4,3,2,1,0:T(8,128)(2,1)}) custom-call(s32[4]{0:T(128)} %pad_add_fusion.1.where_ref, bf16[4,8,144,1024]{3,2,1,0:T(8,128)(2,1)} %get-tuple-element.43.x_ref, bf16[4,8,144,1024]{3,2,1,0:T(8,128)(2,1)} %shard_map.215.g_ref, ...), custom_call_target="tpu_custom_call" | custom-call | flops 21743271936 | bytes 41943040 | tf_op jit(solution)/shard_map/pallas_call | solution.py:545
  256.6 71.6 %all-gather.6.cloned.1.call-done.w_ref = bf16[4,2,3,256,512]{4,3,2,1,0:T(8,128)(2,1)} async-done(((bf16[1,2,3,256,512]{4,3,2,1,0:T(8,128)(2,1)}), bf16[4,2,3,256,512]{4,3,2,1,0:T(8,128)(2,1)}) %all-gather.6.cloned.1.call-update) | async-done | bytes 6291472 | tf_op jit(solution)/shard_map/all_gather | solution.py:469
  328.1 30.8 %shard_map.216 = (bf16[2,8,144,1024]{3,2,1,0:T(8,128)(2,1)}, bf16[2,8,144,1152]{3,2,1,0:T(8,128)(2,1)}, bf16[4,8,2,3,128,128]{5,4,3,2,1,0:T(8,128)(2,1)}) custom-call(s32[4]{0:T(128)} %pad_add_fusion.1.where_ref, bf16[4,8,144,1024]{3,2,1,0:T(8,128)(2,1)} %get-tuple-element.43.x_ref, bf16[4,8,144,1024]{3,2,1,0:T(8,128)(2,1)} %shard_map.215.g_ref, ...), custom_call_target="tpu_custom_call" | custom-call | flops 21743271936 | bytes 41943040 | tf_op jit(solution)/shard_map/pallas_call | solution.py:545
  359.0 8.6 %shard_map.221 = bf16[4,512,1152]{2,1,0:T(8,128)(2,1)} custom-call(s32[4]{0:T(128)} %pad_add_fusion.1.where_ref, bf16[2,8,144,1152]{3,2,1,0:T(8,128)(2,1)} %get-tuple-element.48.refs_0_, bf16[2,8,144,1152]{3,2,1,0:T(8,128)(2,1)} %get-tuple-element.49.refs_1_, bf16[2,4,64,512]{3,2,1,0:T(8,128)(2,1)} %pad_maximum_fusion.9.refs_10_.refs_2_), custom_call_target="tpu_custom_call" | custom-call | flops 2500000000 | bytes 12582912 | tf_op jit(solution)/shard_map/pallas_call | solution.py:570
  367.7 9.0 %shard_map.220 = bf16[4,512,1152]{2,1,0:T(8,128)(2,1)} custom-call(s32[4]{0:T(128)} %pad_add_fusion.1.where_ref, bf16[2,8,144,1152]{3,2,1,0:T(8,128)(2,1)} %get-tuple-element.48.refs_0_, bf16[2,8,144,1152]{3,2,1,0:T(8,128)(2,1)} %get-tuple-element.49.refs_1_, bf16[2,4,64,512]{3,2,1,0:T(8,128)(2,1)} %pad_maximum_fusion.9.refs_10_.refs_2_), custom_call_target="tpu_custom_call" | custom-call | flops 2500000000 | bytes 12582912 | tf_op jit(solution)/shard_map/pallas_call | solution.py:570
  376.6 5.0 add_convert_fusion
  387.7 2.9 fusion.7
  391.2 8.8 %collective-permute-done.31 = bf16[256,1152]{1,0:T(8,128)(2,1)S(1)} collective-permute-done((bf16[256,1152]{1,0:T(8,128)(2,1)S(1)}, bf16[256,1152]{1,0:T(8,128)(2,1)S(1)}, u32[]{:S(2)}, u32[]{:S(2)}) %collective-permute-start.31) | collective-permute-done | bytes 589856 | tf_op jit(solution)/shard_map/ppermute | solution.py:49
  407.1 2.4 slice_bitcast_fusion.part_a
  409.4 3.3 collective-permute-done.35
  412.8 12.1 %collective-permute-done.34 = bf16[256,1152]{1,0:T(8,128)(2,1)S(1)} collective-permute-done((bf16[256,1152]{1,0:T(8,128)(2,1)S(1)}, bf16[256,1152]{1,0:T(8,128)(2,1)S(1)}, u32[]{:S(2)}, u32[]{:S(2)}) %collective-permute-start.34) | collective-permute-done | bytes 589856 | tf_op jit(solution)/shard_map/ppermute | solution.py:49
  424.8 2.2 pad_maximum_fusion.3.part_c
  427.0 4.9 collective-permute-done.32
  433.0 8.1 %shard_map.222 = (f32[512,1024]{1,0:T(8,128)}, bf16[512,1024]{1,0:T(8,128)(2,1)}, f32[32,1024]{1,0:T(8,128)}, f32[1,1024]{1,0:T(1,128)}) custom-call(bf16[512,1024]{1,0:T(8,128)(2,1)} %get-tuple-element.42.refs_0_.normed, f32[512,1024]{1,0:T(8,128)} %get-tuple-element.41.hidden_in, f32[512,1]{1,0:T(8,128)} %get-tuple-element.47.inv, ...), custom_call_target="tpu_custom_call" | custom-call | flops 100000000 | bytes 12582912 | tf_op jit(solution)/shard_map/pallas_call | solution.py:583
  441.1 7.9 %shard_map.219 = bf16[4,512,1024]{2,1,0:T(8,128)(2,1)} custom-call(s32[4]{0:T(128)} %pad_add_fusion.1.where_ref, bf16[2,8,144,1024]{3,2,1,0:T(8,128)(2,1)} %get-tuple-element.45.refs_0_, bf16[2,8,144,1024]{3,2,1,0:T(8,128)(2,1)} %get-tuple-element.46.refs_1_, bf16[2,4,64,512]{3,2,1,0:T(8,128)(2,1)} %pad_maximum_fusion.9.refs_10_.refs_2_), custom_call_target="tpu_custom_call" | custom-call | flops 2500000000 | bytes 12582912 | tf_op jit(solution)/shard_map/pallas_call | solution.py:570
  450.6 29.3 %shard_map.223 = (bf16[1024,1024]{1,0:T(8,128)(2,1)}, bf16[1024,512]{1,0:T(8,128)(2,1)}, bf16[512,1024]{1,0:T(8,128)(2,1)}, bf16[512,1024]{1,0:T(8,128)(2,1)}) custom-call(s32[2]{0:T(128)} %pad_add_fusion.where_ref, bf16[512,1024]{1,0:T(8,128)(2,1)} %copy-done.4, bf16[512,1024]{1,0:T(8,128)(2,1)} %copy-done.19, bf16[512,1024]{1,0:T(8,128)(2,1)} %get-tuple-element.50.gb_own, ...), custom_call_target="tpu_custom_call" | custom-call | flops 24999999488 | bytes 25165824 | tf_op jit(solution)/shard_map/pallas_call | solution.py:599
  483.8 2.8 collective-permute-done.37.got
  486.6 4.6 shard_map.224
  492.6 26.2 %collective-permute-done.38 = bf16[1024,768]{1,0:T(8,128)(2,1)} collective-permute-done((bf16[1024,768]{1,0:T(8,128)(2,1)S(1)}, bf16[1024,768]{1,0:T(8,128)(2,1)}, u32[]{:S(2)}, u32[]{:S(2)}) %collective-permute-start.38) | collective-permute-done | bytes 1572896 | tf_op jit(solution)/shard_map/ppermute | solution.py:49
  518.8 3.0 add_convert_fusion.2
  521.8 8.0 %shard_map.218 = bf16[4,512,1024]{2,1,0:T(8,128)(2,1)} custom-call(s32[4]{0:T(128)} %pad_add_fusion.1.where_ref, bf16[2,8,144,1024]{3,2,1,0:T(8,128)(2,1)} %get-tuple-element.45.refs_0_, bf16[2,8,144,1024]{3,2,1,0:T(8,128)(2,1)} %get-tuple-element.46.refs_1_, bf16[2,4,64,512]{3,2,1,0:T(8,128)(2,1)} %pad_maximum_fusion.9.refs_10_.refs_2_), custom_call_target="tpu_custom_call" | custom-call | flops 2500000000 | bytes 12582912 | tf_op jit(solution)/shard_map/pallas_call | solution.py:570
  529.9 7.6 add_convert_fusion.1
  537.4 4.3 all-to-all-start.3
  541.7 2.7 slice_bitcast_fusion.15
  548.5 25.2 %collective-permute-done.24 = bf16[256,1024]{1,0:T(8,128)(2,1)S(1)} collective-permute-done((bf16[256,1024]{1,0:T(8,128)(2,1)S(1)}, bf16[256,1024]{1,0:T(8,128)(2,1)S(1)}, u32[]{:S(2)}, u32[]{:S(2)}) %collective-permute-start.24) | collective-permute-done | bytes 524320 | tf_op jit(solution)/shard_map/ppermute | solution.py:49
  573.7 2.6 fusion.11
  578.3 2.7 copy.104
  581.1 4.4 all-to-all-start.2
  585.6 11.1 %collective-permute-done.25 = bf16[256,1024]{1,0:T(8,128)(2,1)} collective-permute-done((bf16[256,1024]{1,0:T(8,128)(2,1)}, bf16[256,1024]{1,0:T(8,128)(2,1)}, u32[]{:S(2)}, u32[]{:S(2)}) %collective-permute-start.25) | collective-permute-done | bytes 524320 | tf_op jit(solution)/shard_map/ppermute | solution.py:49
  596.7 3.3 fusion.5
  599.9 81.0 %all-reduce.5.cloned.1.call-done = f32[34,1024]{1,0:T(8,128)} async-done(((f32[34,1024]{1,0:T(8,128)}), f32[34,1024]{1,0:T(8,128)}) %all-reduce.5.cloned.1.call-update) | async-done | bytes 139280 | tf_op jit(solution)/shard_map/psum | solution.py:651
  683.9 67.9 %reduce-scatter.4.cloned.1.call-done = bf16[128,768]{1,0:T(8,128)(2,1)} async-done(((bf16[1024,768]{1,0:T(8,128)(2,1)}), bf16[128,768]{1,0:T(8,128)(2,1)}) %reduce-scatter.4.cloned.1.call-update) | async-done | bytes 196624 | tf_op jit(solution)/shard_map/reduce_scatter | solution.py:646
  758.6 2.5 copy.129
  761.5 2.5 copy.130
  764.5 2.5 copy.131
  (218 shorter events, 86.2 us)
Async XLA Ops:
  7.2 93.7 %all-gather.4.cloned.1.call-start = ((), (), s32[]{:S(2)}) async-start(), calls=%async_computation.7 | async-start | bytes 3538944 | tf_op jit(solution)/shard_map/all_gather | solution.py:426
  9.3 7.9 %collective-permute-start.1 = (bf16[128,768]{1,0:T(8,128)(2,1)S(1)}, bf16[128,768]{1,0:T(8,128)(2,1)S(1)}, u32[]{:S(2)}, u32[]{:S(2)}) collective-permute-start(bf16[128,768]{1,0:T(8,128)(2,1)S(1)} %pad_maximum_fusion.10), channel_id=1, source_target_pairs={{0,2},{1,3},{2,0},{3,1},{4,6},{5,7},{6,4},{7,5},{8,10},{9,11},{10,... | collective-permute-start | bytes 589832 | tf_op jit(solution)/shard_map/ppermute | solution.py:49
  18.9 207.0 %all-gather.8.cloned.1.call-start = ((), (), s32[]{:S(2)}) async-start(), calls=%async_computation.9 | async-start | bytes 7864320 | tf_op jit(solution)/shard_map/all_gather | solution.py:469
  52.6 275.6 %all-gather.6.cloned.1.call-start = ((), (), s32[]{:S(2)}) async-start(), calls=%async_computation.8 | async-start | bytes 7864320 | tf_op jit(solution)/shard_map/all_gather | solution.py:469
  92.0 445.4 %reduce-scatter.8.cloned.1.call-start = ((), (), s32[]{:S(2)}) async-start(), calls=%async_computation.13 | async-start | bytes 7864320 | tf_op jit(solution)/shard_map/reduce_scatter | solution.py:626
  93.0 13.4 %collective-permute-start = (bf16[512,1024]{1,0:T(8,128)(2,1)S(1)}, bf16[512,1024]{1,0:T(8,128)(2,1)S(1)}, u32[]{:S(2)}, u32[]{:S(2)}) collective-permute-start(bf16[512,1024]{1,0:T(8,128)(2,1)S(1)} %fusion.2.own), channel_id=1, source_target_pairs={{0,1},{1,0},{2,3},{3,2},{4,5},{5,4},{6,7},{7,6},{8,9},{9,8},{10,11... | collective-permute-start | bytes 3145736 | tf_op jit(solution)/shard_map/ppermute | solution.py:49
  93.2 36.8 %collective-permute-start.13 = (bf16[512,1024]{1,0:T(8,128)(2,1)S(1)}, bf16[512,1024]{1,0:T(8,128)(2,1)}, u32[]{:S(2)}, u32[]{:S(2)}) collective-permute-start(bf16[512,1024]{1,0:T(8,128)(2,1)S(1)} %copy-done.10), channel_id=1, source_target_pairs={{0,2},{1,3},{2,0},{3,1},{4,6},{5,7},{6,4},{7,5},{8,10},{9,11},{10,... | collective-permute-start | bytes 3145736 | tf_op jit(solution)/shard_map/ppermute | solution.py:49
  94.6 38.0 %collective-permute-start.14 = (bf16[512,1024]{1,0:T(8,128)(2,1)S(1)}, bf16[512,1024]{1,0:T(8,128)(2,1)}, u32[]{:S(2)}, u32[]{:S(2)}) collective-permute-start(bf16[512,1024]{1,0:T(8,128)(2,1)S(1)} %copy-done.10), channel_id=1, source_target_pairs={{0,4},{1,5},{2,6},{3,7},{4,0},{5,1},{6,2},{7,3},{8,12},{9,13},{10,... | collective-permute-start | bytes 3145736 | tf_op jit(solution)/shard_map/ppermute | solution.py:49
  128.4 6.8 collective-permute-start.2
  131.1 42.5 %collective-permute-start.15 = (bf16[256,1024]{1,0:T(8,128)(2,1)S(1)}, bf16[256,1024]{1,0:T(8,128)(2,1)}, u32[]{:S(2)}, u32[]{:S(2)}) collective-permute-start(bf16[256,1024]{1,0:T(8,128)(2,1)S(1)} %slice.204), channel_id=1, source_target_pairs={{0,4},{1,5},{2,6},{3,7},{4,0},{5,1},{6,2},{7,3},{8,12},{9,13},{10,... | collective-permute-start | bytes 1572872 | tf_op jit(solution)/shard_map/ppermute | solution.py:49
  134.5 39.5 %collective-permute-start.16 = (bf16[256,1024]{1,0:T(8,128)(2,1)}, bf16[256,1024]{1,0:T(8,128)(2,1)}, u32[]{:S(2)}, u32[]{:S(2)}) collective-permute-start(bf16[256,1024]{1,0:T(8,128)(2,1)} %slice.205), channel_id=1, source_target_pairs={{0,2},{1,3},{2,0},{3,1},{4,6},{5,7},{6,4},{7,5},{8,10},{9,11},{10,... | collective-permute-start | bytes 1572872 | tf_op jit(solution)/shard_map/ppermute | solution.py:49
  140.4 33.7 %collective-permute-start.3 = (bf16[512,1024]{1,0:T(8,128)(2,1)}, bf16[512,1024]{1,0:T(8,128)(2,1)}, u32[]{:S(2)}, u32[]{:S(2)}) collective-permute-start(bf16[512,1024]{1,0:T(8,128)(2,1)} %get-tuple-element.42.refs_0_.normed), channel_id=1, source_target_pairs={{0,2},{1,3},{2,0},{3,1},{4,6},{5,7},{6,4},{7,5},{8,10},{9,11},{10,... | collective-permute-start | bytes 3145736 | tf_op jit(solution)/shard_map/ppermute | solution.py:49
  141.8 32.8 %collective-permute-start.4 = (bf16[512,1024]{1,0:T(8,128)(2,1)}, bf16[512,1024]{1,0:T(8,128)(2,1)}, u32[]{:S(2)}, u32[]{:S(2)}) collective-permute-start(bf16[512,1024]{1,0:T(8,128)(2,1)} %get-tuple-element.42.refs_0_.normed), channel_id=1, source_target_pairs={{0,4},{1,5},{2,6},{3,7},{4,0},{5,1},{6,2},{7,3},{8,12},{9,13},{10,... | collective-permute-start | bytes 3145736 | tf_op jit(solution)/shard_map/ppermute | solution.py:49
  142.6 30.9 %collective-permute-start.12 = (bf16[4,64,512]{2,1,0:T(8,128)(2,1)S(1)}, bf16[4,64,512]{2,1,0:T(8,128)(2,1)S(1)}, u32[]{:S(2)}, u32[]{:S(2)}) collective-permute-start(bf16[4,64,512]{2,1,0:T(8,128)(2,1)S(1)} %get-tuple-element.157), channel_id=1, source_target_pairs={{0,4},{1,5},{2,6},{3,7},{4,0},{5,1},{6,2},{7,3},{8,12},{9,13},{10,... | collective-permute-start | bytes 786440 | tf_op jit(solution)/shard_map/ppermute | solution.py:49
  173.6 4.1 collective-permute-start.17
  173.6 7.5 collective-permute-start.18
  174.1 8.4 %collective-permute-start.19 = (bf16[512,1024]{1,0:T(8,128)(2,1)}, bf16[512,1024]{1,0:T(8,128)(2,1)}, u32[]{:S(2)}, u32[]{:S(2)}) collective-permute-start(bf16[512,1024]{1,0:T(8,128)(2,1)} %collective-permute-done.14.refs_2_), channel_id=1, source_target_pairs={{0,1},{1,0},{2,3},{3,2},{4,5},{5,4},{6,7},{7,6},{8,9},{9,8},{10,11... | collective-permute-start | bytes 3145736 | tf_op jit(solution)/shard_map/ppermute | solution.py:49
  174.2 5.7 collective-permute-start.20
  174.6 6.3 collective-permute-start.21
  177.7 14.6 %collective-permute-start.5 = (bf16[256,1024]{1,0:T(8,128)(2,1)}, bf16[256,1024]{1,0:T(8,128)(2,1)}, u32[]{:S(2)}, u32[]{:S(2)}) collective-permute-start(bf16[256,1024]{1,0:T(8,128)(2,1)} %slice.202), channel_id=1, source_target_pairs={{0,4},{1,5},{2,6},{3,7},{4,0},{5,1},{6,2},{7,3},{8,12},{9,13},{10,... | collective-permute-start | bytes 1572872 | tf_op jit(solution)/shard_map/ppermute | solution.py:49
  179.8 14.3 %collective-permute-start.6 = (bf16[256,1024]{1,0:T(8,128)(2,1)S(1)}, bf16[256,1024]{1,0:T(8,128)(2,1)}, u32[]{:S(2)}, u32[]{:S(2)}) collective-permute-start(bf16[256,1024]{1,0:T(8,128)(2,1)S(1)} %slice.203), channel_id=1, source_target_pairs={{0,2},{1,3},{2,0},{3,1},{4,6},{5,7},{6,4},{7,5},{8,10},{9,11},{10,... | collective-permute-start | bytes 1572872 | tf_op jit(solution)/shard_map/ppermute | solution.py:49
  180.9 26.9 %collective-permute-start.7 = (bf16[512,1024]{1,0:T(8,128)(2,1)S(1)}, bf16[512,1024]{1,0:T(8,128)(2,1)S(1)}, u32[]{:S(2)}, u32[]{:S(2)}) collective-permute-start(bf16[512,1024]{1,0:T(8,128)(2,1)S(1)} %copy-done.11), channel_id=1, source_target_pairs={{0,1},{1,0},{2,3},{3,2},{4,5},{5,4},{6,7},{7,6},{8,9},{9,8},{10,11... | collective-permute-start | bytes 3145736 | tf_op jit(solution)/shard_map/ppermute | solution.py:49
  182.2 25.7 %collective-permute-start.8 = (bf16[512,1024]{1,0:T(8,128)(2,1)}, bf16[512,1024]{1,0:T(8,128)(2,1)}, u32[]{:S(2)}, u32[]{:S(2)}) collective-permute-start(bf16[512,1024]{1,0:T(8,128)(2,1)} %collective-permute-done.3.refs_1_), channel_id=1, source_target_pairs={{0,1},{1,0},{2,3},{3,2},{4,5},{5,4},{6,7},{7,6},{8,9},{9,8},{10,11... | collective-permute-start | bytes 3145736 | tf_op jit(solution)/shard_map/ppermute | solution.py:49
  182.4 25.4 %collective-permute-start.9 = (bf16[512,1024]{1,0:T(8,128)(2,1)}, bf16[512,1024]{1,0:T(8,128)(2,1)}, u32[]{:S(2)}, u32[]{:S(2)}) collective-permute-start(bf16[512,1024]{1,0:T(8,128)(2,1)} %collective-permute-done.4.refs_2_), channel_id=1, source_target_pairs={{0,1},{1,0},{2,3},{3,2},{4,5},{5,4},{6,7},{7,6},{8,9},{9,8},{10,11... | collective-permute-start | bytes 3145736 | tf_op jit(solution)/shard_map/ppermute | solution.py:49
  192.3 15.6 %collective-permute-start.10 = (bf16[256,1024]{1,0:T(8,128)(2,1)}, bf16[256,1024]{1,0:T(8,128)(2,1)S(1)}, u32[]{:S(2)}, u32[]{:S(2)}) collective-permute-start(bf16[256,1024]{1,0:T(8,128)(2,1)} %collective-permute-done.5.refs_3_), channel_id=1, source_target_pairs={{0,1},{1,0},{2,3},{3,2},{4,5},{5,4},{6,7},{7,6},{8,9},{9,8},{10,11... | collective-permute-start | bytes 1572872 | tf_op jit(solution)/shard_map/ppermute | solution.py:49
  194.1 13.8 %collective-permute-start.11 = (bf16[256,1024]{1,0:T(8,128)(2,1)}, bf16[256,1024]{1,0:T(8,128)(2,1)S(1)}, u32[]{:S(2)}, u32[]{:S(2)}) collective-permute-start(bf16[256,1024]{1,0:T(8,128)(2,1)} %collective-permute-done.6.refs_4_), channel_id=1, source_target_pairs={{0,1},{1,0},{2,3},{3,2},{4,5},{5,4},{6,7},{7,6},{8,9},{9,8},{10,11... | collective-permute-start | bytes 1572872 | tf_op jit(solution)/shard_map/ppermute | solution.py:49
  256.5 321.8 %reduce-scatter.6.cloned.1.call-start = ((), (), s32[]{:S(2)}) async-start(), calls=%async_computation.12 | async-start | bytes 7864320 | tf_op jit(solution)/shard_map/reduce_scatter | solution.py:626
  367.6 9.1 %collective-permute-start.29 = (bf16[4,512,1152]{2,1,0:T(8,128)(2,1)}, bf16[4,512,1152]{2,1,0:T(8,128)(2,1)}, u32[]{:S(2)}, u32[]{:S(2)}) collective-permute-start(bf16[4,512,1152]{2,1,0:T(8,128)(2,1)} %shard_map.221), channel_id=1, source_target_pairs={{0,1},{1,0},{2,3},{3,2},{4,5},{5,4},{6,7},{7,6},{8,9},{9,8},{10,11... | collective-permute-start | bytes 14155784 | tf_op jit(solution)/shard_map/ppermute | solution.py:49
  367.6 313.3 %all-reduce.5.cloned.1.call-start = ((), (), s32[]{:S(2)}) async-start(), calls=%async_computation.10 | async-start | bytes 327680 | tf_op jit(solution)/shard_map/psum | solution.py:651
  383.9 16.1 %collective-permute-start.31 = (bf16[256,1152]{1,0:T(8,128)(2,1)S(1)}, bf16[256,1152]{1,0:T(8,128)(2,1)S(1)}, u32[]{:S(2)}, u32[]{:S(2)}) collective-permute-start(bf16[256,1152]{1,0:T(8,128)(2,1)S(1)} %get-tuple-element.126), channel_id=1, source_target_pairs={{0,2},{1,3},{2,0},{3,1},{4,6},{5,7},{6,4},{7,5},{8,10},{9,11},{10,... | collective-permute-start | bytes 1769480 | tf_op jit(solution)/shard_map/ppermute | solution.py:49
  385.4 15.5 %collective-permute-start.33 = (bf16[256,1152]{1,0:T(8,128)(2,1)S(1)}, bf16[256,1152]{1,0:T(8,128)(2,1)}, u32[]{:S(2)}, u32[]{:S(2)}) collective-permute-start(bf16[256,1152]{1,0:T(8,128)(2,1)S(1)} %get-tuple-element.124), channel_id=1, source_target_pairs={{0,4},{1,5},{2,6},{3,7},{4,0},{5,1},{6,2},{7,3},{8,12},{9,13},{10,... | collective-permute-start | bytes 1769480 | tf_op jit(solution)/shard_map/ppermute | solution.py:49
  390.6 22.2 %collective-permute-start.35 = (bf16[256,1152]{1,0:T(8,128)(2,1)S(1)}, bf16[256,1152]{1,0:T(8,128)(2,1)}, u32[]{:S(2)}, u32[]{:S(2)}) collective-permute-start(bf16[256,1152]{1,0:T(8,128)(2,1)S(1)} %get-tuple-element.125), channel_id=1, source_target_pairs={{0,2},{1,3},{2,0},{3,1},{4,6},{5,7},{6,4},{7,5},{8,10},{9,11},{10,... | collective-permute-start | bytes 1769480 | tf_op jit(solution)/shard_map/ppermute | solution.py:49
  402.5 22.3 %collective-permute-start.34 = (bf16[256,1152]{1,0:T(8,128)(2,1)S(1)}, bf16[256,1152]{1,0:T(8,128)(2,1)S(1)}, u32[]{:S(2)}, u32[]{:S(2)}) collective-permute-start(bf16[256,1152]{1,0:T(8,128)(2,1)S(1)} %get-tuple-element.122), channel_id=1, source_target_pairs={{0,2},{1,3},{2,0},{3,1},{4,6},{5,7},{6,4},{7,5},{8,10},{9,11},{10,... | collective-permute-start | bytes 1769480 | tf_op jit(solution)/shard_map/ppermute | solution.py:49
  405.0 22.0 %collective-permute-start.30 = (bf16[256,1152]{1,0:T(8,128)(2,1)S(1)}, bf16[256,1152]{1,0:T(8,128)(2,1)S(1)}, u32[]{:S(2)}, u32[]{:S(2)}) collective-permute-start(bf16[256,1152]{1,0:T(8,128)(2,1)S(1)} %get-tuple-element.127), channel_id=1, source_target_pairs={{0,4},{1,5},{2,6},{3,7},{4,0},{5,1},{6,2},{7,3},{8,12},{9,13},{10,... | collective-permute-start | bytes 1769480 | tf_op jit(solution)/shard_map/ppermute | solution.py:49
  406.5 25.4 %collective-permute-start.32 = (bf16[256,1152]{1,0:T(8,128)(2,1)S(1)}, bf16[256,1152]{1,0:T(8,128)(2,1)S(1)}, u32[]{:S(2)}, u32[]{:S(2)}) collective-permute-start(bf16[256,1152]{1,0:T(8,128)(2,1)S(1)} %get-tuple-element.123), channel_id=1, source_target_pairs={{0,4},{1,5},{2,6},{3,7},{4,0},{5,1},{6,2},{7,3},{8,12},{9,13},{10,... | collective-permute-start | bytes 1769480 | tf_op jit(solution)/shard_map/ppermute | solution.py:49
  441.1 8.5 %collective-permute-start.36 = (bf16[512,1024]{1,0:T(8,128)(2,1)}, bf16[512,1024]{1,0:T(8,128)(2,1)S(1)}, u32[]{:S(2)}, u32[]{:S(2)}) collective-permute-start(bf16[512,1024]{1,0:T(8,128)(2,1)} %get-tuple-element.50.gb_own), channel_id=1, source_target_pairs={{0,1},{1,0},{2,3},{3,2},{4,5},{5,4},{6,7},{7,6},{8,9},{9,8},{10,11... | collective-permute-start | bytes 3145736 | tf_op jit(solution)/shard_map/ppermute | solution.py:49
  449.0 80.8 %collective-permute-start.22 = (bf16[4,512,1024]{2,1,0:T(8,128)(2,1)}, bf16[4,512,1024]{2,1,0:T(8,128)(2,1)}, u32[]{:S(2)}, u32[]{:S(2)}) collective-permute-start(bf16[4,512,1024]{2,1,0:T(8,128)(2,1)} %shard_map.219), channel_id=1, source_target_pairs={{0,1},{1,0},{2,3},{3,2},{4,5},{5,4},{6,7},{7,6},{8,9},{9,8},{10,11... | collective-permute-start | bytes 12582920 | tf_op jit(solution)/shard_map/ppermute | solution.py:49
  482.3 36.5 %collective-permute-start.38 = (bf16[1024,768]{1,0:T(8,128)(2,1)S(1)}, bf16[1024,768]{1,0:T(8,128)(2,1)}, u32[]{:S(2)}, u32[]{:S(2)}) collective-permute-start(bf16[1024,768]{1,0:T(8,128)(2,1)S(1)} %pad_maximum_fusion.1), channel_id=1, source_target_pairs={{0,2},{1,3},{2,0},{3,1},{4,6},{5,7},{6,4},{7,5},{8,10},{9,11},{10,... | collective-permute-start | bytes 4718600 | tf_op jit(solution)/shard_map/ppermute | solution.py:49
  483.8 2.8 collective-permute-start.37
  492.5 259.3 %reduce-scatter.4.cloned.1.call-start = ((), (), s32[]{:S(2)}) async-start(), calls=%async_computation.11 | async-start | bytes 1769472 | tf_op jit(solution)/shard_map/reduce_scatter | solution.py:646
  537.4 43.7 %all-to-all-start.3 = ((bf16[8,2,3,128,128]{4,3,2,1,0:T(8,128)(2,1)}), bf16[8,2,3,128,128]{4,3,2,1,0:T(8,128)(2,1)}, u32[]{:S(2)}, u32[]{:S(2)}) async-start(bf16[8,2,3,128,128]{4,3,2,1,0:T(8,128)(2,1)} %bitcast.156), calls=%async_computation.6 | async-start | bytes 3145728 | tf_op jit(solution)/shard_map/all_to_all | solution.py:628
  544.4 29.3 %collective-permute-start.24 = (bf16[256,1024]{1,0:T(8,128)(2,1)S(1)}, bf16[256,1024]{1,0:T(8,128)(2,1)S(1)}, u32[]{:S(2)}, u32[]{:S(2)}) collective-permute-start(bf16[256,1024]{1,0:T(8,128)(2,1)S(1)} %get-tuple-element.132), channel_id=1, source_target_pairs={{0,2},{1,3},{2,0},{3,1},{4,6},{5,7},{6,4},{7,5},{8,10},{9,11},{10,... | collective-permute-start | bytes 1572872 | tf_op jit(solution)/shard_map/ppermute | solution.py:49
  546.3 27.4 %collective-permute-start.26 = (bf16[256,1024]{1,0:T(8,128)(2,1)S(1)}, bf16[256,1024]{1,0:T(8,128)(2,1)S(1)}, u32[]{:S(2)}, u32[]{:S(2)}) collective-permute-start(bf16[256,1024]{1,0:T(8,128)(2,1)S(1)} %get-tuple-element.130), channel_id=1, source_target_pairs={{0,4},{1,5},{2,6},{3,7},{4,0},{5,1},{6,2},{7,3},{8,12},{9,13},{10,... | collective-permute-start | bytes 1572872 | tf_op jit(solution)/shard_map/ppermute | solution.py:49
  547.8 37.7 %collective-permute-start.23 = (bf16[256,1024]{1,0:T(8,128)(2,1)}, bf16[256,1024]{1,0:T(8,128)(2,1)S(1)}, u32[]{:S(2)}, u32[]{:S(2)}) collective-permute-start(bf16[256,1024]{1,0:T(8,128)(2,1)} %get-tuple-element.133), channel_id=1, source_target_pairs={{0,4},{1,5},{2,6},{3,7},{4,0},{5,1},{6,2},{7,3},{8,12},{9,13},{10,... | collective-permute-start | bytes 1572872 | tf_op jit(solution)/shard_map/ppermute | solution.py:49
  548.3 37.2 %collective-permute-start.28 = (bf16[256,1024]{1,0:T(8,128)(2,1)}, bf16[256,1024]{1,0:T(8,128)(2,1)S(1)}, u32[]{:S(2)}, u32[]{:S(2)}) collective-permute-start(bf16[256,1024]{1,0:T(8,128)(2,1)} %get-tuple-element.131), channel_id=1, source_target_pairs={{0,2},{1,3},{2,0},{3,1},{4,6},{5,7},{6,4},{7,5},{8,10},{9,11},{10,... | collective-permute-start | bytes 1572872 | tf_op jit(solution)/shard_map/ppermute | solution.py:49
  576.4 20.3 %collective-permute-start.25 = (bf16[256,1024]{1,0:T(8,128)(2,1)}, bf16[256,1024]{1,0:T(8,128)(2,1)}, u32[]{:S(2)}, u32[]{:S(2)}) collective-permute-start(bf16[256,1024]{1,0:T(8,128)(2,1)} %get-tuple-element.129), channel_id=1, source_target_pairs={{0,4},{1,5},{2,6},{3,7},{4,0},{5,1},{6,2},{7,3},{8,12},{9,13},{10,... | collective-permute-start | bytes 1572872 | tf_op jit(solution)/shard_map/ppermute | solution.py:49
  577.8 18.8 %collective-permute-start.27 = (bf16[256,1024]{1,0:T(8,128)(2,1)}, bf16[256,1024]{1,0:T(8,128)(2,1)}, u32[]{:S(2)}, u32[]{:S(2)}) collective-permute-start(bf16[256,1024]{1,0:T(8,128)(2,1)} %get-tuple-element.128), channel_id=1, source_target_pairs={{0,2},{1,3},{2,0},{3,1},{4,6},{5,7},{6,4},{7,5},{8,10},{9,11},{10,... | collective-permute-start | bytes 1572872 | tf_op jit(solution)/shard_map/ppermute | solution.py:49
  581.1 175.6 %all-to-all-start.2 = ((bf16[8,2,3,128,128]{4,3,1,2,0:T(8,128)(2,1)}), bf16[8,2,3,128,128]{4,3,1,2,0:T(8,128)(2,1)}, u32[]{:S(2)}, u32[]{:S(2)}) async-start(bf16[8,2,3,128,128]{4,3,1,2,0:T(8,128)(2,1)} %copy.104), calls=%async_computation.4 | async-start | bytes 3145728 | tf_op jit(solution)/shard_map/all_to_all | solution.py:628
  (29 other events, 193.6 us)
Sparse Core Ops, SparseCore 0:
  19.0 77.5 all-gather.3
  98.2 114.0 all-gather.7
  214.5 113.5 all-gather.5
  330.3 108.9 reduce-scatter.7
  441.5 111.2 reduce-scatter.5
  558.1 122.7 all-reduce.4
  684.9 66.8 reduce-scatter.3

commit v2 on v1

--- a/solution.py
+++ b/solution.py
@@ -61,13 +61,18 @@
     return hop(x, 1, 0)
 
 
-def gather_plane(x):
+def gather_plane(x, from_y=None, from_x=None):
     half = x.shape[0] // 2
-    from_y, from_x = hop_y(x), hop_x(x)
+    if from_y is None:
+        from_y, from_x = hop_y(x), hop_x(x)
     diag_a, diag_b = hop_x(from_y[:half]), hop_y(from_x[half:])
     near = (x, from_y, from_x, diag_a, diag_b)
     far = tuple(hop_c(item) for item in near)
     return near + far
+
+
+def after(x, *others):
+    return lax.optimization_barrier((x, *others))[0]
 
 
 def add16(a, b):
@@ -85,6 +90,31 @@
     return total[0], jnp.concatenate([got_xa, got_xb]), jnp.concatenate([got_ya, got_yb])
 
 
+def gather_z(x, planes, z_groups, by_hops):
+    if by_hops and planes == 4:
+        return (x,) + tuple(hop(x, 2 * k, 0) for k in range(1, planes))
+    return (lax.all_gather(x, "dp", axis_index_groups=z_groups),)
+
+
+def sum_z(x, planes, z, z_groups):
+    if planes != 4:
+        return lax.psum_scatter(x, "dp", scatter_dimension=0, axis_index_groups=z_groups).astype(f32)
+    total = lax.dynamic_index_in_dim(x, z, 0, False).astype(f32)
+    for k in range(1, planes):
+        total += hop(lax.dynamic_index_in_dim(x, z ^ k, 0, False), 2 * k, 0).astype(f32)
+    return total
+
+
+def sum_all(x, nd):
+    for bit in (1, 2):
+        x = x + hop(x, 0, bit)
+    bit = 1
+    while bit < nd:
+        x = x + hop(x, bit, 0)
+        bit *= 2
+    return x
+
+
 def swap_halves(v):
     lane = lax.broadcasted_iota(jnp.int32, v.shape, 1)
     left = pltpu.roll(v, LANES - HD // 2, 1)
@@ -123,30 +153,30 @@
 
 
 def attend_kernel(
-    where_ref, own, peer, w, wo, cos, sin,
+    where_ref, rows, w, cos, sin,
     q_ref, k_ref, v_ref, ctx_ref, lse_ref, keep_ref, send_ref,
-    rows_ref,
 ):
     core, length = where_ref[0], where_ref[1]
-    half = own.shape[0]
-    seq = 2 * half
-    qw, kw = q_ref.shape[1], k_ref.shape[1]
-    rows_ref[pl.ds(pl.multiple_of(core * half, half), half)] = own[...]
-    rows_ref[pl.ds(pl.multiple_of((1 - core) * half, half), half)] = peer[...]
+    seq, width = rows.shape
+    half = seq // 2
+    kw = k_ref.shape[1] // 2
+    qw = 2 * kw
+    cut = qw + 2 * kw
     for blk in range(seq // QBLK):
         sl = slice(blk * QBLK, (blk + 1) * QBLK)
-        pre = dot(rows_ref[sl], w[...], 1, 0)
         c, s = cos[sl], sin[sl]
-        for tile in range((qw + kw) // LANES):
-            col = pre[:, tile * LANES:(tile + 1) * LANES]
-            turned = (col * c + swap_halves(col) * s).astype(bf16)
-            if tile * LANES < qw:
-                q_ref[sl, tile * LANES:(tile + 1) * LANES] = turned
-            else:
-                at = tile * LANES - qw
-                k_ref[sl, at:at + LANES] = turned
-        v_ref[sl] = pre[:, qw + kw:].astype(bf16)
-    for g in range(qw // LANES):
+        for y in range(2):
+            pre = dot(rows[sl], w[y, :, :, :cut].reshape(width, cut), 1, 0)
+            for tile in range((qw + kw) // LANES):
+                col = pre[:, tile * LANES:(tile + 1) * LANES]
+                turned = (col * c + swap_halves(col) * s).astype(bf16)
+                if tile * LANES < qw:
+                    q_ref[sl, y * qw + tile * LANES:y * qw + (tile + 1) * LANES] = turned
+                else:
+                    at = y * kw + tile * LANES - qw
+                    k_ref[sl, at:at + LANES] = turned
+            v_ref[sl, y * kw:(y + 1) * kw] = pre[:, qw + kw:].astype(bf16)
+    for g in range(2 * qw // LANES):
         kv = slice(g // 2 * LANES, (g // 2 + 1) * LANES)
         cols = slice(g * LANES, (g + 1) * LANES)
         kd = spread_head(k_ref[:, kv], g % 2)
@@ -165,33 +195,38 @@
             lse = peak + jnp.log(total)
             lse_ref[2 * g:2 * g + 1, sl] = lse[:, :QBLK]
             lse_ref[2 * g + 1:2 * g + 2, sl] = lse[:, QBLK:]
-    mine = ctx_ref[pl.ds(pl.multiple_of(core * half, half), half)]
-    other = ctx_ref[pl.ds(pl.multiple_of((1 - core) * half, half), half)]
-    send_ref[...] = dot(other, wo[...], 1, 1).astype(bf16)
-    keep_ref[...] = dot(mine, wo[...], 1, 1).astype(bf16)
+    for out_ref, side in ((send_ref, 1 - core), (keep_ref, core)):
+        at = pl.ds(pl.multiple_of(side * half, half), half)
+        out = dot(ctx_ref[at, :qw], w[0, :, :, cut:].reshape(width, qw), 1, 1)
+        out += dot(ctx_ref[at, qw:], w[1, :, :, cut:].reshape(width, qw), 1, 1)
+        out_ref[...] = out.astype(bf16)
 
 
 def attend_back_kernel(
-    where_ref, own, peer, gb_own, gb_peer, w, wo, cos, sin, q_ref, k_ref, v_ref, ctx_ref, lse_ref,
-    dw_ref, dwo_ref, keep_ref, send_ref,
-    rows_ref, gb_ref, gc_ref, dqkv_ref, dk_ref, dv_ref,
+    where_ref, rows, gb_own, gb_peer, w, cos, sin, q_ref, k_ref, v_ref, ctx_ref, lse_ref,
+    dw_ref, keep_ref, send_ref,
+    gb_ref, gc_ref, dqkv_ref, dk_ref, dv_ref,
 ):
     core, length = where_ref[0], where_ref[1]
-    half = own.shape[0]
-    seq = 2 * half
-    qw, kw = q_ref.shape[1], k_ref.shape[1]
+    seq, width = rows.shape
+    half = seq // 2
+    kw = k_ref.shape[1] // 2
+    qw = 2 * kw
+    cut = qw + 2 * kw
+    per_dp = dw_ref.shape[1:3]
     at_own = pl.ds(pl.multiple_of(core * half, half), half)
     at_peer = pl.ds(pl.multiple_of((1 - core) * half, half), half)
-    rows_ref[at_own] = own[...]
-    rows_ref[at_peer] = peer[...]
     gb_ref[at_own] = gb_own[...]
     gb_ref[at_peer] = gb_peer[...]
-    gc_ref[...] = dot(gb_ref[...], wo[...], 1, 0).astype(bf16)
-    dwo_ref[...] = dot(gb_ref[...], ctx_ref[...], 0, 0).astype(bf16)
+    for y in range(2):
+        part = slice(y * qw, (y + 1) * qw)
+        gc_ref[:, part] = dot(gb_ref[...], w[y, :, :, cut:].reshape(width, qw), 1, 0).astype(bf16)
+        dw_ref[y, :, :, cut:] = dot(gb_ref[...], ctx_ref[:, part], 0, 0).astype(bf16).reshape(per_dp + (qw,))
     scale = 1.0 / math.sqrt(HD)
-    folded = {}
-    for g in range(qw // LANES):
-        kv = slice(g // 2 * LANES, (g // 2 + 1) * LANES)
+    folded = None
+    for g in range(2 * qw // LANES):
+        y = g // 2
+        kv = slice(y * LANES, (y + 1) * LANES)
         cols = slice(g * LANES, (g + 1) * LANES)
         kd = spread_head(k_ref[:, kv], g % 2)
         kd_t = kd.T
@@ -218,7 +253,8 @@
                 dv_ref[:top] += dv
             tile = jnp.where(in_head(dq[:QBLK], 0), dq[:QBLK], dq[QBLK:])
             back = tile * cos[sl] - swap_halves(tile) * sin[sl]
-            dqkv_ref[sl, cols] = back.astype(bf16)
+            at = y * cut + g % 2 * LANES
+            dqkv_ref[sl, at:at + LANES] = back.astype(bf16)
         dk_all = dk_ref[...] + pltpu.roll(dk_ref[...], HD, 1)
         dv_all = dv_ref[...] + pltpu.roll(dv_ref[...], HD, 1)
         if g % 2 == 0:
@@ -226,13 +262,153 @@
         else:
             dk_pair = jnp.where(in_head(dk_all, 0), folded[0], dk_all)
             dv_pair = jnp.where(in_head(dv_all, 0), folded[1], dv_all)
-            at = qw + g // 2 * LANES
+            at = y * cut + qw
             back = dk_pair * cos[...] - swap_halves(dk_pair) * sin[...]
             dqkv_ref[:, at:at + LANES] = back.astype(bf16)
-            dqkv_ref[:, at + kw:at + kw + LANES] = dv_pair.astype(bf16)
-    send_ref[...] = dot(dqkv_ref[at_peer], w[...], 1, 1).astype(bf16)
-    keep_ref[...] = dot(dqkv_ref[at_own], w[...], 1, 1).astype(bf16)
-    dw_ref[...] = dot(rows_ref[...], dqkv_ref[...], 0, 0).astype(bf16)
+            dqkv_ref[:, at + LANES:at + 2 * LANES] = dv_pair.astype(bf16)
+            part = slice(y * cut, (y + 1) * cut)
+            dw_ref[y, :, :, :cut] = dot(rows[...], dqkv_ref[:, part], 0, 0).astype(bf16).reshape(per_dp + (cut,))
+    for out_ref, at in ((send_ref, at_peer), (keep_ref, at_own)):
+        out = dot(dqkv_ref[at, :cut], w[0, :, :, :cut].reshape(width, cut), 1, 1)
+        out += dot(dqkv_ref[at, cut:], w[1, :, :, :cut].reshape(width, cut), 1, 1)
+        out_ref[...] = out.astype(bf16)
+
+
+def deal_out(p, plane_peers, w_send, numbers, dealt, send_sem, recv_sem):
+    copies = []
+    for i, e in enumerate(numbers):
+        for j in (6, 7, 2, 4, 3, 5, 1):
+            copies.append(
+                pltpu.make_async_remote_copy(
+                    src_ref=w_send.at[p ^ j, e], dst_ref=dealt[i].at[j], send_sem=send_sem.at[i, j],
+                    recv_sem=recv_sem.at[i, j], device_id=plane_peers[j], device_id_type=pl.DeviceIdType.MESH,
+                )
+            )
+        copies.append(pltpu.make_async_copy(w_send.at[p, e], dealt[i].at[0], send_sem.at[i, 0]))
+    for copy in copies:
+        copy.start()
+    return copies
+
+
+def deal_kernel(w_send, *refs):
+    dealt, (send_sem, recv_sem) = refs[:-2], refs[-2:]
+    d, t = lax.axis_index("dp"), lax.axis_index("tensor")
+    p = d % 2 * 4 + t
+    peers = [{"dp": d // 2 * 2 + (p ^ j) // 4, "tensor": (p ^ j) % 4} for j in range(8)]
+    barrier = pltpu.get_barrier_semaphore()
+    for peer in peers[1:]:
+        pl.semaphore_signal(barrier, inc=1, device_id=peer, device_id_type=pl.DeviceIdType.MESH)
+    pl.semaphore_wait(barrier, 7)
+    for copy in deal_out(p, peers, w_send, range(len(dealt)), dealt, send_sem, recv_sem):
+        copy.wait()
+
+
+def rank_rows(lengths, routes_t, block, ranks_ref):
+    blocks, wide = ranks_ref.shape[1:3]
+    seq_len = block * blocks // lengths.shape[0]
+    local = wide // 16
+    row = lax.broadcasted_iota(jnp.int32, (wide, block), 0)
+    number = jnp.where(row % 8 < local, row // 8 * local + row % 8, -1)
+    low = lax.broadcasted_iota(jnp.int32, (block, block), 0)
+    high = lax.broadcasted_iota(jnp.int32, (block, block), 1)
+    before = (low < high).astype(f32).astype(bf16)
+    for b in range(blocks):
+        at = slice(b * block, (b + 1) * block)
+        position = lax.broadcasted_iota(jnp.int32, (wide, block), 1) + b * block % seq_len
+        hit = jnp.zeros((wide, block), jnp.bool_)
+        for k in range(routes_t.shape[0]):
+            hit = hit | (routes_t[k:k + 1, at] == number)
+        hit = hit & (position < lengths[b * block // seq_len])
+        earlier = dot(hit.astype(f32).astype(bf16), before, 1, 0)
+        ranks_ref[0, b] = jnp.where(hit, earlier, -1.0).astype(bf16)
+
+
+def gather_kernel(later, lengths, tokens, gain, routes_t, w_mine, w_send, rows_ref, w_ref, ranks_ref, *refs):
+    dealt, (send_sem, recv_sem, row_sem, deal_send, deal_recv) = refs[:-5], refs[-5:]
+    d, t = lax.axis_index("dp"), lax.axis_index("tensor")
+    planes = w_ref.shape[1] // 2
+    half = tokens.shape[0]
+    z, x, core = d // 2, d % 2, t % 2
+
+    def device(dp, tensor):
+        return {"dp": dp, "tensor": tensor}
+
+    def plane(dz):
+        return lax.rem(z + dz, planes)
+
+    x_peer, y_peer = device(z * 2 + 1 - x, t), device(d, (t + 2) % 4)
+    core_peer = device(d, t + 1 - 2 * core)
+    z_peers = [device(plane(dz) * 2 + x, t) for dz in range(1, planes)]
+    barrier = pltpu.get_barrier_semaphore()
+    p = x * 4 + t
+    plane_peers = [device(z * 2 + (p ^ j) // 4, (p ^ j) % 4) for j in range(8)]
+    for peer in [*z_peers, *plane_peers[1:]]:
+        pl.semaphore_signal(barrier, inc=1, device_id=peer, device_id_type=pl.DeviceIdType.MESH)
+    pl.semaphore_wait(barrier, planes + 6)
+
+    copies = []
+
+    def push(source, side, dp, peer):
+        copy = pltpu.make_async_remote_copy(
+            src_ref=source, dst_ref=w_ref.at[side, dp], send_sem=send_sem.at[len(copies)],
+            recv_sem=recv_sem.at[side, dp], device_id=peer, device_id_type=pl.DeviceIdType.MESH,
+        )
+        copy.start()
+        copies.append(copy)
+
+    def arrive(side, dp):
+        slot = w_ref.at[side, dp]
+        pltpu.make_async_remote_copy(
+            src_ref=slot, dst_ref=slot, send_sem=send_sem.at[0], recv_sem=recv_sem.at[side, dp],
+            device_id=x_peer, device_id_type=pl.DeviceIdType.MESH,
+        ).wait_recv()
+
+    for peer in z_peers:
+        push(w_mine, 0, d, peer)
+    push(w_mine, 0, d, x_peer)
+    push(w_mine, 1, d, y_peer)
+    deals = deal_out(p, plane_peers, w_send, later, dealt, deal_send, deal_recv)
+    values = tokens[...].astype(f32)
+    inverse = lax.rsqrt(jnp.mean(values * values, axis=1, keepdims=True) + epsilon)
+    at = pl.ds(pl.multiple_of(core * half, half), half)
+    rows_ref[at] = (values * inverse * gain[...]).astype(bf16)
+    row_copy = pltpu.make_async_remote_copy(
+        src_ref=rows_ref.at[at], dst_ref=rows_ref.at[at], send_sem=row_sem.at[0], recv_sem=row_sem.at[1],
+        device_id=core_peer, device_id_type=pl.DeviceIdType.MESH,
+    )
+    row_copy.start()
+    w_ref[0, d] = w_mine[...]
+    rank_rows(lengths, routes_t, half, ranks_ref)
+    rank_copy = pltpu.make_async_remote_copy(
+        src_ref=ranks_ref.at[0], dst_ref=ranks_ref.at[1], send_sem=row_sem.at[2], recv_sem=row_sem.at[3],
+        device_id=x_peer, device_id_type=pl.DeviceIdType.MESH,
+    )
+    rank_copy.start()
+    near = [plane(dz) * 2 + x for dz in range(planes)]
+    over = [plane(dz) * 2 + 1 - x for dz in range(planes)]
+
+    def turn(dz):
+        arrive(0, over[dz])
+        if dz < planes // 2:
+            push(w_ref.at[0, over[dz]], 1, over[dz], y_peer)
+        arrive(1, near[dz])
+        if dz >= planes // 2:
+            push(w_ref.at[1, near[dz]], 1, near[dz], x_peer)
+
+    for dz in range(1, planes):
+        arrive(0, near[dz])
+        push(w_ref.at[0, near[dz]], 0, near[dz], x_peer)
+        push(w_ref.at[0, near[dz]], 1, near[dz], y_peer)
+        turn(dz - 1)
+    turn(planes - 1)
+    for dz in range(planes):
+        arrive(1, over[dz])
+    for copy in copies:
+        copy.wait_send()
+    row_copy.wait()
+    rank_copy.wait()
+    for copy in deals:
+        copy.wait()
 
 
 def mix_norm_kernel(tokens, keep, got, live, gain, hidden_ref, normed_ref, inv_ref):
@@ -348,13 +524,46 @@
     out_ref[0] = dot(matrix, rows, 0, 0).astype(bf16)
 
 
-def expert_kernel(base, where_ref, x_ref, g_ref, gates_ref, w_ref, y_ref, dx_ref, dw_ref):
+def expert_kernel(first, steps, where_ref, x_ref, g_ref, gates_ref, *refs):
+    sources, (y_ref, dx_ref, dw_ref, w_buf, sem) = refs[:steps], refs[steps:]
+    i = pl.program_id(0)
+    last = pl.num_programs(0) - 1
+    z = where_ref[4]
+    planes = w_buf.shape[1]
+
+    def each(expert, slot, act):
+        if steps == 1:
+            act(pltpu.make_async_copy(sources[0], w_buf.at[slot], sem.at[slot, 0]))
+            return
+        for k, source in enumerate(sources):
+            act(pltpu.make_async_copy(source, w_buf.at[slot, z ^ k], sem.at[slot, k]))
+
+    @pl.when(i == 0)
+    def _():
+        each(0, 0, lambda copy: copy.start())
+
+    @pl.when(i < last)
+    def _():
+        each(i + 1, (i + 1) % 2, lambda copy: copy.start())
+
+    slot = i % 2
+    each(i, slot, lambda copy: copy.wait())
     slots, width = x_ref.shape[1] * x_ref.shape[2], x_ref.shape[3]
-    hidden = w_ref.shape[-1]
+    deep, quarter = w_buf.shape[4:]
     x = x_ref[0].reshape(slots, width)
     g = g_ref[0].reshape(slots, width)
     gates = gates_ref[0].reshape(slots, 1)
-    w_gate, w_up, w_down = (w_ref[:, 0, i].reshape(width, hidden) for i in range(3))
+
+    def weight(which):
+        rows = []
+        for plane in range(planes):
+            for side in range(2):
+                rows.append(
+                    jnp.concatenate([w_buf[slot, plane, (side * 4 + q) ^ where_ref[1], which] for q in range(4)], axis=1)
+                )
+        return jnp.concatenate(rows, axis=0)
+
+    w_gate, w_up, w_down = weight(0), weight(1), weight(2)
     gate_lin = dot(x, w_gate, 1, 0)
     up_lin = dot(x, w_up, 1, 0)
     grad_scaled = dot(g, w_down, 1, 0)
@@ -369,18 +578,16 @@
     dx = dot(grad_gate_lin, w_gate, 1, 1) + dot(grad_up_lin, w_up, 1, 1)
     dx_ref[0, :, :, :width] = dx.astype(bf16).reshape(dx_ref.shape[1:3] + (width,))
     lane = lax.broadcasted_iota(jnp.int32, (slots, LANES), 1)
-    number = where_ref[2] + base + pl.program_id(0)
+    number = where_ref[2] + first + i
     tail = jnp.where(lane == number, grad_gates, 0.0).astype(bf16)
     dx_ref[0, :, :, width:] = tail.reshape(dx_ref.shape[1:3] + (LANES,))
-    planes, _, _, _, deep, _, = dw_ref.shape[0], 0, 0, 0, dw_ref.shape[4], 0
-    quarter = dw_ref.shape[5]
-    for i, (left, right) in enumerate(((x, grad_gate_lin), (x, grad_up_lin), (g, scaled_hidden))):
+    for which, (left, right) in enumerate(((x, grad_gate_lin), (x, grad_up_lin), (g, scaled_hidden))):
         grad = dot(left, right, 0, 0).astype(bf16)
-        for z in range(planes):
+        for plane in range(planes):
             for q in range(8):
-                row = (z * 2 + q // 4) * deep
+                row = (plane * 2 + q // 4) * deep
                 col = q % 4 * quarter
-                dw_ref[z, q, 0, i] = grad[row:row + deep, col:col + quarter]
+                dw_ref[plane, q, 0, which] = grad[row:row + deep, col:col + quarter]
 
 
 def shards(
@@ -414,37 +621,59 @@
     plane_id = (dp_id % 2) * nt + t_id
     core = t_id % 2
     z_groups = [[x + 2 * z for z in range(planes)] for x in range(2)]
+    group_sizes = (1,) * local
+    groups = len(group_sizes)
     plane_groups = [[(z * 2 + x) * nt + t for x in range(2) for t in range(nt)] for z in range(planes)]
 
+    quarter = hidden // nt
+
+    def for_plane(w):
+        return jnp.transpose(w.reshape(deep, 8, local, quarter), (1, 2, 0, 3))
+
+    w_send = jnp.stack([for_plane(w_gate), for_plane(w_up), for_plane(w_down)], axis=2)
     q_cols, kv_cols = w_query.shape[1], w_keyvalue.shape[2]
+    cut = q_cols + 2 * kv_cols
     w_mine = jnp.concatenate([w_query, w_keyvalue[:, 0], w_keyvalue[:, 1], w_out], axis=1)
-    w_other = hop_y(w_mine)
-    cuts = [0, q_cols, q_cols + kv_cols, q_cols + 2 * kv_cols, 2 * q_cols + 2 * kv_cols]
-    w_pairs = []
-    for lo, hi in zip(cuts[:-1], cuts[1:]):
-        w_pairs += [w_mine[:, lo:hi], w_other[:, lo:hi]]
-    w_attn = lax.all_gather(jnp.concatenate(w_pairs, axis=1), "dp", axis=0, tiled=True)
-    w_qkv, wo = w_attn[:, : 2 * q_cols + 4 * kv_cols], w_attn[:, 2 * q_cols + 4 * kv_cols:]
-
-    tokens_f = tokens.astype(f32)
-    inverse_attn = lax.rsqrt(jnp.mean(tokens_f * tokens_f, axis=1, keepdims=True) + epsilon)
-    normed_attn = (tokens_f * inverse_attn * gain_attn[None, :]).astype(bf16)
-    normed_peer = hop_c(normed_attn)
+    pushes = 3 * planes + 2 * (planes - 1)
+    hbm = pl.BlockSpec(memory_space=pl.ANY)
+    dealt_shape = sds((8, 3, deep, quarter), bf16)
+    early = 2
+    dealt_early = pl.pallas_call(
+        deal_kernel,
+        out_shape=[dealt_shape] * early,
+        in_specs=[hbm], out_specs=[hbm] * early,
+        scratch_shapes=[pltpu.SemaphoreType.DMA((early, 8)), pltpu.SemaphoreType.DMA((early, 8))],
+        compiler_params=pltpu.CompilerParams(
+            vmem_limit_bytes=VMEM_LIMIT, collective_id=1, has_side_effects=True
+        ),
+        cost_estimate=pl.CostEstimate(flops=10**6, bytes_accessed=20 * 2**20, transcendentals=0),
+    )(w_send)
+    later = tuple(range(early, local))
+    normed_rows, w_attn, ranks, *dealt = pl.pallas_call(
+        functools.partial(gather_kernel, later),
+        out_shape=[
+            sds((2 * rows, width), bf16), sds((2, nd, deep, cut + q_cols), bf16), sds((2, nt, 64, rows), bf16),
+        ]
+        + [dealt_shape] * len(later),
+        in_specs=[SM] + [VM] * 4 + [hbm], out_specs=[VM] * 3 + [hbm] * len(later),
+        scratch_shapes=[
+            pltpu.SemaphoreType.DMA((pushes,)), pltpu.SemaphoreType.DMA((2, nd)), pltpu.SemaphoreType.DMA((4,)),
+            pltpu.SemaphoreType.DMA((len(later), 8)), pltpu.SemaphoreType.DMA((len(later), 8)),
+        ],
+        compiler_params=pltpu.CompilerParams(
+            vmem_limit_bytes=VMEM_LIMIT, collective_id=0, has_side_effects=True
+        ),
+        cost_estimate=pl.CostEstimate(flops=10**7, bytes_accessed=100 * 2**20, transcendentals=0),
+    )(lengths, tokens, gain_attn[None, :], routes.T, after(w_mine, *dealt_early), w_send)
+
+    w_groups = []
+    for n, piece in enumerate([*dealt_early, *dealt]):
+        if n > 1:
+            piece = after(piece, w_groups[n - 2][0])
+        w_groups.append(gather_z(piece, planes, z_groups, False))
 
     positions = jnp.arange(group_rows, dtype=jnp.int32) % seq_len
-    row_length = jnp.repeat(lengths, seq_len)
-    live = positions < row_length
-    ids = jnp.arange(experts, dtype=jnp.int32)
-    hits_t = jnp.any(routes.T[:, None, :] == ids[None, :, None], axis=0) & live[None, :]
-    order = jnp.arange(rows, dtype=jnp.int32)
-    before = (order[:, None] < order[None, :]).astype(bf16)
-    hits_blocks = hits_t.reshape(experts, nt, rows)
-    earlier = jnp.einsum("ebr,rs->ebs", hits_blocks.astype(bf16), before, preferred_element_type=f32)
-    ranks = jnp.where(hits_blocks, earlier, -1.0).astype(bf16)
-    ranks = jnp.transpose(ranks.reshape(8, local, nt, rows), (2, 0, 1, 3))
-    ranks = jnp.pad(ranks, ((0, 0), (0, 0), (0, 8 - local), (0, 0)), constant_values=-1.0)
-    ranks = ranks.reshape(nt, 64, rows)
-    ranks = jnp.stack([ranks, hop_x(ranks)])
+    live = positions < jnp.repeat(lengths, seq_len)
     own_start = t_id * rows
     live_own = lax.dynamic_slice_in_dim(live, own_start, rows, 0).astype(f32)[:, None]
     routes_own = lax.dynamic_slice_in_dim(routes, own_start, rows, 0)
@@ -453,21 +682,6 @@
     router = jnp.pad(w_router, ((0, 0), (0, LANES - experts)))
     router_t = jnp.pad(w_router.T.reshape(8, local, width), ((0, 0), (0, 8 - local), (0, 0))).reshape(64, width)
 
-    def for_plane(w):
-        return jnp.transpose(w.reshape(deep, 8, local, hidden // nt), (1, 2, 0, 3))
-
-    w_send = jnp.stack([for_plane(w_gate), for_plane(w_up), for_plane(w_down)], axis=2)
-    groups = 2
-    per = local // groups
-    w_groups = []
-    for i in range(groups):
-        piece = lax.all_to_all(
-            w_send[:, i * per:(i + 1) * per], BOTH, 0, 0, tiled=True, axis_index_groups=plane_groups
-        )
-        piece = piece.reshape(2, nt, per, 3, deep, hidden // nt)
-        piece = jnp.transpose(piece, (2, 3, 0, 4, 1, 5)).reshape(per, 3, 2 * deep, hidden)
-        w_groups.append(lax.all_gather(piece, "dp", axis_index_groups=z_groups))
-
     half_head = HD // 2
     exponent = 2.0 * jnp.arange(half_head, dtype=f32) / HD
     angles = jnp.arange(seq_len, dtype=f32)[:, None] * jnp.exp(-math.log(rope_base) * exponent)[None, :]
@@ -476,11 +690,13 @@
     sin_table = jnp.concatenate([-sine, sine] * 2, axis=1)
 
     place = jnp.stack(
-        [core, plane_id, plane_id * local, t_id]
+        [core, plane_id, plane_id * local, t_id, dp_id // 2]
     ).astype(jnp.int32)
     length = lax.dynamic_slice_in_dim(lengths, own_start // seq_len, 1, 0)[0]
     where_attn = jnp.stack([core, length]).astype(jnp.int32)
 
+    out_late = after(out_grad, w_attn)
+    out_y, out_x = hop_y(out_late), hop_x(out_late)
     q_width, k_width = 2 * q_cols, 2 * kv_cols
     heads = q_width // HD
     q, k, v, ctx, lse, keep, send = call(
@@ -491,16 +707,15 @@
             sds((rows, width), bf16), sds((rows, width), bf16),
         ],
         12 * 10**9, 16 * 2**20,
-        in_specs=[SM] + [VM] * 6, out_specs=[VM] * 7,
-        scratch_shapes=[pltpu.VMEM((seq_len, width), bf16)],
-    )(where_attn, normed_attn, normed_peer, w_qkv, wo, cos_table, sin_table)
+        in_specs=[SM] + [VM] * 4, out_specs=[VM] * 7,
+    )(where_attn, after(normed_rows, w_groups[0][0]), w_attn, cos_table, sin_table)
     got = hop_c(send)
     hidden_own, normed_mix, inverse_mix = call(
         mix_norm_kernel,
         [sds((rows, width), f32), sds((rows, width), bf16), sds((rows, 1), f32)],
         10**7, 8 * 2**20,
         in_specs=[VM] * 5, out_specs=[VM] * 3,
-    )(tokens, keep, got, live_own, gain_mixer[None, :])
+    )(tokens, after(keep, out_y, out_x), got, live_own, gain_mixer[None, :])
 
     slots_shape = (local, 8, cap, width)
 
@@ -533,37 +748,42 @@
             ),
         )(place, *blocks, ranks, *extra)
 
-    (grads_in,) = dispatch(gather_plane(out_grad), False)
+    (grads_in,) = dispatch(gather_plane(out_late, out_y, out_x), False)
     rows_in, gates_in = dispatch(gather_plane(normed_mix), True)
 
     ys, dxs, dws = [], [], []
-    for i in range(groups):
-        def slot_spec(last):
-            return pl.BlockSpec((1, 8, cap, last), lambda e, where, i=i: (i * per + e, 0, 0, 0))
+    first = 0
+    for per, sources in zip(group_sizes, w_groups):
+        def slot_spec(last, first=first, per=per):
+            return pl.BlockSpec((1, 8, cap, last), lambda e, where: (first + e, 0, 0, 0))
+
         def out_spec(last):
             return pl.BlockSpec((1, 8, cap, last), lambda e, where: (e, 0, 0, 0))
+
         y, dx, dw = call(
-            functools.partial(expert_kernel, i * per),
+            functools.partial(expert_kernel, first, len(sources)),
             [
                 sds((per, 8, cap, width), bf16), sds((per, 8, cap, width + LANES), bf16),
-                sds((planes, 8, per, 3, deep, hidden // nt), bf16),
+                sds((planes, 8, per, 3, deep, quarter), bf16),
             ],
             per * 18 * 8 * cap * width * hidden, per * 20 * 2**20,
             grid_spec=pltpu.PrefetchScalarGridSpec(
                 num_scalar_prefetch=1, grid=(per,),
-                in_specs=[
-                    slot_spec(width), slot_spec(width), slot_spec(1),
-                    pl.BlockSpec((planes, 1, 3, 2 * deep, hidden), lambda e, where: (0, e, 0, 0, 0)),
-                ],
+                in_specs=[slot_spec(width), slot_spec(width), slot_spec(1)]
+                + [pl.BlockSpec(memory_space=pl.ANY)] * len(sources),
                 out_specs=[
                     out_spec(width), out_spec(width + LANES),
-                    pl.BlockSpec((planes, 8, 1, 3, deep, hidden // nt), lambda e, where: (0, 0, e, 0, 0, 0)),
+                    pl.BlockSpec((planes, 8, 1, 3, deep, quarter), lambda e, where: (0, 0, e, 0, 0, 0)),
+                ],
+                scratch_shapes=[
+                    pltpu.VMEM((2, planes, 8, 3, deep, quarter), bf16), pltpu.SemaphoreType.DMA((2, len(sources))),
                 ],
             ),
-        )(place, rows_in, grads_in, gates_in, w_groups[i])
+        )(after(place, *dws[-1:], ), rows_in, grads_in, gates_in, *sources)
         ys.append(y)
         dxs.append(dx)
         dws.append(dw)
+        first += per
 
     def combine(values, start):
         last = values[0].shape[-1]
@@ -573,13 +793,17 @@
             grid_spec=pltpu.PrefetchScalarGridSpec(
                 num_scalar_prefetch=1, grid=(4,),
                 in_specs=[
-                    pl.BlockSpec((per, 1, cap, last), lambda i, where: (0, 2 * i + start, 0, 0)) for _ in values
+                    pl.BlockSpec((v.shape[0], 1, cap, last), lambda i, where: (0, 2 * i + start, 0, 0)) for v in values
                 ] + [ranks_spec(2, start)],
                 out_specs=pl.BlockSpec((1, rows, last), lambda i, where: (i, 0, 0)),
             ),
         )(place, *values, ranks)
 
-    grad_terms = scatter_plane(combine(dxs, 1), combine(dxs, 0))
+    dx_send = combine(dxs, 1)
+    dx_keep = combine(dxs, 0)
+    grad_terms = scatter_plane(dx_send, dx_keep)
+    y_send = combine([after(v, dx_keep) for v in ys], 1)
+    y_keep = combine([after(v, dx_keep) for v in ys], 0)
     grad_hidden, grad_branch, router_grad, gain_mix_grad = call(
         mix_back_kernel,
         [
@@ -588,29 +812,28 @@
         10**8, 12 * 2**20,
         in_specs=[VM] * 11, out_specs=[VM] * 4,
     )(
-        normed_mix, hidden_own, inverse_mix, *grad_terms, out_grad, router, hits_own, live_own,
+        after(normed_mix, y_send, y_keep), hidden_own, inverse_mix, *grad_terms, out_grad, router, hits_own, live_own,
         gain_mixer[None, :],
     )
     branch_peer = hop_c(grad_branch)
 
-    out_terms = scatter_plane(combine(ys, 1), combine(ys, 0))
+    out_terms = scatter_plane(after(y_send, grad_branch), y_keep)
     mixed = (hidden_own + sum(term.astype(f32) for term in out_terms)).astype(bf16)
 
-    dw_qkv, dwo, keep_back, send_back = call(
+    dw_attn, keep_back, send_back = call(
         attend_back_kernel,
         [
-            sds((width, q_width + 2 * k_width), bf16), sds((width, q_width), bf16),
-            sds((rows, width), bf16), sds((rows, width), bf16),
+            sds((2, nd, deep, cut + q_cols), bf16), sds((rows, width), bf16), sds((rows, width), bf16),
         ],
         25 * 10**9, 24 * 2**20,
-        in_specs=[SM] + [VM] * 13, out_specs=[VM] * 4,
+        in_specs=[SM] + [VM] * 11, out_specs=[VM] * 3,
         scratch_shapes=[
-            pltpu.VMEM((seq_len, width), bf16), pltpu.VMEM((seq_len, width), bf16),
-            pltpu.VMEM((seq_len, q_width), bf16), pltpu.VMEM((seq_len, q_width + 2 * k_width), bf16),
+            pltpu.VMEM((seq_len, width), bf16),
+            pltpu.VMEM((seq_len, q_width), bf16), pltpu.VMEM((seq_len, 2 * cut), bf16),
             pltpu.VMEM((seq_len, LANES), f32), pltpu.VMEM((seq_len, LANES), f32),
         ],
     )(
-        where_attn, normed_attn, normed_peer, grad_branch, branch_peer, w_qkv, wo, cos_table, sin_table,
+        where_attn, normed_rows, grad_branch, branch_peer, w_attn, cos_table, sin_table,
         q, k, v, ctx, lse,
     )
     got_back = hop_c(send_back)
@@ -633,31 +856,28 @@
         whole_grad = jnp.concatenate(parts, axis=1).reshape(experts, deep, hidden // nt)
         return jnp.transpose(whole_grad, (1, 0, 2))
 
-    def halves(grad, start, cols):
-        return grad[:, start:start + cols], grad[:, start + cols:start + 2 * cols]
-
-    pieces = [
-        halves(dw_qkv, 0, q_cols), halves(dw_qkv, q_width, kv_cols),
-        halves(dw_qkv, q_width + k_width, kv_cols), halves(dwo, 0, q_cols),
-    ]
-    mine = jnp.concatenate([a for a, _ in pieces], axis=1)
-    other = jnp.concatenate([b for _, b in pieces], axis=1)
-    attn_grad = add16(mine, hop_y(other))
-    attn_grad = lax.psum_scatter(attn_grad, "dp", scatter_dimension=0, tiled=True).astype(f32)
-    grad_query = attn_grad[:, cuts[0]:cuts[1]]
-    grad_keyval = jnp.stack([attn_grad[:, cuts[1]:cuts[2]], attn_grad[:, cuts[2]:cuts[3]]], axis=1)
-    grad_out = attn_grad[:, cuts[3]:cuts[4]]
-
-    small = lax.psum(jnp.concatenate([router_grad, gain_mix_grad, gain_attn_grad], axis=0), BOTH)
+    attn_grad = add16(dw_attn[0], hop_y(dw_attn[1])).reshape(planes, 2, deep, cut + q_cols)
+    x_id = dp_id % 2
+    attn_grad = add16(
+        lax.dynamic_index_in_dim(attn_grad, x_id, 1, False),
+        hop_x(lax.dynamic_index_in_dim(attn_grad, 1 - x_id, 1, False)),
+    )
+    attn_grad = sum_z(attn_grad, planes, dp_id // 2, z_groups)
+    grad_query = attn_grad[:, :q_cols]
+    grad_keyval = attn_grad[:, q_cols:cut].reshape(deep, 2, kv_cols)
+    grad_out = attn_grad[:, cut:]
+
+    router_all = sum_all(jnp.concatenate([router_grad, gain_mix_grad], axis=0), nd)
+    gain_attn_all = sum_all(gain_attn_grad, nd)
     return (
         mixed,
         grad_tokens,
-        small[experts + 1],
+        gain_attn_all[0],
         grad_query,
         grad_keyval,
         grad_out,
-        small[experts],
-        small[:experts].T,
+        router_all[experts],
+        router_all[:experts].T,
         to_owner(0),
         to_owner(1),
         to_owner(2),

time: 781 us -> 683 us (0.87)
  waiting for transfers between devices: 360 us -> 242 us
  Pallas kernels: 191 us -> 288 us
  blocking collectives: 64.2 us -> 0 us
  local copies, waits for them, and re-layouts: 62 us -> 40.2 us
  starting transfers between devices: 38.7 us -> 56.4 us
    pallas_call x3 -> x7, Pallas kernels: 90.7 us -> 189 us  [the longest x4 76.2 us: shards(): call(functools.partial(expert_kernel, first, len(sources)), [sds((per, 8,...]
    psum x1 -> x0, waiting for transfers between devices: 81 us -> none  [shards(): lax.psum(jnp.concatenate([router_grad, gain_mix_grad, gain_attn_grad], ax...]
    reduce_scatter x1 -> x0, waiting for transfers between devices: 67.9 us -> none  [shards(): lax.psum_scatter(attn_grad, 'dp', scatter_dimension=0, tiled=True)]
    all_to_all x2 -> x0, blocking collectives: 64.2 us -> none  [shards(): lax.all_to_all(w_send[:, i * per:(i + 1) * per], BOTH, 0, 0, tiled=True,...]
    reduce_scatter x2 -> x4, waiting for transfers between devices: 0.01 us -> 26.9 us  [shards(): lax.psum_scatter(dw, 'dp', scatter_dimension=0, axis_index_groups=z_groups)]
    all_gather x3 -> x4, waiting for transfers between devices: 71.6 us -> 51.9 us  [gather_z(): return (lax.all_gather(x, 'dp', axis_index_groups=z_groups),)]
    ppermute x39 -> x50, waiting for transfers between devices: 140 us -> 156 us  [hop(): return lax.ppermute(x, BOTH, pairs)]
    transpose x6 -> x1, local copies, waits for them, and re-layouts: 11.6 us -> 0.66 us  [shards(): router_all[:experts]]
  transfers between devices with their start and end apart: 48 -> 62, of which waited for: 18 -> 28; matrix products, arithmetic and copies ran while one was open for 11% -> 9% of each run, Pallas kernels for 25% -> 39%
where the time goes in v2:
time: 683 us; the launch traced here: 678 us
  Pallas kernels  288 us (42%)
  waiting for transfers between devices  242 us (35%)
  starting transfers between devices  56.4 us (8%)
  local copies, waits for them, and re-layouts  40.2 us (6%)
  other arithmetic  36.3 us (5%)
  between operations  15 us (2%)
    ppermute x50, waiting for transfers between devices, hop(): return lax.ppermute(x, BOTH, pairs)  156 us
    pallas_call x4, Pallas kernels, shards(): call(functools.partial(expert_kernel, first, len(sources)), [sds((per, 8,...  76.2 us
    pallas_call x1, Pallas kernels, shards(): pl.pallas_call(functools.partial(gather_kernel, later), out_shape=[sds((2...  58.1 us
    all_gather x4, waiting for transfers between devices, gather_z(): return (lax.all_gather(x, 'dp', axis_index_groups=z_groups),)  51.9 us
    ppermute x50, starting transfers between devices, hop(): return lax.ppermute(x, BOTH, pairs)  40.1 us
    pallas_call x4, Pallas kernels, combine(): call(functools.partial(combine_kernel, local, cap, groups), sds((4, rows,...  32.9 us
    pallas_call x1, Pallas kernels, shards(): call(attend_back_kernel, [sds((2, nd, deep, cut + q_cols), bf16), sds((ro...  31.4 us
    pallas_call x2, Pallas kernels, dispatch(): call(functools.partial(dispatch_gates_kernel if gated else dispatch_kerne...  29.1 us
  transfers between devices with their start and end apart: 62, of which 28 were waited for; matrix products, arithmetic and copies ran while one was open for 9% of the time, Pallas kernels for 39%

profile of v2, /device:TPU:0, one launch (start us, length us, event | category | flops | bytes accessed | tf_op | source)
XLA Modules:
  0.0 677.6 jit_solution(11691846915192624587)
XLA Ops:
  11.9 22.8 %shard_map.212 = (bf16[8,3,128,128]{3,2,1,0:T(8,128)(2,1)}, bf16[8,3,128,128]{3,2,1,0:T(8,128)(2,1)}) custom-call(bf16[8,4,3,128,128]{4,3,2,1,0:T(8,128)(2,1)} %pad_maximum_fusion.w_send), custom_call_target="tpu_custom_call" | custom-call | flops 1000000 | bytes 20971520 | tf_op jit(solution)/shard_map/pallas_call | solution.py:641
  36.4 58.1 %shard_map.213 = (bf16[1024,1024]{1,0:T(8,128)(2,1)}, bf16[2,8,128,768]{3,2,1,0:T(8,128)(2,1)}, bf16[2,4,64,512]{3,2,1,0:T(8,128)(2,1)}, bf16[8,3,128,128]{3,2,1,0:T(8,128)(2,1)}, bf16[8,3,128,128]{3,2,1,0:T(8,128)(2,1)}) custom-call(s32[2]{0:T(128)} %lengths.1, bf16[512,1024]{1,0:T(8,128)(2,1)} %tokens.5, f32[1,1024]{1,0:T(1,128)} %bitcast.198, ...), custom_call_target="tpu_custom_call" | custom-call | flops 10000000 | bytes 104857600 | tf_op jit(solution)/shard_map/pallas_call | solution.py:652
  94.5 16.4 %all-gather.9.cloned.1.call-done = bf16[32,3,128,128]{3,2,1,0:T(8,128)(2,1)} async-done(((bf16[8,3,128,128]{3,2,1,0:T(8,128)(2,1)}), bf16[32,3,128,128]{3,2,1,0:T(8,128)(2,1)}) %all-gather.9.cloned.1.call-update) | async-done | bytes 3145744 | tf_op jit(solution)/shard_map/all_gather | solution.py:96
  119.2 20.2 %shard_map.214 = (bf16[1024,512]{1,0:T(8,128)(2,1)}, bf16[1024,256]{1,0:T(8,128)(2,1)}, bf16[1024,256]{1,0:T(8,128)(2,1)}, bf16[1024,512]{1,0:T(8,128)(2,1)}, f3...) custom-call(s32[2]{0:T(128)} %pad_add_fusion.where_ref, ...), custom_call_target="tpu_custom_call" | custom-call | flops 12000000000 | bytes 16777216 | tf_op jit(solution)/shard_map/pallas_call | solution.py:702
  139.4 35.5 %all-gather.11.cloned.1.call-done = bf16[32,3,128,128]{3,2,1,0:T(8,128)(2,1)} async-done(((bf16[8,3,128,128]{3,2,1,0:T(8,128)(2,1)}), bf16[32,3,128,128]{3,2,1,0:T(8,128)(2,1)}) %all-gather.11.cloned.1.call-update) | async-done | bytes 3145744 | tf_op jit(solution)/shard_map/all_gather | solution.py:96
  177.3 4.3 shard_map.215
  188.0 11.1 %collective-permute-done.13.refs_4_ = bf16[256,1024]{1,0:T(8,128)(2,1)S(1)} collective-permute-done((bf16[256,1024]{1,0:T(8,128)(2,1)S(1)}, bf16[256,1024]{1,0:T(8,128)(2,1)S(1)}, u32[]{:S(2)}, u32[]{:S(2)}) %collective-permute-start.13) | collective-permute-done | bytes 524320 | tf_op jit(solution)/shard_map/ppermute | solution.py:49
  199.1 18.8 %collective-permute-done.12.refs_3_ = bf16[256,1024]{1,0:T(8,128)(2,1)S(1)} collective-permute-done((bf16[256,1024]{1,0:T(8,128)(2,1)S(1)}, bf16[256,1024]{1,0:T(8,128)(2,1)S(1)}, u32[]{:S(2)}, u32[]{:S(2)}) %collective-permute-start.12) | collective-permute-done | bytes 524320 | tf_op jit(solution)/shard_map/ppermute | solution.py:49
  226.2 10.6 %collective-permute-done.6.refs_4_ = bf16[256,1024]{1,0:T(8,128)(2,1)S(1)} collective-permute-done((bf16[256,1024]{1,0:T(8,128)(2,1)S(1)}, bf16[256,1024]{1,0:T(8,128)(2,1)S(1)}, u32[]{:S(2)}, u32[]{:S(2)}) %collective-permute-start.6) | collective-permute-done | bytes 524320 | tf_op jit(solution)/shard_map/ppermute | solution.py:49
  239.4 12.8 %shard_map.217.g_ref = bf16[4,8,144,1024]{3,2,1,0:T(8,128)(2,1)} custom-call(s32[5]{0:T(128)} %stack.44.where_ref, bf16[512,1024]{1,0:T(8,128)(2,1)} %out_grad.1, bf16[512,1024]{1,0:T(8,128)(2,1)} %collective-permute-done.refs_1_, bf16[512,1024]{1,0:T(8,128)(2,1)} %copy-done.21, bf16[256,1024]{1,0:T(8,128)(2,1)} %copy-done.32, bf16[256,1024]{1,0:T(8,128)(2,1)} %copy-done.31, ...), custom_call_target="tpu_custom_call" | custom-call | flops 5000000000 | bytes 20971520 | tf_op jit(solution)/shard_map/pallas_call | solution.py:741
  253.8 16.3 %shard_map.216 = (bf16[4,8,144,1024]{3,2,1,0:T(8,128)(2,1)}, f32[4,8,144,1]{3,2,1,0:T(8,128)}) custom-call(s32[5]{0:T(128)} %stack.44.where_ref, bf16[512,1024]{1,0:T(8,128)(2,1)} %get-tuple-element.103.refs_0_.normed, bf16[512,1024]{1,0:T(8,128)(2,1)} %collective-permute-done.3.refs_1_, bf16[512,1024]{1,0:T(8,128)(2,1)} %collective-permute-done.4.refs_2_, ...), custom_call_target="tpu_custom_call" | custom-call | flops 5000000000 | bytes 20971520 | tf_op jit(solution)/shard_map/pallas_call | solution.py:741
  270.1 19.1 %shard_map.218 = (bf16[1,8,144,1024]{3,2,1,0:T(8,128)(2,1)}, bf16[1,8,144,1152]{3,2,1,0:T(8,128)(2,1)}, bf16[4,8,1,3,128,128]{5,4,3,2,1,0:T(8,128)(2,1)}) custom-call(s32[5]{0:T(128)} %stack.44.where_ref, bf16[4,8,144,1024]{3,2,1,0:T(8,128)(2,1)} %get-tuple-element.79.x_ref, bf16[4,8,144,1024]{3,2,1,0:T(8,128)(2,1)} %shard_map.217.g_ref, ...), custom_call_target="tpu_custom_call" | custom-call | flops 10871635968 | bytes 20971520 | tf_op jit(solution)/shard_map/pallas_call | solution.py:763
  289.7 19.0 %shard_map.219 = (bf16[1,8,144,1024]{3,2,1,0:T(8,128)(2,1)}, bf16[1,8,144,1152]{3,2,1,0:T(8,128)(2,1)}, bf16[4,8,1,3,128,128]{5,4,3,2,1,0:T(8,128)(2,1)}) custom-call(s32[5]{0:T(128)} %stack.44.where_ref, bf16[4,8,144,1024]{3,2,1,0:T(8,128)(2,1)} %get-tuple-element.79.x_ref, bf16[4,8,144,1024]{3,2,1,0:T(8,128)(2,1)} %shard_map.217.g_ref, ...), custom_call_target="tpu_custom_call" | custom-call | flops 10871635968 | bytes 20971520 | tf_op jit(solution)/shard_map/pallas_call | solution.py:763
  308.9 19.1 %shard_map.220 = (bf16[1,8,144,1024]{3,2,1,0:T(8,128)(2,1)}, bf16[1,8,144,1152]{3,2,1,0:T(8,128)(2,1)}, bf16[4,8,1,3,128,128]{5,4,3,2,1,0:T(8,128)(2,1)}) custom-call(s32[5]{0:T(128)} %stack.44.where_ref, bf16[4,8,144,1024]{3,2,1,0:T(8,128)(2,1)} %get-tuple-element.79.x_ref, bf16[4,8,144,1024]{3,2,1,0:T(8,128)(2,1)} %shard_map.217.g_ref, ...), custom_call_target="tpu_custom_call" | custom-call | flops 10871635968 | bytes 20971520 | tf_op jit(solution)/shard_map/pallas_call | solution.py:763
  328.4 19.1 %shard_map.221 = (bf16[1,8,144,1024]{3,2,1,0:T(8,128)(2,1)}, bf16[1,8,144,1152]{3,2,1,0:T(8,128)(2,1)}, bf16[4,8,1,3,128,128]{5,4,3,2,1,0:T(8,128)(2,1)}) custom-call(s32[5]{0:T(128)} %stack.44.where_ref, bf16[4,8,144,1024]{3,2,1,0:T(8,128)(2,1)} %get-tuple-element.79.x_ref, bf16[4,8,144,1024]{3,2,1,0:T(8,128)(2,1)} %shard_map.217.g_ref, ...), custom_call_target="tpu_custom_call" | custom-call | flops 10871635968 | bytes 20971520 | tf_op jit(solution)/shard_map/pallas_call | solution.py:763
  347.5 8.9 %shard_map.225 = bf16[4,512,1152]{2,1,0:T(8,128)(2,1)} custom-call(s32[5]{0:T(128)} %stack.44.where_ref, bf16[1,8,144,1152]{3,2,1,0:T(8,128)(2,1)} %get-tuple-element.82.refs_0_, bf16[1,8,144,1152]{3,2,1,0:T(8,128)(2,1)} %get-tuple-element.85.refs_1_, bf16[1,8,144,1152]{3,2,1,0:T(8,128)(2,1)} %get-tuple-element.90.refs_2_, ...), custom_call_target="tpu_custom_call" | custom-call | flops 2500000000 | bytes 12582912 | tf_op jit(solution)/shard_map/pallas_call | solution.py:790
  358.8 8.5 %shard_map.222 = bf16[4,512,1152]{2,1,0:T(8,128)(2,1)} custom-call(s32[5]{0:T(128)} %stack.44.where_ref, bf16[1,8,144,1152]{3,2,1,0:T(8,128)(2,1)} %get-tuple-element.82.refs_0_, bf16[1,8,144,1152]{3,2,1,0:T(8,128)(2,1)} %get-tuple-element.85.refs_1_, bf16[1,8,144,1152]{3,2,1,0:T(8,128)(2,1)} %get-tuple-element.90.refs_2_, ...), custom_call_target="tpu_custom_call" | custom-call | flops 2500000000 | bytes 12582912 | tf_op jit(solution)/shard_map/pallas_call | solution.py:790
  367.3 4.9 add_convert_fusion
  376.1 2.9 fusion.4
  379.8 7.8 %shard_map.224 = bf16[4,512,1024]{2,1,0:T(8,128)(2,1)} custom-call(s32[5]{0:T(128)} %stack.44.where_ref, bf16[1,8,144,1024]{3,2,1,0:T(8,128)(2,1)} %get-tuple-element.96.refs_0_, bf16[1,8,144,1024]{3,2,1,0:T(8,128)(2,1)} %get-tuple-element.98.refs_1_, bf16[1,8,144,1024]{3,2,1,0:T(8,128)(2,1)} %get-tuple-element.100.refs_2_, ...), custom_call_target="tpu_custom_call" | custom-call | flops 2500000000 | bytes 12582912 | tf_op jit(solution)/shard_map/pallas_call | solution.py:790
  393.5 7.8 %shard_map.223 = bf16[4,512,1024]{2,1,0:T(8,128)(2,1)} custom-call(s32[5]{0:T(128)} %stack.44.where_ref, bf16[1,8,144,1024]{3,2,1,0:T(8,128)(2,1)} %get-tuple-element.96.refs_0_, bf16[1,8,144,1024]{3,2,1,0:T(8,128)(2,1)} %get-tuple-element.98.refs_1_, bf16[1,8,144,1024]{3,2,1,0:T(8,128)(2,1)} %get-tuple-element.100.refs_2_, ...), custom_call_target="tpu_custom_call" | custom-call | flops 2500000000 | bytes 12582912 | tf_op jit(solution)/shard_map/pallas_call | solution.py:790
  401.2 3.5 all-to-all-start
  409.3 11.5 %collective-permute-done.24 = bf16[256,1152]{1,0:T(8,128)(2,1)} collective-permute-done((bf16[256,1152]{1,0:T(8,128)(2,1)S(1)}, bf16[256,1152]{1,0:T(8,128)(2,1)}, u32[]{:S(2)}, u32[]{:S(2)}) %collective-permute-start.24) | collective-permute-done | bytes 589856 | tf_op jit(solution)/shard_map/ppermute | solution.py:49
  423.2 6.3 collective-permute-done.20
  429.5 12.2 %collective-permute-done.22 = bf16[256,1152]{1,0:T(8,128)(2,1)S(1)} collective-permute-done((bf16[256,1152]{1,0:T(8,128)(2,1)S(1)}, bf16[256,1152]{1,0:T(8,128)(2,1)S(1)}, u32[]{:S(2)}, u32[]{:S(2)}) %collective-permute-start.22) | collective-permute-done | bytes 589856 | tf_op jit(solution)/shard_map/ppermute | solution.py:49
  442.8 8.1 %shard_map.226 = (f32[512,1024]{1,0:T(8,128)}, bf16[512,1024]{1,0:T(8,128)(2,1)}, f32[32,1024]{1,0:T(8,128)}, f32[1,1024]{1,0:T(1,128)}) custom-call(bf16[512,1024]{1,0:T(8,128)(2,1)} %get-tuple-element.103.refs_0_.normed, f32[512,1024]{1,0:T(8,128)} %get-tuple-element.76.hidden_in, f32[512,1]{1,0:T(8,128)} %get-tuple-element.104.inv, ...), custom_call_target="tpu_custom_call" | custom-call | flops 100000000 | bytes 12582912 | tf_op jit(solution)/shard_map/pallas_call | solution.py:807
  450.9 3.6 all-to-all-start.1
  459.7 9.9 %collective-permute-done.46 = f32[33,1024]{1,0:T(8,128)S(1)} collective-permute-done((f32[33,1024]{1,0:T(8,128)S(1)}, f32[33,1024]{1,0:T(8,128)S(1)}, u32[]{:S(2)}, u32[]{:S(2)}) %collective-permute-start.46) | collective-permute-done | bytes 135200 | tf_op jit(solution)/shard_map/ppermute | solution.py:49
  471.1 4.4 collective-permute-done.47
  476.4 11.6 %collective-permute-done.48 = f32[33,1024]{1,0:T(8,128)S(1)} collective-permute-done((f32[33,1024]{1,0:T(8,128)S(1)}, f32[33,1024]{1,0:T(8,128)S(1)}, u32[]{:S(2)}, u32[]{:S(2)}) %collective-permute-start.48) | collective-permute-done | bytes 135200 | tf_op jit(solution)/shard_map/ppermute | solution.py:49
  489.4 2.5 reduce-scatter.9.cloned.1.call-done
  491.9 3.8 all-to-all-start.2
  495.7 2.8 collective-permute-done.49
  500.2 31.4 %shard_map.227 = (bf16[2,8,128,768]{3,2,1,0:T(8,128)(2,1)}, bf16[512,1024]{1,0:T(8,128)(2,1)}, bf16[512,1024]{1,0:T(8,128)(2,1)}) custom-call(s32[2]{0:T(128)} %pad_add_fusion.where_ref, bf16[1024,1024]{1,0:T(8,128)(2,1)} %get-tuple-element.70.rows, bf16[512,1024]{1,0:T(8,128)(2,1)} %get-tuple-element.105.gb_own, bf16[512,1024]{1,0:T(8,128)(2,1)} %copy-done.27, ...), custom_call_target="tpu_custom_call" | custom-call | flops 24999999488 | bytes 25165824 | tf_op jit(solution)/shard_map/pallas_call | solution.py:823
  531.6 24.4 %reduce-scatter.11.cloned.1.call-done = bf16[1,8,1,3,128,128]{5,4,3,2,1,0:T(8,128)(2,1)} async-done(((bf16[4,8,1,3,128,128]{5,4,3,2,1,0:T(8,128)(2,1)}), bf16[1,8,1,3,128,128]{5,4,3,2,1,0:T(8,128)(2,1)}) %reduce-scatter.11.cloned.1.call-update) | async-done | bytes 786448 | tf_op jit(solution)/shard_map/reduce_scatter | solution.py:849
  556.0 3.8 all-to-all-start.3
  565.1 6.8 all-to-all-done.3
  573.9 4.5 shard_map.228
  581.1 24.1 %collective-permute-done.36 = f32[1,1024]{1,0:T(1,128)S(1)} collective-permute-done((f32[1,1024]{1,0:T(1,128)S(1)}, f32[1,1024]{1,0:T(1,128)S(1)}, u32[]{:S(2)}, u32[]{:S(2)}) %collective-permute-start.36) | collective-permute-done | bytes 4128 | tf_op jit(solution)/shard_map/ppermute | solution.py:49
  613.5 4.3 add_convert_fusion.1
  622.1 10.4 %collective-permute-done.41 = bf16[4,128,768]{2,1,0:T(8,128)(2,1)S(1)} collective-permute-done((bf16[4,128,768]{2,1,0:T(8,128)(2,1)S(1)}, bf16[4,128,768]{2,1,0:T(8,128)(2,1)S(1)}, u32[]{:S(2)}, u32[]{:S(2)}) %collective-permute-start.41) | collective-permute-done | bytes 786464 | tf_op jit(solution)/shard_map/ppermute | solution.py:49
  633.8 2.4 collective-permute-start.44
  636.3 4.9 collective-permute-done.30
  648.7 2.5 copy.113
  651.2 2.5 copy.114
  653.8 2.5 copy.115
  660.0 5.1 collective-permute-done.31
  667.3 3.3 fusion.3
  (251 shorter events, 105.7 us)
Async XLA Ops:
  7.2 103.7 %all-gather.9.cloned.1.call-start = ((), (), s32[]{:S(2)}) async-start(), calls=%async_computation.12 | async-start | bytes 3932160 | tf_op jit(solution)/shard_map/all_gather | solution.py:96
  34.7 140.2 %all-gather.11.cloned.1.call-start = ((), (), s32[]{:S(2)}) async-start(), calls=%async_computation.13 | async-start | bytes 3932160 | tf_op jit(solution)/shard_map/all_gather | solution.py:96
  35.5 273.4 %all-gather.13.cloned.1.call-start = ((), (), s32[]{:S(2)}) async-start(), calls=%async_computation.14 | async-start | bytes 3932160 | tf_op jit(solution)/shard_map/all_gather | solution.py:96
  110.9 217.4 %all-gather.15.cloned.1.call-start = ((), (), s32[]{:S(2)}) async-start(), calls=%async_computation.15 | async-start | bytes 3932160 | tf_op jit(solution)/shard_map/all_gather | solution.py:96
  111.5 64.5 %collective-permute-start.1 = (bf16[512,1024]{1,0:T(8,128)(2,1)S(1)}, bf16[512,1024]{1,0:T(8,128)(2,1)S(1)}, u32[]{:S(2)}, u32[]{:S(2)}) collective-permute-start(bf16[512,1024]{1,0:T(8,128)(2,1)S(1)} %copy-done.15), channel_id=1, source_target_pairs={{0,4},{1,5},{2,6},{3,7},{4,0},{5,1},{6,2},{7,3},{8,12},{9,13},{10,... | collective-permute-start | bytes 3145736 | tf_op jit(solution)/shard_map/ppermute | solution.py:49
  113.0 63.0 %collective-permute-start = (bf16[512,1024]{1,0:T(8,128)(2,1)S(1)}, bf16[512,1024]{1,0:T(8,128)(2,1)}, u32[]{:S(2)}, u32[]{:S(2)}) collective-permute-start(bf16[512,1024]{1,0:T(8,128)(2,1)S(1)} %copy-done.15), channel_id=1, source_target_pairs={{0,2},{1,3},{2,0},{3,1},{4,6},{5,7},{6,4},{7,5},{8,10},{9,11},{10,... | collective-permute-start | bytes 3145736 | tf_op jit(solution)/shard_map/ppermute | solution.py:49
  139.4 36.6 %collective-permute-start.2 = (bf16[512,1024]{1,0:T(8,128)(2,1)}, bf16[512,1024]{1,0:T(8,128)(2,1)S(1)}, u32[]{:S(2)}, u32[]{:S(2)}) collective-permute-start(bf16[512,1024]{1,0:T(8,128)(2,1)} %get-tuple-element.75), channel_id=1, source_target_pairs={{0,1},{1,0},{2,3},{3,2},{4,5},{5,4},{6,7},{7,6},{8,9},{9,8},{10,11... | collective-permute-start | bytes 3145736 | tf_op jit(solution)/shard_map/ppermute | solution.py:49
  174.9 226.3 %reduce-scatter.5.cloned.1.call-start = ((), (), s32[]{:S(2)}) async-start(), calls=%async_computation.8 | async-start | bytes 3932160 | tf_op jit(solution)/shard_map/reduce_scatter | solution.py:849
  181.6 36.3 %collective-permute-start.4 = (bf16[512,1024]{1,0:T(8,128)(2,1)}, bf16[512,1024]{1,0:T(8,128)(2,1)}, u32[]{:S(2)}, u32[]{:S(2)}) collective-permute-start(bf16[512,1024]{1,0:T(8,128)(2,1)} %get-tuple-element.103.refs_0_.normed), channel_id=1, source_target_pairs={{0,4},{1,5},{2,6},{3,7},{4,0},{5,1},{6,2},{7,3},{8,12},{9,13},{10,... | collective-permute-start | bytes 3145736 | tf_op jit(solution)/shard_map/ppermute | solution.py:49
  184.1 14.9 %collective-permute-start.13 = (bf16[256,1024]{1,0:T(8,128)(2,1)S(1)}, bf16[256,1024]{1,0:T(8,128)(2,1)S(1)}, u32[]{:S(2)}, u32[]{:S(2)}) collective-permute-start(bf16[256,1024]{1,0:T(8,128)(2,1)S(1)} %slice.159), channel_id=1, source_target_pairs={{0,2},{1,3},{2,0},{3,1},{4,6},{5,7},{6,4},{7,5},{8,10},{9,11},{10,... | collective-permute-start | bytes 1572872 | tf_op jit(solution)/shard_map/ppermute | solution.py:49
  185.7 34.5 %collective-permute-start.3 = (bf16[512,1024]{1,0:T(8,128)(2,1)}, bf16[512,1024]{1,0:T(8,128)(2,1)}, u32[]{:S(2)}, u32[]{:S(2)}) collective-permute-start(bf16[512,1024]{1,0:T(8,128)(2,1)} %get-tuple-element.103.refs_0_.normed), channel_id=1, source_target_pairs={{0,2},{1,3},{2,0},{3,1},{4,6},{5,7},{6,4},{7,5},{8,10},{9,11},{10,... | collective-permute-start | bytes 3145736 | tf_op jit(solution)/shard_map/ppermute | solution.py:49
  187.3 30.6 %collective-permute-start.12 = (bf16[256,1024]{1,0:T(8,128)(2,1)S(1)}, bf16[256,1024]{1,0:T(8,128)(2,1)S(1)}, u32[]{:S(2)}, u32[]{:S(2)}) collective-permute-start(bf16[256,1024]{1,0:T(8,128)(2,1)S(1)} %slice.158), channel_id=1, source_target_pairs={{0,4},{1,5},{2,6},{3,7},{4,0},{5,1},{6,2},{7,3},{8,12},{9,13},{10,... | collective-permute-start | bytes 1572872 | tf_op jit(solution)/shard_map/ppermute | solution.py:49
  188.0 34.4 %collective-permute-start.14 = (bf16[512,1024]{1,0:T(8,128)(2,1)S(1)}, bf16[512,1024]{1,0:T(8,128)(2,1)S(1)}, u32[]{:S(2)}, u32[]{:S(2)}) collective-permute-start(bf16[512,1024]{1,0:T(8,128)(2,1)S(1)} %copy-done.15), channel_id=1, source_target_pairs={{0,1},{1,0},{2,3},{3,2},{4,5},{5,4},{6,7},{7,6},{8,9},{9,8},{10,11... | collective-permute-start | bytes 3145736 | tf_op jit(solution)/shard_map/ppermute | solution.py:49
  199.1 25.5 %collective-permute-start.16 = (bf16[512,1024]{1,0:T(8,128)(2,1)}, bf16[512,1024]{1,0:T(8,128)(2,1)S(1)}, u32[]{:S(2)}, u32[]{:S(2)}) collective-permute-start(bf16[512,1024]{1,0:T(8,128)(2,1)} %copy-done.21), channel_id=1, source_target_pairs={{0,1},{1,0},{2,3},{3,2},{4,5},{5,4},{6,7},{7,6},{8,9},{9,8},{10,11... | collective-permute-start | bytes 3145736 | tf_op jit(solution)/shard_map/ppermute | solution.py:49
  222.3 14.4 %collective-permute-start.6 = (bf16[256,1024]{1,0:T(8,128)(2,1)S(1)}, bf16[256,1024]{1,0:T(8,128)(2,1)S(1)}, u32[]{:S(2)}, u32[]{:S(2)}) collective-permute-start(bf16[256,1024]{1,0:T(8,128)(2,1)S(1)} %slice.157), channel_id=1, source_target_pairs={{0,2},{1,3},{2,0},{3,1},{4,6},{5,7},{6,4},{7,5},{8,10},{9,11},{10,... | collective-permute-start | bytes 1572872 | tf_op jit(solution)/shard_map/ppermute | solution.py:49
  223.9 14.2 %collective-permute-start.5 = (bf16[256,1024]{1,0:T(8,128)(2,1)S(1)}, bf16[256,1024]{1,0:T(8,128)(2,1)}, u32[]{:S(2)}, u32[]{:S(2)}) collective-permute-start(bf16[256,1024]{1,0:T(8,128)(2,1)S(1)} %slice.156), channel_id=1, source_target_pairs={{0,4},{1,5},{2,6},{3,7},{4,0},{5,1},{6,2},{7,3},{8,12},{9,13},{10,... | collective-permute-start | bytes 1572872 | tf_op jit(solution)/shard_map/ppermute | solution.py:49
  224.6 27.6 %collective-permute-start.7 = (bf16[512,1024]{1,0:T(8,128)(2,1)S(1)}, bf16[512,1024]{1,0:T(8,128)(2,1)}, u32[]{:S(2)}, u32[]{:S(2)}) collective-permute-start(bf16[512,1024]{1,0:T(8,128)(2,1)S(1)} %copy-done.16), channel_id=1, source_target_pairs={{0,1},{1,0},{2,3},{3,2},{4,5},{5,4},{6,7},{7,6},{8,9},{9,8},{10,11... | collective-permute-start | bytes 3145736 | tf_op jit(solution)/shard_map/ppermute | solution.py:49
  224.7 27.5 %collective-permute-start.9 = (bf16[512,1024]{1,0:T(8,128)(2,1)}, bf16[512,1024]{1,0:T(8,128)(2,1)}, u32[]{:S(2)}, u32[]{:S(2)}) collective-permute-start(bf16[512,1024]{1,0:T(8,128)(2,1)} %collective-permute-done.4.refs_2_), channel_id=1, source_target_pairs={{0,1},{1,0},{2,3},{3,2},{4,5},{5,4},{6,7},{7,6},{8,9},{9,8},{10,11... | collective-permute-start | bytes 3145736 | tf_op jit(solution)/shard_map/ppermute | solution.py:49
  225.2 27.0 %collective-permute-start.8 = (bf16[512,1024]{1,0:T(8,128)(2,1)}, bf16[512,1024]{1,0:T(8,128)(2,1)}, u32[]{:S(2)}, u32[]{:S(2)}) collective-permute-start(bf16[512,1024]{1,0:T(8,128)(2,1)} %collective-permute-done.3.refs_1_), channel_id=1, source_target_pairs={{0,1},{1,0},{2,3},{3,2},{4,5},{5,4},{6,7},{7,6},{8,9},{9,8},{10,11... | collective-permute-start | bytes 3145736 | tf_op jit(solution)/shard_map/ppermute | solution.py:49
  236.8 15.5 %collective-permute-start.11 = (bf16[256,1024]{1,0:T(8,128)(2,1)S(1)}, bf16[256,1024]{1,0:T(8,128)(2,1)S(1)}, u32[]{:S(2)}, u32[]{:S(2)}) collective-permute-start(bf16[256,1024]{1,0:T(8,128)(2,1)S(1)} %collective-permute-done.6.refs_4_), channel_id=1, source_target_pairs={{0,1},{1,0},{2,3},{3,2},{4,5},{5,4},{6,7},{7,6},{8,9},{9,8},{10,11... | collective-permute-start | bytes 1572872 | tf_op jit(solution)/shard_map/ppermute | solution.py:49
  238.1 14.2 %collective-permute-start.10 = (bf16[256,1024]{1,0:T(8,128)(2,1)}, bf16[256,1024]{1,0:T(8,128)(2,1)S(1)}, u32[]{:S(2)}, u32[]{:S(2)}) collective-permute-start(bf16[256,1024]{1,0:T(8,128)(2,1)} %collective-permute-done.5.refs_3_), channel_id=1, source_target_pairs={{0,1},{1,0},{2,3},{3,2},{4,5},{5,4},{6,7},{7,6},{8,9},{9,8},{10,11... | collective-permute-start | bytes 1572872 | tf_op jit(solution)/shard_map/ppermute | solution.py:49
  289.2 161.6 %reduce-scatter.7.cloned.1.call-start = ((), (), s32[]{:S(2)}) async-start(), calls=%async_computation.9 | async-start | bytes 3932160 | tf_op jit(solution)/shard_map/reduce_scatter | solution.py:849
  308.7 183.2 %reduce-scatter.9.cloned.1.call-start = ((), (), s32[]{:S(2)}) async-start(), calls=%async_computation.10 | async-start | bytes 3932160 | tf_op jit(solution)/shard_map/reduce_scatter | solution.py:849
  328.1 227.9 %reduce-scatter.11.cloned.1.call-start = ((), (), s32[]{:S(2)}) async-start(), calls=%async_computation.11 | async-start | bytes 3932160 | tf_op jit(solution)/shard_map/reduce_scatter | solution.py:849
  374.3 15.2 %collective-permute-start.23 = (bf16[256,1152]{1,0:T(8,128)(2,1)S(1)}, bf16[256,1152]{1,0:T(8,128)(2,1)S(1)}, u32[]{:S(2)}, u32[]{:S(2)}) collective-permute-start(bf16[256,1152]{1,0:T(8,128)(2,1)S(1)} %get-tuple-element.156), channel_id=1, source_target_pairs={{0,4},{1,5},{2,6},{3,7},{4,0},{5,1},{6,2},{7,3},{8,12},{9,13},{10,... | collective-permute-start | bytes 1769480 | tf_op jit(solution)/shard_map/ppermute | solution.py:49
  375.2 15.6 %collective-permute-start.21 = (bf16[256,1152]{1,0:T(8,128)(2,1)S(1)}, bf16[256,1152]{1,0:T(8,128)(2,1)}, u32[]{:S(2)}, u32[]{:S(2)}) collective-permute-start(bf16[256,1152]{1,0:T(8,128)(2,1)S(1)} %get-tuple-element.158), channel_id=1, source_target_pairs={{0,2},{1,3},{2,0},{3,1},{4,6},{5,7},{6,4},{7,5},{8,10},{9,11},{10,... | collective-permute-start | bytes 1769480 | tf_op jit(solution)/shard_map/ppermute | solution.py:49
  387.6 21.7 %collective-permute-start.25 = (bf16[256,1152]{1,0:T(8,128)(2,1)S(1)}, bf16[256,1152]{1,0:T(8,128)(2,1)}, u32[]{:S(2)}, u32[]{:S(2)}) collective-permute-start(bf16[256,1152]{1,0:T(8,128)(2,1)S(1)} %get-tuple-element.157), channel_id=1, source_target_pairs={{0,2},{1,3},{2,0},{3,1},{4,6},{5,7},{6,4},{7,5},{8,10},{9,11},{10,... | collective-permute-start | bytes 1769480 | tf_op jit(solution)/shard_map/ppermute | solution.py:49
  392.6 28.1 %collective-permute-start.24 = (bf16[256,1152]{1,0:T(8,128)(2,1)S(1)}, bf16[256,1152]{1,0:T(8,128)(2,1)}, u32[]{:S(2)}, u32[]{:S(2)}) collective-permute-start(bf16[256,1152]{1,0:T(8,128)(2,1)S(1)} %get-tuple-element.154), channel_id=1, source_target_pairs={{0,2},{1,3},{2,0},{3,1},{4,6},{5,7},{6,4},{7,5},{8,10},{9,11},{10,... | collective-permute-start | bytes 1769480 | tf_op jit(solution)/shard_map/ppermute | solution.py:49
  401.2 49.6 %all-to-all-start = ((bf16[8,1,3,128,128]{4,3,2,1,0:T(8,128)(2,1)}), bf16[8,1,3,128,128]{4,3,2,1,0:T(8,128)(2,1)S(1)}, u32[]{:S(2)}, u32[]{:S(2)}) async-start(bf16[8,1,3,128,128]{4,3,2,1,0:T(8,128)(2,1)} %bitcast.192), calls=%async_computation.1 | async-start | bytes 1572864 | tf_op jit(solution)/shard_map/all_to_all | solution.py:851
  404.8 24.7 %collective-permute-start.20 = (bf16[256,1152]{1,0:T(8,128)(2,1)S(1)}, bf16[256,1152]{1,0:T(8,128)(2,1)S(1)}, u32[]{:S(2)}, u32[]{:S(2)}) collective-permute-start(bf16[256,1152]{1,0:T(8,128)(2,1)S(1)} %get-tuple-element.159), channel_id=1, source_target_pairs={{0,4},{1,5},{2,6},{3,7},{4,0},{5,1},{6,2},{7,3},{8,12},{9,13},{10,... | collective-permute-start | bytes 1769480 | tf_op jit(solution)/shard_map/ppermute | solution.py:49
  406.7 34.9 %collective-permute-start.22 = (bf16[256,1152]{1,0:T(8,128)(2,1)S(1)}, bf16[256,1152]{1,0:T(8,128)(2,1)S(1)}, u32[]{:S(2)}, u32[]{:S(2)}) collective-permute-start(bf16[256,1152]{1,0:T(8,128)(2,1)S(1)} %get-tuple-element.155), channel_id=1, source_target_pairs={{0,4},{1,5},{2,6},{3,7},{4,0},{5,1},{6,2},{7,3},{8,12},{9,13},{10,... | collective-permute-start | bytes 1769480 | tf_op jit(solution)/shard_map/ppermute | solution.py:49
  450.8 48.3 %collective-permute-start.33 = (bf16[512,1024]{1,0:T(8,128)(2,1)}, bf16[512,1024]{1,0:T(8,128)(2,1)S(1)}, u32[]{:S(2)}, u32[]{:S(2)}) collective-permute-start(bf16[512,1024]{1,0:T(8,128)(2,1)} %get-tuple-element.105.gb_own), channel_id=1, source_target_pairs={{0,1},{1,0},{2,3},{3,2},{4,5},{5,4},{6,7},{7,6},{8,9},{9,8},{10,11... | collective-permute-start | bytes 3145736 | tf_op jit(solution)/shard_map/ppermute | solution.py:49
  450.9 37.6 %all-to-all-start.1 = ((bf16[8,1,3,128,128]{4,3,2,1,0:T(8,128)(2,1)}), bf16[8,1,3,128,128]{4,3,2,1,0:T(8,128)(2,1)S(1)}, u32[]{:S(2)}, u32[]{:S(2)}) async-start(bf16[8,1,3,128,128]{4,3,2,1,0:T(8,128)(2,1)} %bitcast.191), calls=%async_computation.3 | async-start | bytes 1572864 | tf_op jit(solution)/shard_map/all_to_all | solution.py:851
  489.4 124.1 %collective-permute-start.26 = (bf16[4,512,1024]{2,1,0:T(8,128)(2,1)}, bf16[4,512,1024]{2,1,0:T(8,128)(2,1)}, u32[]{:S(2)}, u32[]{:S(2)}) collective-permute-start(bf16[4,512,1024]{2,1,0:T(8,128)(2,1)} %shard_map.224), channel_id=1, source_target_pairs={{0,1},{1,0},{2,3},{3,2},{4,5},{5,4},{6,7},{7,6},{8,9},{9,8},{10,11... | collective-permute-start | bytes 12582920 | tf_op jit(solution)/shard_map/ppermute | solution.py:49
  491.9 64.2 %all-to-all-start.2 = ((bf16[8,1,3,128,128]{4,3,2,1,0:T(8,128)(2,1)}), bf16[8,1,3,128,128]{4,3,2,1,0:T(8,128)(2,1)S(1)}, u32[]{:S(2)}, u32[]{:S(2)}) async-start(bf16[8,1,3,128,128]{4,3,2,1,0:T(8,128)(2,1)} %bitcast.189), calls=%async_computation.5 | async-start | bytes 1572864 | tf_op jit(solution)/shard_map/all_to_all | solution.py:851
  531.6 42.3 %collective-permute-start.34 = (bf16[512,1024]{1,0:T(8,128)(2,1)}, bf16[512,1024]{1,0:T(8,128)(2,1)}, u32[]{:S(2)}, u32[]{:S(2)}) collective-permute-start(bf16[512,1024]{1,0:T(8,128)(2,1)} %get-tuple-element.113), channel_id=1, source_target_pairs={{0,1},{1,0},{2,3},{3,2},{4,5},{5,4},{6,7},{7,6},{8,9},{9,8},{10,11... | collective-permute-start | bytes 3145736 | tf_op jit(solution)/shard_map/ppermute | solution.py:49
  556.0 15.8 %all-to-all-start.3 = ((bf16[8,1,3,128,128]{4,3,2,1,0:T(8,128)(2,1)}), bf16[8,1,3,128,128]{4,3,2,1,0:T(8,128)(2,1)S(1)}, u32[]{:S(2)}, u32[]{:S(2)}) async-start(bf16[8,1,3,128,128]{4,3,2,1,0:T(8,128)(2,1)} %bitcast.190), calls=%async_computation.7 | async-start | bytes 1572864 | tf_op jit(solution)/shard_map/all_to_all | solution.py:851
  561.4 48.5 %collective-permute-start.40 = (bf16[8,128,768]{2,1,0:T(8,128)(2,1)S(1)}, bf16[8,128,768]{2,1,0:T(8,128)(2,1)}, u32[]{:S(2)}, u32[]{:S(2)}) collective-permute-start(bf16[8,128,768]{2,1,0:T(8,128)(2,1)S(1)} %slice_bitcast_fusion), channel_id=1, source_target_pairs={{0,2},{1,3},{2,0},{3,1},{4,6},{5,7},{6,4},{7,5},{8,10},{9,11},{10,... | collective-permute-start | bytes 4718600 | tf_op jit(solution)/shard_map/ppermute | solution.py:49
  579.9 25.3 %collective-permute-start.36 = (f32[1,1024]{1,0:T(1,128)S(1)}, f32[1,1024]{1,0:T(1,128)S(1)}, u32[]{:S(2)}, u32[]{:S(2)}) collective-permute-start(f32[1,1024]{1,0:T(1,128)S(1)} %add.146), channel_id=1, source_target_pairs={{0,2},{1,3},{2,0},{3,1},{4,6},{5,7},{6,4},{7,5},{8,10},{9,11},{10,... | collective-permute-start | bytes 12296 | tf_op jit(solution)/shard_map/ppermute | solution.py:49
  612.0 20.5 %collective-permute-start.41 = (bf16[4,128,768]{2,1,0:T(8,128)(2,1)S(1)}, bf16[4,128,768]{2,1,0:T(8,128)(2,1)S(1)}, u32[]{:S(2)}, u32[]{:S(2)}) collective-permute-start(bf16[4,128,768]{2,1,0:T(8,128)(2,1)S(1)} %dynamic-slice_bitcast_fusion), channel_id=1, source_target_pairs={{0,4},{1,5},{2,6},{3,7},{4,0},{5,1},{6,2},{7,3},{8,12},{9,13},{10,... | collective-permute-start | bytes 2359304 | tf_op jit(solution)/shard_map/ppermute | solution.py:49
  619.0 22.2 %collective-permute-start.30 = (bf16[256,1024]{1,0:T(8,128)(2,1)S(1)}, bf16[256,1024]{1,0:T(8,128)(2,1)S(1)}, u32[]{:S(2)}, u32[]{:S(2)}) collective-permute-start(bf16[256,1024]{1,0:T(8,128)(2,1)S(1)} %get-tuple-element.162), channel_id=1, source_target_pairs={{0,4},{1,5},{2,6},{3,7},{4,0},{5,1},{6,2},{7,3},{8,12},{9,13},{10,... | collective-permute-start | bytes 1572872 | tf_op jit(solution)/shard_map/ppermute | solution.py:49
  619.6 23.3 %collective-permute-start.28 = (bf16[256,1024]{1,0:T(8,128)(2,1)S(1)}, bf16[256,1024]{1,0:T(8,128)(2,1)S(1)}, u32[]{:S(2)}, u32[]{:S(2)}) collective-permute-start(bf16[256,1024]{1,0:T(8,128)(2,1)S(1)} %get-tuple-element.164), channel_id=1, source_target_pairs={{0,2},{1,3},{2,0},{3,1},{4,6},{5,7},{6,4},{7,5},{8,10},{9,11},{10,... | collective-permute-start | bytes 1572872 | tf_op jit(solution)/shard_map/ppermute | solution.py:49
  620.1 24.9 %collective-permute-start.39 = (f32[1,1024]{1,0:T(1,128)S(1)}, f32[1,1024]{1,0:T(1,128)S(1)}, u32[]{:S(2)}, u32[]{:S(2)}) collective-permute-start(f32[1,1024]{1,0:T(1,128)S(1)} %add.149), channel_id=1, source_target_pairs={{0,16},{1,17},{2,18},{3,19},{4,20},{5,21},{6,22},{7,23},{8,24},{9,... | collective-permute-start | bytes 12296 | tf_op jit(solution)/shard_map/ppermute | solution.py:49
  641.2 15.7 %collective-permute-start.43 = (bf16[128,768]{1,0:T(8,128)(2,1)S(1)}, bf16[128,768]{1,0:T(8,128)(2,1)S(1)}, u32[]{:S(2)}, u32[]{:S(2)}) collective-permute-start(bf16[128,768]{1,0:T(8,128)(2,1)S(1)} %get-tuple-element.180), channel_id=1, source_target_pairs={{0,16},{1,17},{2,18},{3,19},{4,20},{5,21},{6,22},{7,23},{8,24},{9,... | collective-permute-start | bytes 589832 | tf_op jit(solution)/shard_map/ppermute | solution.py:49
  642.8 15.6 %collective-permute-start.32 = (bf16[256,1024]{1,0:T(8,128)(2,1)}, bf16[256,1024]{1,0:T(8,128)(2,1)S(1)}, u32[]{:S(2)}, u32[]{:S(2)}) collective-permute-start(bf16[256,1024]{1,0:T(8,128)(2,1)} %get-tuple-element.163), channel_id=1, source_target_pairs={{0,2},{1,3},{2,0},{3,1},{4,6},{5,7},{6,4},{7,5},{8,10},{9,11},{10,... | collective-permute-start | bytes 1572872 | tf_op jit(solution)/shard_map/ppermute | solution.py:49
  645.0 15.1 %collective-permute-start.27 = (bf16[256,1024]{1,0:T(8,128)(2,1)}, bf16[256,1024]{1,0:T(8,128)(2,1)S(1)}, u32[]{:S(2)}, u32[]{:S(2)}) collective-permute-start(bf16[256,1024]{1,0:T(8,128)(2,1)} %get-tuple-element.165), channel_id=1, source_target_pairs={{0,4},{1,5},{2,6},{3,7},{4,0},{5,1},{6,2},{7,3},{8,12},{9,13},{10,... | collective-permute-start | bytes 1572872 | tf_op jit(solution)/shard_map/ppermute | solution.py:49
  646.5 18.6 %collective-permute-start.31 = (bf16[256,1024]{1,0:T(8,128)(2,1)}, bf16[256,1024]{1,0:T(8,128)(2,1)}, u32[]{:S(2)}, u32[]{:S(2)}) collective-permute-start(bf16[256,1024]{1,0:T(8,128)(2,1)} %get-tuple-element.160), channel_id=1, source_target_pairs={{0,2},{1,3},{2,0},{3,1},{4,6},{5,7},{6,4},{7,5},{8,10},{9,11},{10,... | collective-permute-start | bytes 1572872 | tf_op jit(solution)/shard_map/ppermute | solution.py:49
  647.8 19.5 %collective-permute-start.29 = (bf16[256,1024]{1,0:T(8,128)(2,1)}, bf16[256,1024]{1,0:T(8,128)(2,1)}, u32[]{:S(2)}, u32[]{:S(2)}) collective-permute-start(bf16[256,1024]{1,0:T(8,128)(2,1)} %get-tuple-element.161), channel_id=1, source_target_pairs={{0,4},{1,5},{2,6},{3,7},{4,0},{5,1},{6,2},{7,3},{8,12},{9,13},{10,... | collective-permute-start | bytes 1572872 | tf_op jit(solution)/shard_map/ppermute | solution.py:49
  (52 other events, 622.0 us)
Sparse Core Ops, SparseCore 0:
  34.9 76.0 all-gather.8
  112.5 62.3 all-gather.10
  176.5 62.1 all-gather.12
  240.1 62.1 all-gather.14
  304.4 58.8 reduce-scatter.4
  365.5 60.2 reduce-scatter.6
  428.1 63.6 reduce-scatter.8
  494.2 61.8 reduce-scatter.10

commit v3 on v2

v3 whole, which is shorter than its diff:
```python
import functools
import math

import jax
import jax.numpy as jnp
from jax import lax
from jax.experimental import pallas as pl
from jax.experimental.pallas import tpu as pltpu
from jax.sharding import PartitionSpec as P

HD = 64
LANES = 128
epsilon = 1e-06
rope_base = 10000.0
bf16 = jnp.bfloat16
f32 = jnp.float32
BOTH = ("dp", "tensor")
VMEM_LIMIT = 60 * 1024 * 1024
QBLK = 256


def dot(a, b, ca, cb):
    return lax.dot_general(a, b, (((ca,), (cb,)), ((), ())), preferred_element_type=f32)


def call(kernel, out_shape, flops, nbytes, **kw):
    return pl.pallas_call(
        kernel,
        out_shape=out_shape,
        compiler_params=pltpu.CompilerParams(vmem_limit_bytes=VMEM_LIMIT),
        cost_estimate=pl.CostEstimate(flops=flops, bytes_accessed=nbytes, transcendentals=0),
        **kw,
    )


def sds(shape, dtype):
    return jax.ShapeDtypeStruct(shape, dtype)


VM = pl.BlockSpec(memory_space=pltpu.VMEM)
SM = pl.BlockSpec(memory_space=pltpu.SMEM)


def hop(x, dp_bit, t_bits):
    nd, nt = lax.axis_size("dp"), lax.axis_size("tensor")
    pairs = [
        (d * nt + t, (d ^ dp_bit) * nt + (t ^ t_bits)) for d in range(nd) for t in range(nt)
    ]
    return lax.ppermute(x, BOTH, pairs)


def hop_c(x):
    return hop(x, 0, 1)


def hop_y(x):
    return hop(x, 0, 2)


def hop_x(x):
    return hop(x, 1, 0)


def after(x, *others):
    return lax.optimization_barrier((x, *others))[0]


def gather_weights(x, weight_groups):
    return lax.all_gather(x, "dp", axis_index_groups=weight_groups)


def swap_halves(v):
    lane = lax.broadcasted_iota(jnp.int32, v.shape, 1)
    left = pltpu.roll(v, LANES - HD // 2, 1)
    right = pltpu.roll(v, HD // 2, 1)
    return jnp.where(lane % HD < HD // 2, left, right)


def in_head(tile, h):
    lane = lax.broadcasted_iota(jnp.int32, tile.shape, 1)
    return (lane < HD) if h == 0 else (lane >= HD)


def only_head(tile, h):
    return jnp.where(in_head(tile, h), tile, jnp.zeros_like(tile))


def spread_head(tile, h):
    wide = tile.astype(f32)
    return jnp.where(in_head(wide, h), wide, pltpu.roll(wide, HD, 1)).astype(tile.dtype)


def stacked(tile):
    return jnp.concatenate([only_head(tile, 0), only_head(tile, 1)], axis=0)


def key_limit(start, rows, length):
    column = lax.broadcasted_iota(jnp.int32, (1, 2 * rows), 1)
    position = start + jnp.where(column >= rows, column - rows, column)
    return jnp.minimum(position, length - 1)


def scores_t(kd, qm, limit):
    raw = dot(kd, qm, 1, 1) * (1.0 / math.sqrt(HD))
    key = lax.broadcasted_iota(jnp.int32, raw.shape, 0)
    return jnp.where(key <= limit, raw, -1e30)


def attend_kernel(
    where_ref, rows, w, cos, sin,
    q_ref, k_ref, v_ref, ctx_ref, lse_ref, keep_ref, send_ref,
):
    core, length = where_ref[0], where_ref[1]
    seq, width = rows.shape
    half = seq // 2
    kw = k_ref.shape[1] // 2
    qw = 2 * kw
    cut = qw + 2 * kw
    for blk in range(seq // QBLK):
        sl = slice(blk * QBLK, (blk + 1) * QBLK)
        c, s = cos[sl], sin[sl]
        for y in range(2):
            pre = dot(rows[sl], w[y, :, :, :cut].reshape(width, cut), 1, 0)
            for tile in range((qw + kw) // LANES):
                col = pre[:, tile * LANES:(tile + 1) * LANES]
                turned = (col * c + swap_halves(col) * s).astype(bf16)
                if tile * LANES < qw:
                    q_ref[sl, y * qw + tile * LANES:y * qw + (tile + 1) * LANES] = turned
                else:
                    at = y * kw + tile * LANES - qw
                    k_ref[sl, at:at + LANES] = turned
            v_ref[sl, y * kw:(y + 1) * kw] = pre[:, qw + kw:].astype(bf16)
    for g in range(2 * qw // LANES):
        kv = slice(g // 2 * LANES, (g // 2 + 1) * LANES)
        cols = slice(g * LANES, (g + 1) * LANES)
        kd = spread_head(k_ref[:, kv], g % 2)
        vd_t = spread_head(v_ref[:, kv], g % 2).T
        for blk in range(seq // QBLK):
            top = (blk + 1) * QBLK
            sl = slice(blk * QBLK, top)
            s = scores_t(kd[:top], stacked(q_ref[sl, cols]), key_limit(blk * QBLK, QBLK, length))
            peak = jnp.max(s, axis=0, keepdims=True)
            e = jnp.exp(s - peak)
            total = jnp.sum(e, axis=0, keepdims=True)
            p = (e * (1.0 / total)).astype(bf16)
            ctx = dot(vd_t[:, :top], p, 1, 0).T
            tile = jnp.where(in_head(ctx[:QBLK], 0), ctx[:QBLK], ctx[QBLK:])
            ctx_ref[sl, cols] = tile.astype(bf16)
            lse = peak + jnp.log(total)
            lse_ref[2 * g:2 * g + 1, sl] = lse[:, :QBLK]
            lse_ref[2 * g + 1:2 * g + 2, sl] = lse[:, QBLK:]
    for out_ref, side in ((send_ref, 1 - core), (keep_ref, core)):
        at = pl.ds(pl.multiple_of(side * half, half), half)
        out = dot(ctx_ref[at, :qw], w[0, :, :, cut:].reshape(width, qw), 1, 1)
        out += dot(ctx_ref[at, qw:], w[1, :, :, cut:].reshape(width, qw), 1, 1)
        out_ref[...] = out.astype(bf16)


def attend_back_kernel(
    where_ref, rows, gb_ref, w, cos, sin, q_ref, k_ref, v_ref, ctx_ref, lse_ref,
    dw_ref, keep_ref, send_ref,
    gc_ref, dqkv_ref, dk_ref, dv_ref,
):
    core, length = where_ref[0], where_ref[1]
    seq, width = rows.shape
    half = seq // 2
    kw = k_ref.shape[1] // 2
    qw = 2 * kw
    cut = qw + 2 * kw
    per_dp = dw_ref.shape[1:3]
    at_own = pl.ds(pl.multiple_of(core * half, half), half)
    at_peer = pl.ds(pl.multiple_of((1 - core) * half, half), half)
    for y in range(2):
        part = slice(y * qw, (y + 1) * qw)
        gc_ref[:, part] = dot(gb_ref[...], w[y, :, :, cut:].reshape(width, qw), 1, 0).astype(bf16)
        dw_ref[y, :, :, cut:] = dot(gb_ref[...], ctx_ref[:, part], 0, 0).astype(bf16).reshape(per_dp + (qw,))
    scale = 1.0 / math.sqrt(HD)
    folded = None
    for g in range(2 * qw // LANES):
        y = g // 2
        kv = slice(y * LANES, (y + 1) * LANES)
        cols = slice(g * LANES, (g + 1) * LANES)
        kd = spread_head(k_ref[:, kv], g % 2)
        kd_t = kd.T
        vd = spread_head(v_ref[:, kv], g % 2)
        for blk in reversed(range(seq // QBLK)):
            top = (blk + 1) * QBLK
            sl = slice(blk * QBLK, top)
            qm = stacked(q_ref[sl, cols])
            gm = stacked(gc_ref[sl, cols])
            s = scores_t(kd[:top], qm, key_limit(blk * QBLK, QBLK, length))
            lse = jnp.concatenate([lse_ref[2 * g:2 * g + 1, sl], lse_ref[2 * g + 1:2 * g + 2, sl]], axis=1)
            p = jnp.exp(s - lse)
            gw = dot(vd[:top], gm, 1, 1)
            centre = jnp.sum(p * gw, axis=0, keepdims=True)
            ds = (p * (gw - centre) * scale).astype(bf16)
            dv = dot(p.astype(bf16), gm, 1, 0)
            dk = dot(ds, qm, 1, 0)
            dq = dot(kd_t[:, :top], ds, 1, 0).T
            if top == seq:
                dk_ref[...] = dk
                dv_ref[...] = dv
            else:
                dk_ref[:top] += dk
                dv_ref[:top] += dv
            tile = jnp.where(in_head(dq[:QBLK], 0), dq[:QBLK], dq[QBLK:])
            back = tile * cos[sl] - swap_halves(tile) * sin[sl]
            at = y * cut + g % 2 * LANES
            dqkv_ref[sl, at:at + LANES] = back.astype(bf16)
        dk_all = dk_ref[...] + pltpu.roll(dk_ref[...], HD, 1)
        dv_all = dv_ref[...] + pltpu.roll(dv_ref[...], HD, 1)
        if g % 2 == 0:
            folded = (dk_all, dv_all)
        else:
            dk_pair = jnp.where(in_head(dk_all, 0), folded[0], dk_all)
            dv_pair = jnp.where(in_head(dv_all, 0), folded[1], dv_all)
            at = y * cut + qw
            back = dk_pair * cos[...] - swap_halves(dk_pair) * sin[...]
            dqkv_ref[:, at:at + LANES] = back.astype(bf16)
            dqkv_ref[:, at + LANES:at + 2 * LANES] = dv_pair.astype(bf16)
            part = slice(y * cut, (y + 1) * cut)
            dw_ref[y, :, :, :cut] = dot(rows[...], dqkv_ref[:, part], 0, 0).astype(bf16).reshape(per_dp + (cut,))
    for out_ref, at in ((send_ref, at_peer), (keep_ref, at_own)):
        out = dot(dqkv_ref[at, :cut], w[0, :, :, :cut].reshape(width, cut), 1, 1)
        out += dot(dqkv_ref[at, cut:], w[1, :, :, :cut].reshape(width, cut), 1, 1)
        out_ref[...] = out.astype(bf16)


def own_place():
    return lax.axis_index("dp") % 2 * 4 + lax.axis_index("tensor")


def plane_devices():
    d, p = lax.axis_index("dp"), own_place()
    return [{"dp": d + ((p ^ j) // 4 - p // 4), "tensor": (p ^ j) % 4} for j in range(8)]


def deal_out(p, plane_peers, w_send, numbers, dealt, send_sem, recv_sem):
    copies = []
    for i, e in enumerate(numbers):
        for j in (6, 7, 2, 4, 3, 5, 1):
            copies.append(
                pltpu.make_async_remote_copy(
                    src_ref=w_send.at[p ^ j, e], dst_ref=dealt[i].at[j], send_sem=send_sem.at[i, j],
                    recv_sem=recv_sem.at[i, j], device_id=plane_peers[j], device_id_type=pl.DeviceIdType.MESH,
                )
            )
        copies.append(pltpu.make_async_copy(w_send.at[p, e], dealt[i].at[0], send_sem.at[i, 0]))
    for copy in copies:
        copy.start()
    return copies


def deal_kernel(w_send, *refs):
    dealt, (send_sem, recv_sem) = refs[:-2], refs[-2:]
    p = own_place()
    peers = plane_devices()
    barrier = pltpu.get_barrier_semaphore()
    for peer in peers[1:]:
        pl.semaphore_signal(barrier, inc=1, device_id=peer, device_id_type=pl.DeviceIdType.MESH)
    pl.semaphore_wait(barrier, 7)
    for copy in deal_out(p, peers, w_send, range(len(dealt)), dealt, send_sem, recv_sem):
        copy.wait()


def rank_rows(lengths, routes_t, block, ranks_ref):
    blocks, wide = ranks_ref.shape[1:3]
    seq_len = block * blocks // lengths.shape[0]
    local = wide // 16
    row = lax.broadcasted_iota(jnp.int32, (wide, block), 0)
    number = jnp.where(row % 8 < local, row // 8 * local + row % 8, -1)
    low = lax.broadcasted_iota(jnp.int32, (block, block), 0)
    high = lax.broadcasted_iota(jnp.int32, (block, block), 1)
    before = (low < high).astype(f32).astype(bf16)
    for b in range(blocks):
        at = slice(b * block, (b + 1) * block)
        position = lax.broadcasted_iota(jnp.int32, (wide, block), 1) + b * block % seq_len
        hit = jnp.zeros((wide, block), jnp.bool_)
        for k in range(routes_t.shape[0]):
            hit = hit | (routes_t[k:k + 1, at] == number)
        hit = hit & (position < lengths[b * block // seq_len])
        earlier = dot(hit.astype(f32).astype(bf16), before, 1, 0)
        ranks_ref[0, b] = jnp.where(hit, earlier, -1.0).astype(bf16)


def gather_kernel(later, lengths, tokens, gain, routes_t, w_mine, w_send, rows_ref, w_ref, ranks_ref, *refs):
    dealt, (send_sem, recv_sem, row_sem, deal_send, deal_recv) = refs[:-5], refs[-5:]
    d, t = lax.axis_index("dp"), lax.axis_index("tensor")
    planes = w_ref.shape[1] // 2
    half = tokens.shape[0]
    z, x, core = d // 2, d % 2, t % 2

    def device(dp, tensor):
        return {"dp": dp, "tensor": tensor}

    def plane(dz):
        return lax.rem(z + dz, planes)

    x_peer, y_peer = device(z * 2 + 1 - x, t), device(d, (t + 2) % 4)
    core_peer = device(d, t + 1 - 2 * core)
    z_peers = [device(plane(dz) * 2 + x, t) for dz in range(1, planes)]
    barrier = pltpu.get_barrier_semaphore()
    p = own_place()
    plane_peers = plane_devices()
    for peer in [*z_peers, x_peer, *plane_peers[1:4], *plane_peers[5:]]:
        pl.semaphore_signal(barrier, inc=1, device_id=peer, device_id_type=pl.DeviceIdType.MESH)
    pl.semaphore_wait(barrier, planes + 6)

    copies = []

    def push(source, side, dp, peer):
        copy = pltpu.make_async_remote_copy(
            src_ref=source, dst_ref=w_ref.at[side, dp], send_sem=send_sem.at[len(copies)],
            recv_sem=recv_sem.at[side, dp], device_id=peer, device_id_type=pl.DeviceIdType.MESH,
        )
        copy.start()
        copies.append(copy)

    def arrive(side, dp):
        slot = w_ref.at[side, dp]
        pltpu.make_async_remote_copy(
            src_ref=slot, dst_ref=slot, send_sem=send_sem.at[0], recv_sem=recv_sem.at[side, dp],
            device_id=x_peer, device_id_type=pl.DeviceIdType.MESH,
        ).wait_recv()

    for peer in z_peers:
        push(w_mine, 0, d, peer)
    push(w_mine, 0, d, x_peer)
    push(w_mine, 1, d, y_peer)
    pair, last = dealt
    deals = deal_out(p, plane_peers, w_send, later, (pair.at[0], pair.at[1], last), deal_send, deal_recv)
    values = tokens[...].astype(f32)
    inverse = lax.rsqrt(jnp.mean(values * values, axis=1, keepdims=True) + epsilon)
    at = pl.ds(pl.multiple_of(core * half, half), half)
    rows_ref[at] = (values * inverse * gain[...]).astype(bf16)
    row_copy = pltpu.make_async_remote_copy(
        src_ref=rows_ref.at[at], dst_ref=rows_ref.at[at], send_sem=row_sem.at[0], recv_sem=row_sem.at[1],
        device_id=core_peer, device_id_type=pl.DeviceIdType.MESH,
    )
    row_copy.start()
    w_ref[0, d] = w_mine[...]
    rank_rows(lengths, routes_t, half, ranks_ref)
    rank_copy = pltpu.make_async_remote_copy(
        src_ref=ranks_ref.at[0], dst_ref=ranks_ref.at[1], send_sem=row_sem.at[2], recv_sem=row_sem.at[3],
        device_id=plane_peers[4], device_id_type=pl.DeviceIdType.MESH,
    )
    rank_copy.start()
    near = [plane(dz) * 2 + x for dz in range(planes)]
    over = [plane(dz) * 2 + 1 - x for dz in range(planes)]

    def turn(dz):
        arrive(0, over[dz])
        if dz < planes // 2:
            push(w_ref.at[0, over[dz]], 1, over[dz], y_peer)
        arrive(1, near[dz])
        if dz >= planes // 2:
            push(w_ref.at[1, near[dz]], 1, near[dz], x_peer)

    for dz in range(1, planes):
        arrive(0, near[dz])
        push(w_ref.at[0, near[dz]], 0, near[dz], x_peer)
        push(w_ref.at[0, near[dz]], 1, near[dz], y_peer)
        turn(dz - 1)
    turn(planes - 1)
    for dz in range(planes):
        arrive(1, over[dz])
    for copy in copies:
        copy.wait_send()
    row_copy.wait()
    rank_copy.wait()
    for copy in deals:
        copy.wait()


def masked_shares(logits, hit, axis):
    peak = jnp.max(jnp.where(hit, logits, -1e30), axis=axis, keepdims=True)
    e = jnp.where(hit, jnp.exp(jnp.where(hit, logits - peak, 0.0)), 0.0)
    total = jnp.sum(e, axis=axis, keepdims=True)
    return e / jnp.where(total > 0.0, total, 1.0)


def split16(v):
    high = v.astype(bf16)
    return high, (v - high.astype(f32)).astype(bf16)


def neighbours():
    peers = plane_devices()
    return peers[4], peers[2], peers[1]


def greet(peers):
    barrier = pltpu.get_barrier_semaphore()
    for peer in peers:
        pl.semaphore_signal(barrier, inc=1, device_id=peer, device_id_type=pl.DeviceIdType.MESH)
    pl.semaphore_wait(barrier, len(peers))


def remote(source, target, send_sem, recv_sem, peer):
    return pltpu.make_async_remote_copy(
        src_ref=source, dst_ref=target, send_sem=send_sem, recv_sem=recv_sem,
        device_id=peer, device_id_type=pl.DeviceIdType.MESH,
    )


def block_ranks(ranks, j):
    return ranks[j // 4, lax.axis_index("tensor") ^ (j % 4)].astype(f32)


def own_group():
    return pl.multiple_of(own_place() * 8, 8)


def placing(ranks, cap):
    slot = lax.broadcasted_iota(jnp.int32, (cap, ranks.shape[1]), 0).astype(f32)
    return [(slot == ranks[e:e + 1]).astype(f32) for e in range(ranks.shape[0])]


def mix_kernel(
    local, cap, tokens, keep, send, live, gain, out_own, out_y, out_x, ranks, router_t,
    hidden_ref, normed_ref, inv_ref, gates_ref, x_hbm, g_hbm,
    normed_buf, out_buf, got_ref, stage_ref, ranks_ref, shares_ref,
    send_sem, recv_sem, core_sem, stage_sem,
):
    x_peer, y_peer, core_peer = neighbours()
    greet((x_peer, y_peer, core_peer))
    rows = tokens.shape[0]
    low, high = pl.ds(0, rows // 2), pl.ds(rows // 2, rows // 2)
    sent = []

    def push(kind, source, target, slot, peer):
        copy = remote(source, target, send_sem.at[kind, slot], recv_sem.at[kind, slot], peer)
        copy.start()
        sent.append(copy)

    def arrive(kind, target, slot):
        remote(target, target, send_sem.at[kind, slot], recv_sem.at[kind, slot], x_peer).wait_recv()

    core_copy = remote(send, got_ref, core_sem.at[0], core_sem.at[1], core_peer)
    core_copy.start()
    push(1, out_y.at[low], out_buf.at[6, low], 6, x_peer)
    push(1, out_x.at[high], out_buf.at[6, high], 8, y_peer)
    push(1, out_own, out_buf.at[1], 1, core_peer)
    push(1, out_y, out_buf.at[3], 3, core_peer)
    push(1, out_x, out_buf.at[5], 5, core_peer)
    core_copy.wait()
    branch = keep[...].astype(f32) + got_ref[...].astype(f32)
    hidden = tokens[...].astype(f32) + live[...] * branch
    inverse = lax.rsqrt(jnp.mean(hidden * hidden, axis=1, keepdims=True) + epsilon)
    hidden_ref[...] = hidden
    inv_ref[...] = inverse
    normed = (hidden * inverse * gain[...]).astype(bf16)
    normed_ref[...] = normed
    normed_buf[0] = normed
    own = normed_buf.at[0]
    push(0, own, normed_buf.at[2], 2, y_peer)
    push(0, own, normed_buf.at[4], 4, x_peer)
    push(0, own, normed_buf.at[1], 1, core_peer)

    staged = []

    def place(kind, j, source):
        n = len(staged)
        if n >= 2:
            staged[n - 2].wait()
        group = own_group()
        ranks_ref[...] = block_ranks(ranks, j)
        places = placing(ranks_ref[pl.ds(group, 8)][:local], cap)
        if kind == 0:
            logits = dot(router_t[...], source[...], 1, 1)
            shares_ref[...] = masked_shares(logits, ranks_ref[...] >= 0.0, 0)
            shares = shares_ref[pl.ds(group, 8)]
            for e in range(local):
                gates_ref[e, j] = jnp.sum(places[e] * shares[e:e + 1], axis=1, keepdims=True)
        matrix = jnp.concatenate([m.astype(bf16) for m in places], axis=0)
        placed = dot(matrix, source[...], 1, 0).astype(bf16)
        stage_ref[n % 2] = placed.reshape(local, cap, -1)
        copy = pltpu.make_async_copy(
            stage_ref.at[n % 2], (x_hbm if kind == 0 else g_hbm).at[:, j], stage_sem.at[n % 2]
        )
        copy.start()
        staged.append(copy)

    place(1, 0, out_own)
    place(1, 2, out_y)
    place(1, 4, out_x)
    place(0, 0, own)
    for j in (1, 3, 5):
        arrive(1, out_buf.at[j], j)
        place(1, j, out_buf.at[j])
    arrive(1, out_buf.at[6, low], 6)
    arrive(1, out_buf.at[6, high], 8)
    push(1, out_buf.at[6], out_buf.at[7], 7, core_peer)
    arrive(0, normed_buf.at[1], 1)
    place(0, 1, normed_buf.at[1])
    place(1, 6, out_buf.at[6])
    arrive(0, normed_buf.at[2], 2)
    push(0, normed_buf.at[2, low], normed_buf.at[6, low], 6, x_peer)
    push(0, normed_buf.at[2], normed_buf.at[3], 3, core_peer)
    arrive(0, normed_buf.at[4], 4)
    push(0, normed_buf.at[4, high], normed_buf.at[6, high], 8, y_peer)
    push(0, normed_buf.at[4], normed_buf.at[5], 5, core_peer)
    arrive(1, out_buf.at[7], 7)
    place(1, 7, out_buf.at[7])
    place(0, 2, normed_buf.at[2])
    place(0, 4, normed_buf.at[4])
    for j in (3, 5):
        arrive(0, normed_buf.at[j], j)
        place(0, j, normed_buf.at[j])
    arrive(0, normed_buf.at[6, low], 6)
    arrive(0, normed_buf.at[6, high], 8)
    push(0, normed_buf.at[6], normed_buf.at[7], 7, core_peer)
    place(0, 6, normed_buf.at[6])
    arrive(0, normed_buf.at[7], 7)
    place(0, 7, normed_buf.at[7])
    for copy in sent:
        copy.wait_send()
    for copy in staged[-2:]:
        copy.wait()


def return_kernel(local, cap, *refs):
    dxs, ys, refs = refs[:local], refs[local:2 * local], refs[2 * local:]
    (
        ranks, normed, hidden_in, inv, out_grad, router, hits, live, gain,
        grad_hidden_ref, branch_ref, router_grad_ref, gain_grad_ref, y_ref,
        load_ref, part_ref, core_ref, total_ref, diag_ref, last_ref, y_part, y_core, ranks_ref,
        load_sem, send_sem, recv_sem, y_send, y_recv, branch_sem,
    ) = refs
    x_peer, y_peer, core_peer = neighbours()
    core = lax.axis_index("tensor") % 2
    greet((x_peer, y_peer, core_peer))
    rows, width = normed.shape
    wide = part_ref.shape[-1]
    half = rows // 2
    low, high = pl.ds(0, half), pl.ds(half, half)
    order = [(0, j) for j in (7, 6, 5, 4, 3, 2, 1, 0)] + [(1, j) for j in (7, 5, 3, 1, 6, 4, 2, 0)]
    depth = load_ref.shape[0]
    sent = []

    def loads(n):
        kind, j = order[n]
        slot = n % depth
        cols = wide if kind == 0 else width
        return [
            pltpu.make_async_copy(
                (ys if kind else dxs)[e].at[j],
                load_ref.at[slot, pl.ds(e * cap, cap), pl.ds(0, cols)], load_sem.at[slot, e],
            )
            for e in range(local)
        ]

    def start(n):
        if n < len(order):
            for copy in loads(n):
                copy.start()

    for n in range(depth - 1):
        start(n)
    done = [0]

    def combined():
        n = done[0]
        done[0] += 1
        start(n + depth - 1)
        for copy in loads(n):
            copy.wait()
        kind, j = order[n]
        ranks_ref[...] = block_ranks(ranks, j)
        places = placing(ranks_ref[pl.ds(own_group(), 8)][:local], cap)
        matrix = jnp.concatenate([m.astype(bf16) for m in places], axis=0)
        values = load_ref[n % depth] if kind == 0 else load_ref[n % depth, :, :width]
        return dot(matrix, values, 0, 0)

    def push(source, target, n, peer):
        copy = remote(source, target, send_sem.at[n], recv_sem.at[n], peer)
        copy.start()
        sent.append(copy)

    def arrive(target, n):
        remote(target, target, send_sem.at[n], recv_sem.at[n], x_peer).wait_recv()

    def far_core(k):
        part_ref[k] = combined().astype(bf16)
        push(part_ref.at[k], core_ref.at[k], k, core_peer)

    def near_core(k):
        mine = combined()
        arrive(core_ref.at[k], k)
        return mine + core_ref[k].astype(f32)

    far_core(3)
    total_ref[2] = near_core(3).astype(bf16)
    push(total_ref.at[2, low], diag_ref.at[0], 4, x_peer)
    push(total_ref.at[2, high], diag_ref.at[1], 5, y_peer)
    far_core(2)
    total_ref[1] = near_core(2).astype(bf16)
    push(total_ref.at[1, low], last_ref.at[0, low], 6, x_peer)
    far_core(1)
    total_ref[0] = near_core(1).astype(bf16)
    push(total_ref.at[0, high], last_ref.at[1, high], 7, y_peer)
    far_core(0)
    part_own = near_core(0).astype(bf16)
    y_copies = []
    total_ref[3] = part_own

    def y_far(k):
        y_part[k] = combined().astype(bf16)
        copy = remote(y_part.at[k], y_core.at[k], y_send.at[k], y_recv.at[k], core_peer)
        copy.start()
        y_copies.append(copy)

    y_far(3)
    y_far(2)
    arrive(diag_ref.at[1], 5)
    total_ref[1, high] = (total_ref[1, high].astype(f32) + diag_ref[1].astype(f32)).astype(bf16)
    push(total_ref.at[1, high], last_ref.at[0, high], 8, x_peer)
    arrive(diag_ref.at[0], 4)
    total_ref[0, low] = (total_ref[0, low].astype(f32) + diag_ref[0].astype(f32)).astype(bf16)
    push(total_ref.at[0, low], last_ref.at[1, low], 9, y_peer)
    y_far(1)
    y_far(0)
    for k in (3, 2, 1, 0):
        mine = combined()
        y_copies[3 - k].wait()
        y_ref[k ^ (own_place() // 2)] = (mine + y_core[k].astype(f32)).astype(bf16)

    hit = hits[...] > 0.0
    shares = masked_shares(dot(normed[...], router[...], 1, 0), hit, 1)
    arrive(last_ref.at[0, low], 6)
    arrive(last_ref.at[1, high], 7)
    arrive(last_ref.at[0, high], 8)
    arrive(last_ref.at[1, low], 9)
    for copy in sent:
        copy.wait_send()

    def summed(lo, hi):
        cols = pl.ds(lo, hi - lo)
        return (
            total_ref[3, :, cols].astype(f32) + last_ref[0, :, cols].astype(f32) + last_ref[1, :, cols].astype(f32)
        )

    grad_shares = jnp.where(hit, summed(width, wide), 0.0)
    grad_chosen = shares * (grad_shares - jnp.sum(shares * grad_shares, axis=1, keepdims=True))
    top, rest = split16(grad_chosen)
    hidden, inverse = hidden_in[...], inv[...]
    grad_mix = summed(0, width) + dot(top, router[...], 1, 1) + dot(rest, router[...], 1, 1)
    weighted = grad_mix * gain[...]
    centre = jnp.mean(hidden * weighted, axis=1, keepdims=True)
    grad_hidden = out_grad[...].astype(f32) + inverse * weighted - hidden * (inverse * inverse * inverse * centre)
    grad_hidden_ref[...] = grad_hidden
    at = pl.ds(pl.multiple_of(core * rows, rows), rows)
    branch_ref[at] = (live[...] * grad_hidden).astype(bf16)
    branch_copy = remote(branch_ref.at[at], branch_ref.at[at], branch_sem.at[0], branch_sem.at[1], core_peer)
    branch_copy.start()
    gain_grad_ref[...] = jnp.sum(grad_mix * hidden * inverse, axis=0, keepdims=True)
    experts = router_grad_ref.shape[0]
    router_grad_ref[...] = (dot(top, normed[...], 0, 0) + dot(rest, normed[...], 0, 0))[:experts]
    branch_copy.wait()


def expert_kernel(expert, local, steps, carry, chained, x_hbm, g_hbm, gates_hbm, *refs):
    sources, refs = refs[:steps], refs[steps:]
    if carry:
        (up_from, down_from), refs = refs[:2], refs[2:]
    if expert % 2:
        refs = refs[1:]
    if carry:
        (up_to, down_to), refs = refs[3:5], refs[:3] + refs[5:]
    y_hbm, dx_hbm, dw_hbm, x_ref, g_ref, gates_ref, w_buf, y_ref, dx_ref, dw_ref, in_sem, w_sem, out_sem, z_sem = refs
    d, t, p = lax.axis_index("dp"), lax.axis_index("tensor"), own_place()
    members, _, _, deep, quarter = w_buf.shape
    blocks = [(dp // 2, dp % 2 * 4) for dp in range(2 * members)]
    z = d // 2
    if carry:
        above = {"dp": lax.rem(z + 1, members) * 2 + d % 2, "tensor": t}
        below = {"dp": lax.rem(z + members - 1, members) * 2 + d % 2, "tensor": t}
        greet((above, below))
        up = remote(up_from, up_to, z_sem.at[0], z_sem.at[1], above)
        down = remote(down_from, down_to, z_sem.at[2], z_sem.at[3], below)

        @pl.when((z >= carry - 1) & (z < members - 1))
        def _():
            up.start()

        @pl.when((z > 0) & (z <= members - carry))
        def _():
            down.start()

    def settle():
        @pl.when((z >= carry - 1) & (z < members - 1))
        def _():
            up.wait_send()

        @pl.when(z >= carry)
        def _():
            up.wait_recv()

        @pl.when((z > 0) & (z <= members - carry))
        def _():
            down.wait_send()

        @pl.when(z < members - carry)
        def _():
            down.wait_recv()

    def fetch(act):
        if not chained:
            source = sources[0] if expert in (0, local - 1) else sources[0].at[:, expert - 1]
            act(pltpu.make_async_copy(source, w_buf, w_sem.at[0]))
            return
        act(pltpu.make_async_copy(sources[0], w_buf.at[z], w_sem.at[0]))
        for n, source in enumerate(sources[1:]):
            origin = z - (n // 2 + 1) if n % 2 == 0 else z + n // 2 + 1

            @pl.when((origin >= 0) & (origin < members))
            def _():
                act(pltpu.make_async_copy(source, w_buf.at[origin], w_sem.at[n + 1]))

    x_copy = pltpu.make_async_copy(x_hbm.at[expert], x_ref, in_sem.at[0])
    g_copy = pltpu.make_async_copy(g_hbm.at[expert], g_ref, in_sem.at[1])
    gates_copy = pltpu.make_async_copy(gates_hbm.at[expert], gates_ref, in_sem.at[2])
    x_copy.start()
    fetch(lambda copy: copy.start())
    g_copy.start()
    gates_copy.start()
    slots, width = x_ref.shape[0] * x_ref.shape[1], x_ref.shape[2]

    def weight(which):
        rows = [
            jnp.concatenate([w_buf[at, (side + q) ^ p, which] for q in range(4)], axis=1) for at, side in blocks
        ]
        return jnp.concatenate(rows, axis=0)

    outs = []

    def send(source, target):
        copy = pltpu.make_async_copy(source, target, out_sem.at[len(outs)])
        copy.start()
        outs.append(copy)

    x_copy.wait()
    fetch(lambda copy: copy.wait())
    x = x_ref[...].reshape(slots, width)
    w_gate, w_up, w_down = weight(0), weight(1), weight(2)
    gate_lin = dot(x, w_gate, 1, 0)
    up_lin = dot(x, w_up, 1, 0)
    g_copy.wait()
    gates_copy.wait()
    g = g_ref[...].reshape(slots, width)
    gates = gates_ref[...].reshape(slots, 1)
    grad_scaled = dot(g, w_down, 1, 0)
    sigmoid = 1.0 / (1.0 + jnp.exp(-gate_lin))
    silu = gate_lin * sigmoid
    product = silu * up_lin
    grad_gates = jnp.sum(grad_scaled * product, axis=1, keepdims=True)
    scaled_hidden = (gates * product).astype(bf16)
    grad_act = gates * grad_scaled
    grad_gate_lin = (grad_act * up_lin * sigmoid * (1.0 + gate_lin * (1.0 - sigmoid))).astype(bf16)
    grad_up_lin = (grad_act * silu).astype(bf16)
    y_ref[...] = dot(scaled_hidden, w_down, 1, 1).astype(bf16).reshape(y_ref.shape)
    send(y_ref, y_hbm)
    dx = dot(grad_gate_lin, w_gate, 1, 1) + dot(grad_up_lin, w_up, 1, 1)
    dx_ref[:, :, :width] = dx.astype(bf16).reshape(y_ref.shape)
    lane = lax.broadcasted_iota(jnp.int32, (slots, LANES), 1)
    tail = jnp.where(lane == p * local + expert, grad_gates, 0.0).astype(bf16)
    dx_ref[:, :, width:] = tail.reshape(dx_ref.shape[:2] + (LANES,))
    send(dx_ref, dx_hbm)
    for which, (left, right) in enumerate(((x, grad_gate_lin), (x, grad_up_lin), (g, scaled_hidden))):
        grad = dot(left, right, 0, 0).astype(bf16)
        for dp, (at, side) in enumerate(blocks):
            for q in range(4):
                dw_ref[at, side + q, which] = grad[dp * deep:(dp + 1) * deep, q * quarter:(q + 1) * quarter]
        send(dw_ref.at[:, :, which], dw_hbm.at[:, expert % 2, :, which])
    for copy in outs:
        copy.wait()
    if carry:
        settle()


def all_peers(d, t, planes):
    peers = [{"dp": d, "tensor": t ^ 1}, {"dp": d, "tensor": t ^ 2}]
    bit = 1
    while bit < 2 * planes:
        peers.append({"dp": d ^ bit, "tensor": t})
        bit *= 2
    return peers


def tail_kernel(
    tokens, keep, send, grad_hidden, gain, router_grad, gain_mix_grad, dw, sums,
    out_ref, small_ref, grad_ref, back_ref,
    got_ref, first_ref, second_ref, diag_ref, own_ref, far_ref, small_buf,
    core_sem, send_sem, recv_sem, far_send, far_recv, small_send, small_recv, back_send, back_recv,
):
    d, t = lax.axis_index("dp"), lax.axis_index("tensor")
    planes = dw.shape[1] // 2
    half = planes // 2
    z, x = d // 2, d % 2
    doubling = all_peers(d, t, planes)
    core_peer, y_peer, x_peer = doubling[:3]
    z_peers = [{"dp": lax.rem(z + k, planes) * 2 + x, "tensor": t} for k in range(1, planes)]
    p, plane_peers = own_place(), plane_devices()
    greet((*plane_peers[1:], *z_peers))
    experts = router_grad.shape[0]
    sent = []

    def push(source, target, kind, k, peer):
        copy = remote(source, target, send_sem.at[kind, k], recv_sem.at[kind, k], peer)
        copy.start()
        sent.append(copy)

    def arrive(target, kind, k):
        remote(target, target, send_sem.at[kind, k], recv_sem.at[kind, k], x_peer).wait_recv()

    core_copy = remote(send, got_ref, core_sem.at[0], core_sem.at[1], core_peer)
    core_copy.start()
    near = [k * 2 + x for k in range(planes)]
    over = [k * 2 + 1 - x for k in range(planes)]
    for k in range(half):
        push(dw.at[1, over[k]], diag_ref.at[k], 2, k, x_peer)
        push(dw.at[1, over[half + k]], diag_ref.at[half + k], 2, half + k, y_peer)
    for k in range(half):
        push(dw.at[0, over[k]], first_ref.at[k], 0, k, x_peer)
        push(dw.at[1, near[half + k]], second_ref.at[half + k], 1, half + k, y_peer)
    backs = []
    for e in range(2):
        for j in (6, 7, 2, 4, 3, 5, 1):
            backs.append(
                remote(sums.at[e, p ^ j], back_ref.at[e, p], back_send.at[e, j], back_recv.at[e, j], plane_peers[j])
            )
        backs.append(pltpu.make_async_copy(sums.at[e, p], back_ref.at[e, p], back_send.at[e, 0]))
    for copy in backs:
        copy.start()

    core_copy.wait()
    source = tokens[...].astype(f32)
    inverse = lax.rsqrt(jnp.mean(source * source, axis=1, keepdims=True) + epsilon)
    grad = keep[...].astype(f32) + got_ref[...].astype(f32)
    small_ref[:experts] = router_grad[...]
    small_ref[experts:experts + 1] = gain_mix_grad[...]
    small_ref[experts + 1:experts + 2] = jnp.sum(grad * source * inverse, axis=0, keepdims=True)
    small_ref[experts + 2:] = jnp.zeros_like(small_ref[experts + 2:])
    small_copies = []

    def small_start(n):
        copy = remote(small_ref, small_buf.at[n], small_send.at[n], small_recv.at[n], doubling[n])
        copy.start()
        small_copies.append(copy)

    def small_end(n):
        small_copies[n].wait()
        small_ref[...] = small_ref[...] + small_buf[n]

    small_start(0)
    weighted = grad * gain[...]
    centre = jnp.mean(source * weighted, axis=1, keepdims=True)
    total = grad_hidden[...] + inverse * weighted - source * (inverse * inverse * inverse * centre)
    out_ref[...] = total.astype(bf16)
    small_end(0)
    small_start(1)
    for k in range(half):
        arrive(diag_ref.at[k], 2, k)
        own_ref[k] = (dw[1, near[k]].astype(f32) + diag_ref[k].astype(f32)).astype(bf16)
        push(own_ref.at[k], second_ref.at[k], 1, k, y_peer)
        arrive(diag_ref.at[half + k], 2, half + k)
        own_ref[half + k] = (dw[0, over[half + k]].astype(f32) + diag_ref[half + k].astype(f32)).astype(bf16)
        push(own_ref.at[half + k], first_ref.at[half + k], 0, half + k, x_peer)
    small_end(1)
    small_start(2)
    for copy in sent:
        copy.wait_send()
    for k in range(planes):
        arrive(first_ref.at[k], 0, k)
        arrive(second_ref.at[k], 1, k)
        own_ref[k] = (
            dw[0, near[k]].astype(f32) + first_ref[k].astype(f32) + second_ref[k].astype(f32)
        ).astype(bf16)
    far = []
    for k, peer in enumerate(z_peers):
        copy = remote(
            own_ref.at[lax.rem(z + k + 1, planes)], far_ref.at[k], far_send.at[k], far_recv.at[k], peer
        )
        copy.start()
        far.append(copy)
    small_end(2)
    for n in range(3, len(doubling)):
        small_start(n)
        small_end(n)
    mine = own_ref[z].astype(f32)
    for k, copy in enumerate(far):
        copy.wait()
        mine += far_ref[k].astype(f32)
    grad_ref[...] = mine
    for e in range(2):
        for n, j in enumerate((6, 7, 2, 4, 3, 5, 1)):
            backs[8 * e + n].wait_send()
            slot = back_ref.at[e, p ^ j]
            remote(slot, slot, back_send.at[e, j], back_recv.at[e, j], x_peer).wait_recv()
        backs[8 * e + 7].wait()


def shards(
    tokens,
    lengths,
    routes,
    gain_attn,
    w_query,
    w_keyvalue,
    w_out,
    gain_mixer,
    w_router,
    w_gate,
    w_up,
    w_down,
    out_grad,
):
    nd, nt = lax.axis_size("dp"), lax.axis_size("tensor")
    dp_id, t_id = lax.axis_index("dp"), lax.axis_index("tensor")
    rows, width = tokens.shape
    group_rows, top_count = routes.shape
    seq_count = lengths.shape[0]
    seq_len = group_rows // seq_count
    experts = w_router.shape[1]
    local = experts // 8
    planes = nd // 2
    deep = width // nd
    hidden = w_gate.shape[2] * nt
    capacity = (rows * top_count * 17 + experts * 16 - 1) // (experts * 16)
    cap = -(-capacity // 16) * 16
    core = t_id % 2
    z_groups = [[x + 2 * z for z in range(planes)] for x in range(2)]
    members = nd // 2
    with_place = [[a * 2 + side for a in range(members)] for side in range(2)]
    plane_groups = [
        [with_place[side][a] * nt + t for side in range(2) for t in range(nt)] for a in range(members)
    ]

    quarter = hidden // nt

    def for_plane(w):
        return jnp.transpose(w.reshape(deep, 8, local, quarter), (1, 2, 0, 3))

    w_send = jnp.stack([for_plane(w_gate), for_plane(w_up), for_plane(w_down)], axis=2)
    q_cols, kv_cols = w_query.shape[1], w_keyvalue.shape[2]
    cut = q_cols + 2 * kv_cols
    w_mine = jnp.concatenate([w_query, w_keyvalue[:, 0], w_keyvalue[:, 1], w_out], axis=1)
    pushes = 3 * planes + 2 * (planes - 1)
    hbm = pl.BlockSpec(memory_space=pl.ANY)
    dealt_shape = sds((8, 3, deep, quarter), bf16)
    early = 1
    dealt_early = pl.pallas_call(
        deal_kernel,
        out_shape=[dealt_shape] * early,
        in_specs=[hbm], out_specs=[hbm] * early,
        scratch_shapes=[pltpu.SemaphoreType.DMA((early, 8)), pltpu.SemaphoreType.DMA((early, 8))],
        compiler_params=pltpu.CompilerParams(
            vmem_limit_bytes=VMEM_LIMIT, collective_id=1, has_side_effects=True
        ),
        cost_estimate=pl.CostEstimate(flops=10**6, bytes_accessed=20 * 2**20, transcendentals=0),
    )(w_send)
    later = tuple(range(early, local))
    normed_rows, w_attn, ranks, dealt_pair, dealt_last = pl.pallas_call(
        functools.partial(gather_kernel, later),
        out_shape=[
            sds((2 * rows, width), bf16), sds((2, nd, deep, cut + q_cols), bf16), sds((2, nt, 64, rows), bf16),
        ]
        + [sds((2,) + dealt_shape.shape, bf16), dealt_shape],
        in_specs=[SM] + [VM] * 4 + [hbm], out_specs=[VM] * 3 + [hbm] * 2,
        scratch_shapes=[
            pltpu.SemaphoreType.DMA((pushes,)), pltpu.SemaphoreType.DMA((2, nd)), pltpu.SemaphoreType.DMA((4,)),
            pltpu.SemaphoreType.DMA((len(later), 8)), pltpu.SemaphoreType.DMA((len(later), 8)),
        ],
        compiler_params=pltpu.CompilerParams(
            vmem_limit_bytes=VMEM_LIMIT, collective_id=0, has_side_effects=True
        ),
        cost_estimate=pl.CostEstimate(flops=10**7, bytes_accessed=100 * 2**20, transcendentals=0),
    )(lengths, tokens, gain_attn[None, :], routes.T, after(w_mine, *dealt_early), w_send)

    w_first = gather_weights(dealt_early[0], with_place)
    w_pair = gather_weights(dealt_pair, with_place)
    by_steps = members == local == 4
    w_last = dealt_last if by_steps else gather_weights(dealt_last, with_place)

    positions = jnp.arange(group_rows, dtype=jnp.int32) % seq_len
    live = positions < jnp.repeat(lengths, seq_len)
    own_start = t_id * rows
    live_own = lax.dynamic_slice_in_dim(live, own_start, rows, 0).astype(f32)[:, None]
    routes_own = lax.dynamic_slice_in_dim(routes, own_start, rows, 0)
    lane_ids = jnp.arange(LANES, dtype=jnp.int32)
    hits_own = jnp.any(routes_own[:, :, None] == lane_ids[None, None, :], axis=1).astype(f32) * live_own
    router = jnp.pad(w_router, ((0, 0), (0, LANES - experts)))
    router_t = jnp.pad(w_router.T.reshape(8, local, width), ((0, 0), (0, 8 - local), (0, 0))).reshape(64, width)

    half_head = HD // 2
    exponent = 2.0 * jnp.arange(half_head, dtype=f32) / HD
    angles = jnp.arange(seq_len, dtype=f32)[:, None] * jnp.exp(-math.log(rope_base) * exponent)[None, :]
    cosine, sine = jnp.cos(angles), jnp.sin(angles)
    cos_table = jnp.concatenate([cosine] * 4, axis=1)
    sin_table = jnp.concatenate([-sine, sine] * 2, axis=1)

    length = lax.dynamic_slice_in_dim(lengths, own_start // seq_len, 1, 0)[0]
    where_attn = jnp.stack([core, length]).astype(jnp.int32)

    out_late = after(out_grad, w_attn)
    out_y, out_x = hop_y(out_late), hop_x(out_late)
    q_width, k_width = 2 * q_cols, 2 * kv_cols
    heads = q_width // HD
    q, k, v, ctx, lse, keep, send = call(
        attend_kernel,
        [
            sds((seq_len, q_width), bf16), sds((seq_len, k_width), bf16), sds((seq_len, k_width), bf16),
            sds((seq_len, q_width), bf16), sds((heads, seq_len), f32),
            sds((rows, width), bf16), sds((rows, width), bf16),
        ],
        12 * 10**9, 16 * 2**20,
        in_specs=[SM] + [VM] * 4, out_specs=[VM] * 7,
    )(where_attn, normed_rows, w_attn, cos_table, sin_table)

    def remote_call(kernel, number, out_shape, flops, nbytes, **kw):
        return pl.pallas_call(
            kernel, out_shape=out_shape,
            compiler_params=pltpu.CompilerParams(
                vmem_limit_bytes=VMEM_LIMIT, collective_id=number, has_side_effects=True
            ),
            cost_estimate=pl.CostEstimate(flops=flops, bytes_accessed=nbytes, transcendentals=0),
            **kw,
        )

    dma = pltpu.SemaphoreType.DMA
    slots_shape = (local, 8, cap, width)
    hidden_own, normed_mix, inverse_mix, gates_in, rows_in, grads_in = remote_call(
        functools.partial(mix_kernel, local, cap), 2,
        [
            sds((rows, width), f32), sds((rows, width), bf16), sds((rows, 1), f32),
            sds((local, 8, cap, 1), f32), sds(slots_shape, bf16), sds(slots_shape, bf16),
        ],
        10**10, 100 * 2**20,
        in_specs=[VM] * 10, out_specs=[VM] * 4 + [hbm] * 2,
        scratch_shapes=[
            pltpu.VMEM((8, rows, width), bf16), pltpu.VMEM((8, rows, width), bf16), pltpu.VMEM((rows, width), bf16),
            pltpu.VMEM((2, local, cap, width), bf16), pltpu.VMEM((64, rows), f32), pltpu.VMEM((64, rows), f32),
            dma((2, 9)), dma((2, 9)), dma((2,)), dma((2,)),
        ],
    )(
        tokens, after(keep, w_first), send, live_own, gain_mixer[None, :], out_grad, out_y, out_x, ranks, router_t
    )
    ys, dxs, dw_pairs = [], [], []
    moving = (dealt_last, dealt_last)
    arrived = (w_last,)
    pair_shape = sds((members, 2, 8, 3, deep, quarter), bf16)
    before = []
    for e in range(local):
        step = e + 1 if by_steps and e < local - 1 else 0
        sources = ((w_first,), (w_pair,), (w_pair,), arrived)[e]
        inputs = [after(rows_in, *before), grads_in, gates_in, *sources, *(moving if step else ())]
        aliases = {}
        if e % 2:
            aliases = {len(inputs): 2}
            inputs.append(dw_pairs.pop())
        y, dx, dw, *moved = pl.pallas_call(
            functools.partial(expert_kernel, e, local, len(sources), step, len(sources) > 1),
            out_shape=[
                sds((8, cap, width), bf16), sds((8, cap, width + LANES), bf16), pair_shape,
            ] + [dealt_shape] * (2 if step else 0),
            in_specs=[hbm] * len(inputs),
            out_specs=[hbm] * (5 if step else 3),
            scratch_shapes=[
                pltpu.VMEM((8, cap, width), bf16), pltpu.VMEM((8, cap, width), bf16), pltpu.VMEM((8, cap, 1), f32),
                pltpu.VMEM((members, 8, 3, deep, quarter), bf16),
                pltpu.VMEM((8, cap, width), bf16), pltpu.VMEM((8, cap, width + LANES), bf16),
                pltpu.VMEM((members, 8, 3, deep, quarter), bf16),
                dma((3,)), dma((len(sources),)), dma((5,)), dma((4,)),
            ],
            input_output_aliases=aliases,
            compiler_params=pltpu.CompilerParams(
                vmem_limit_bytes=VMEM_LIMIT, **(dict(collective_id=3 + step, has_side_effects=True) if step else {})
            ),
            cost_estimate=pl.CostEstimate(flops=10**10, bytes_accessed=20 * 2**20, transcendentals=0),
        )(*inputs)
        if step:
            moving = tuple(moved)
            arrived += moving
        ys.append(y)
        dxs.append(dx)
        dw_pairs.append(dw)
        before = [y]

    wide = width + LANES
    grad_hidden, grad_branch, router_grad, gain_mix_grad, y_totals = remote_call(
        functools.partial(return_kernel, local, cap), 3,
        [
            sds((rows, width), f32), sds((2 * rows, width), bf16), sds((experts, width), f32), sds((1, width), f32),
            sds((4, rows, width), bf16),
        ],
        10**10, 100 * 2**20,
        in_specs=[hbm] * (2 * local) + [VM] * 9, out_specs=[VM] * 5,
        scratch_shapes=[
            pltpu.VMEM((3, local * cap, wide), bf16),
            pltpu.VMEM((4, rows, wide), bf16), pltpu.VMEM((4, rows, wide), bf16), pltpu.VMEM((4, rows, wide), bf16),
            pltpu.VMEM((2, rows // 2, wide), bf16), pltpu.VMEM((2, rows, wide), bf16),
            pltpu.VMEM((4, rows, width), bf16), pltpu.VMEM((4, rows, width), bf16), pltpu.VMEM((64, rows), f32),
            dma((3, local)), dma((10,)), dma((10,)), dma((4,)), dma((4,)), dma((2,)),
        ],
    )(
        *dxs, *ys, ranks, normed_mix, hidden_own, inverse_mix, out_grad, router, hits_own, live_own,
        gain_mixer[None, :],
    )
    chip_groups = [
        [with_place[side][a] * nt + y * 2 + c for side in range(2) for y in range(2)]
        for a in range(members) for c in range(2)
    ]
    y_terms = lax.all_to_all(y_totals, BOTH, 0, 0, tiled=True, axis_index_groups=chip_groups)
    mixed = (hidden_own + jnp.sum(y_terms.astype(f32), axis=0)).astype(bf16)

    dw_attn, keep_back, send_back = call(
        attend_back_kernel,
        [
            sds((2, nd, deep, cut + q_cols), bf16), sds((rows, width), bf16), sds((rows, width), bf16),
        ],
        25 * 10**9, 24 * 2**20,
        in_specs=[SM] + [VM] * 10, out_specs=[VM] * 3,
        scratch_shapes=[
            pltpu.VMEM((seq_len, q_width), bf16), pltpu.VMEM((seq_len, 2 * cut), bf16),
            pltpu.VMEM((seq_len, LANES), f32), pltpu.VMEM((seq_len, LANES), f32),
        ],
    )(
        where_attn, normed_rows, grad_branch, w_attn, cos_table, sin_table,
        q, k, v, ctx, lse,
    )
    doublings = 2 + (nd - 1).bit_length()
    per_dp = (deep, cut + q_cols)
    sums = [
        lax.psum_scatter(dw, "dp", scatter_dimension=0, axis_index_groups=with_place) for dw in dw_pairs
    ]
    grad_tokens, small, attn_grad, back_first = remote_call(
        tail_kernel, 8,
        [
            sds((rows, width), bf16), sds((experts + 8, width), f32), sds(per_dp, f32),
            sds((2, 8, 3, deep, quarter), bf16),
        ],
        10**8, 30 * 2**20,
        in_specs=[VM] * 8 + [hbm], out_specs=[VM] * 3 + [hbm],
        scratch_shapes=[pltpu.VMEM((rows, width), bf16)]
        + [pltpu.VMEM((planes,) + per_dp, bf16)] * 4
        + [
            pltpu.VMEM((planes - 1,) + per_dp, bf16), pltpu.VMEM((doublings, experts + 8, width), f32),
            dma((2,)), dma((3, planes)), dma((3, planes)), dma((planes - 1,)), dma((planes - 1,)),
            dma((doublings,)), dma((doublings,)), dma((2, 8)), dma((2, 8)),
        ],
    )(
        after(tokens, y_terms), keep_back, send_back, grad_hidden, gain_attn[None, :], router_grad, gain_mix_grad,
        dw_attn, sums[0],
    )

    back_last = lax.all_to_all(
        after(sums[1], grad_tokens), BOTH, 1, 1, tiled=True, axis_index_groups=plane_groups
    )

    def to_owner(which):
        parts = jnp.concatenate([back_first[:, :, which], back_last[:, :, which]], axis=0).astype(f32)
        return jnp.transpose(parts, (2, 1, 0, 3)).reshape(deep, experts, quarter)

    grad_query = attn_grad[:, :q_cols]
    grad_keyval = attn_grad[:, q_cols:cut].reshape(deep, 2, kv_cols)
    grad_out = attn_grad[:, cut:]
    return (
        mixed,
        grad_tokens,
        small[experts + 1],
        grad_query,
        grad_keyval,
        grad_out,
        small[experts],
        small[:experts].T,
        to_owner(0),
        to_owner(1),
        to_owner(2),
    )


def solution(mesh):
    placed = (
        P(("dp", "tensor"), None),
        P("dp"),
        P("dp", None),
        P(),
        P("dp", "tensor"),
        P("dp", None, "tensor"),
        P("dp", "tensor"),
        P(),
        P(),
        P("dp", None, "tensor"),
        P("dp", None, "tensor"),
        P("dp", None, "tensor"),
        P(("dp", "tensor"), None),
    )
    return jax.shard_map(
        shards,
        mesh=mesh,
        in_specs=placed,
        out_specs=(
            P(("dp", "tensor"), None),
            P(("dp", "tensor"), None),
            P(),
            P("dp", "tensor"),
            P("dp", None, "tensor"),
            P("dp", "tensor"),
            P(),
            P(),
            P("dp", None, "tensor"),
            P("dp", None, "tensor"),
            P("dp", None, "tensor"),
        ),
        check_vma=False,
    )
```

time: 683 us -> 571 us (0.84)
  waiting for transfers between devices: 242 us -> 28.6 us
  Pallas kernels: 288 us -> 471 us
  starting transfers between devices: 56.4 us -> 11.6 us
  other arithmetic: 36.3 us -> 17.3 us
  local copies, waits for them, and re-layouts: 40.2 us -> 24.1 us
    pallas_call x13 -> x7, Pallas kernels: 155 us -> 340 us  [the longest x4 145 us: shards(): pl.pallas_call(functools.partial(expert_kernel, e, local, len(sources), s...]
    ppermute x50 -> x2, waiting for transfers between devices: 156 us -> 0.01 us  [hop(): return lax.ppermute(x, BOTH, pairs)]
    all_gather x4 -> x2, waiting for transfers between devices: 51.9 us -> 0.02 us  [gather_weights(): return lax.all_gather(x, 'dp', axis_index_groups=weight_groups)]
    ppermute x50 -> x2, starting transfers between devices: 40.1 us -> 2.27 us  [hop(): return lax.ppermute(x, BOTH, pairs)]
    reduce_scatter x4 -> x2, waiting for transfers between devices: 26.9 us -> 0.02 us  [shards(): lax.psum_scatter(dw, 'dp', scatter_dimension=0, axis_index_groups=with_pl...]
    all_to_all x4 -> x2, waiting for transfers between devices: 6.76 us -> 28.5 us  [the longest x1 17.5 us: shards(): lax.all_to_all(y_totals, BOTH, 0, 0, tiled=True, axis_index_groups=chip_g...]
    convert_element_type x7 -> x1, other arithmetic: 18 us -> 1.29 us  [shards(): mixed = (hidden_own + jnp.sum(y_terms.astype(f32), axis=0)).astype(bf16)]
    pallas_call x1, Pallas kernels: 58.1 us -> 66.7 us  [shards(): pl.pallas_call(functools.partial(gather_kernel, later), out_shape=[sds((2...]
  transfers between devices with their start and end apart: 62 -> 8, of which waited for: 28 -> 2; matrix products, arithmetic and copies ran while one was open for 9% -> 4% of each run, Pallas kernels for 39% -> 77%
where the time goes in v3:
time: 571 us; the launch traced here: 567 us
  Pallas kernels  471 us (82%)
  waiting for transfers between devices  28.6 us (5%)
  local copies, waits for them, and re-layouts  24.1 us (4%)
  other arithmetic  17.3 us (3%)
  between operations  14.3 us (3%)
  starting transfers between devices  11.6 us (2%)
    pallas_call x4, Pallas kernels, shards(): pl.pallas_call(functools.partial(expert_kernel, e, local, len(sources), s...  145 us
    pallas_call x1, Pallas kernels, shards(): remote_call(tail_kernel, 8, [sds((rows, width), bf16), sds((experts + 8,...  78.8 us
    pallas_call x1, Pallas kernels, shards(): pl.pallas_call(functools.partial(gather_kernel, later), out_shape=[sds((2...  66.7 us
    pallas_call x1, Pallas kernels, shards(): remote_call(functools.partial(return_kernel, local, cap), 3, [sds((rows,...  58 us
    pallas_call x1, Pallas kernels, shards(): remote_call(functools.partial(mix_kernel, local, cap), 2, [sds((rows, wid...  57.9 us
    pallas_call x1, Pallas kernels, shards(): call(attend_back_kernel, [sds((2, nd, deep, cut + q_cols), bf16), sds((ro...  30.7 us
    pallas_call x1, Pallas kernels, shards(): call(attend_kernel, [sds((seq_len, q_width), bf16), sds((seq_len, k_width...  20 us
    all_to_all x1, waiting for transfers between devices, shards(): lax.all_to_all(y_totals, BOTH, 0, 0, tiled=True, axis_index_groups=chip_g...  17.5 us
  transfers between devices with their start and end apart: 8, of which 2 were waited for; matrix products, arithmetic and copies ran while one was open for 4% of the time, Pallas kernels for 77%

profile of v3, /device:TPU:0, one launch (start us, length us, event | category | flops | bytes accessed | tf_op | source)
XLA Modules:
  0.0 567.1 jit_solution(17584556862102104017)
XLA Ops:
  7.2 1.8 copy.75
  9.0 0.4 copy.76
  9.5 0.4 copy.77
  9.9 2.0 pad_maximum_fusion.w_send
  11.9 14.3 %shard_map.212 = bf16[8,3,128,128]{3,2,1,0:T(8,128)(2,1)} custom-call(bf16[8,4,3,128,128]{4,3,2,1,0:T(8,128)(2,1)} %pad_maximum_fusion.w_send), custom_call_target="tpu_custom_call" | custom-call | flops 1000000 | bytes 20971520 | tf_op jit(solution)/shard_map/pallas_call | solution.py:952
  26.4 0.7 pad_maximum_fusion.3.w_mine
  27.1 66.7 %shard_map.213 = (bf16[1024,1024]{1,0:T(8,128)(2,1)}, bf16[2,8,128,768]{3,2,1,0:T(8,128)(2,1)}, bf16[2,4,64,512]{3,2,1,0:T(8,128)(2,1)}, bf16[2,8,3,128,128]{4,3,2,1,0:T(8,128)(2,1)}, bf16[8,3,128,128]{3,2,1,0:T(8,128)(2,1)}) custom-call(s32[2]{0:T(128)} %lengths.1, bf16[512,1024]{1,0:T(8,128)(2,1)} %tokens.4, f32[1,1024]{1,0:T(1,128)} %bitcast.78, ...), custom_call_target="tpu_custom_call" | custom-call | flops 10000000 | bytes 104857600 | tf_op jit(solution)/shard_map/pallas_call | solution.py:963
  93.8 0.5 reduce-scatter.3.cloned.1.call-start
  94.3 1.0 collective-permute-start.1
  95.3 1.3 collective-permute-start
  96.6 0.6 dynamic_slice.9
  97.4 0.9 copy.78.live.refs_15_
  98.3 1.2 pad_add_fusion.where_ref
  99.5 0.7 pad_bitcast_fusion.router_t
  100.2 2.0 fusion.3
  102.1 1.9 pad_maximum_fusion.1
  104.0 20.0 %shard_map.214 = (bf16[1024,512]{1,0:T(8,128)(2,1)}, bf16[1024,256]{1,0:T(8,128)(2,1)}, bf16[1024,256]{1,0:T(8,128)(2,1)}, bf16[1024,512]{1,0:T(8,128)(2,1)}, f3...) custom-call(s32[2]{0:T(128)} %pad_add_fusion.where_ref, ...), custom_call_target="tpu_custom_call" | custom-call | flops 12000000000 | bytes 16777216 | tf_op jit(solution)/shard_map/pallas_call | solution.py:1009
  124.0 0.9 copy-done.12
  124.9 57.9 %shard_map.215 = (f32[512,1024]{1,0:T(8,128)}, bf16[512,1024]{1,0:T(8,128)(2,1)}, f32[512,1]{1,0:T(8,128)}, f32[4,8,144,1]{3,2,1,0:T(8,128)}, bf16[4,8,144,1024]...) custom-call(bf16[512,1024]{1,0:T(8,128)(2,1)} %tokens.4, bf16[512,1024]{1,0:T(8,128)(2,1)} %get-tuple-element.71.keep, ...), custom_call_target="tpu_custom_call" | custom-call | flops 10000000000 | bytes 104857600 | tf_op jit(solution)/shard_map/pallas_call | solution.py:1032
  182.8 49.0 %shard_map.216 = (bf16[8,144,1024]{2,1,0:T(8,128)(2,1)}, bf16[8,144,1152]{2,1,0:T(8,128)(2,1)}, bf16[4,2,8,3,128,128]{5,4,3,2,1,0:T(8,128)(2,1)}, bf16[8,3,128,1...) custom-call(bf16[4,8,144,1024]{3,2,1,0:T(8,128)(2,1)} %get-tuple-element.94.x_hbm, ...), custom_call_target="tpu_custom_call" | custom-call | flops 10000000000 | bytes 20971520 | tf_op jit(solution)/shard_map/pallas_call | solution.py:1061
  231.9 21.2 %shard_map.217 = (bf16[8,144,1024]{2,1,0:T(8,128)(2,1)}, bf16[8,144,1152]{2,1,0:T(8,128)(2,1)}, bf16[4,2,8,3,128,128]{5,4,3,2,1,0:T(8,128)(2,1)}, bf16[8,3,128,1...) custom-call(bf16[4,8,144,1024]{3,2,1,0:T(8,128)(2,1)} %get-tuple-element.94.x_hbm, ...), custom_call_target="tpu_custom_call", output_to_operand_aliasing={{2}: (6, {})} | custom-call | flops 10000000000 | bytes 20971520 | tf_op jit(solution)/shard_map/pallas_call | solution.py:1061
  253.2 56.9 %shard_map.218 = (bf16[8,144,1024]{2,1,0:T(8,128)(2,1)}, bf16[8,144,1152]{2,1,0:T(8,128)(2,1)}, bf16[4,2,8,3,128,128]{5,4,3,2,1,0:T(8,128)(2,1)}, bf16[8,3,128,1...) custom-call(bf16[4,8,144,1024]{3,2,1,0:T(8,128)(2,1)} %get-tuple-element.94.x_hbm, ...), custom_call_target="tpu_custom_call" | custom-call | flops 10000000000 | bytes 20971520 | tf_op jit(solution)/shard_map/pallas_call | solution.py:1061
  310.0 17.9 %shard_map.219 = (bf16[8,144,1024]{2,1,0:T(8,128)(2,1)}, bf16[8,144,1152]{2,1,0:T(8,128)(2,1)}, bf16[4,2,8,3,128,128]{5,4,3,2,1,0:T(8,128)(2,1)}) custom-call(bf16[4,8,144,1024]{3,2,1,0:T(8,128)(2,1)} %get-tuple-element.94.x_hbm, bf16[4,8,144,1024]{3,2,1,0:T(8,128)(2,1)} %get-tuple-element.77.g_hbm, ...), custom_call_target="tpu_custom_call", output_to_operand_aliasing={{2}: (10, {})} | custom-call | flops 10000000000 | bytes 20971520 | tf_op jit(solution)/shard_map/pallas_call | solution.py:1061
  328.1 0.7 constant_dynamic-slice_fusion
  328.9 0.8 pad.9.refs_13_
  329.7 3.4 fusion
  333.1 0.8 broadcast_select_fusion.refs_14_
  333.9 58.0 %shard_map.220 = (f32[512,1024]{1,0:T(8,128)}, bf16[1024,1024]{1,0:T(8,128)(2,1)}, f32[32,1024]{1,0:T(8,128)}, f32[1,1024]{1,0:T(1,128)}, bf16[4,512,1024]{2,1,0:T(8,128)(2,1)}) custom-call(bf16[8,144,1152]{2,1,0:T(8,128)(2,1)} %get-tuple-element.80.refs_0_, bf16[8,144,1152]{2,1,0:T(8,128)(2,1)} %get-tuple-element.87.refs_1_, ...), custom_call_target="tpu_custom_call" | custom-call | flops 10000000000 | bytes 104857600 | tf_op jit(solution)/shard_map/pallas_call | solution.py:1090
  391.9 4.9 all-to-all-start
  396.8 30.7 %shard_map.221 = (bf16[2,8,128,768]{3,2,1,0:T(8,128)(2,1)}, bf16[512,1024]{1,0:T(8,128)(2,1)}, bf16[512,1024]{1,0:T(8,128)(2,1)}) custom-call(s32[2]{0:T(128)} %pad_add_fusion.where_ref, bf16[1024,1024]{1,0:T(8,128)(2,1)} %get-tuple-element.68.rows, bf16[1024,1024]{1,0:T(8,128)(2,1)} %get-tuple-element.104.gb_ref, ...), custom_call_target="tpu_custom_call" | custom-call | flops 24999999488 | bytes 25165824 | tf_op jit(solution)/shard_map/pallas_call | solution.py:1116
  427.5 17.5 %all-to-all-done = bf16[4,512,1024]{2,1,0:T(8,128)(2,1)} async-done(((bf16[4,512,1024]{2,1,0:T(8,128)(2,1)}), bf16[4,512,1024]{2,1,0:T(8,128)(2,1)}, u32[]{:S(2)}, u32[]{:S(2)}) %all-to-all-start) | async-done | bytes 4194336 | tf_op jit(solution)/shard_map/all_to_all | solution.py:1113
  445.0 78.8 %shard_map.222 = (bf16[512,1024]{1,0:T(8,128)(2,1)}, f32[40,1024]{1,0:T(8,128)}, f32[128,768]{1,0:T(8,128)}, bf16[2,8,3,128,128]{4,3,2,1,0:T(8,128)(2,1)}) custom-call(bf16[512,1024]{1,0:T(8,128)(2,1)} %tokens.4, bf16[512,1024]{1,0:T(8,128)(2,1)} %get-tuple-element.110.keep, bf16[512,1024]{1,0:T(8,128)(2,1)} %get-tuple-element.111.send, ...), custom_call_target="tpu_custom_call" | custom-call | flops 100000000 | bytes 31457280 | tf_op jit(solution)/shard_map/pallas_call | solution.py:1136
  523.8 2.7 copy.82
  526.6 3.8 all-to-all-start.1
  530.4 3.5 convert_reduce_fusion
  533.9 1.3 add_convert_fusion
  535.2 0.7 fusion.10
  536.0 0.7 reshape.74
  536.7 0.6 fusion.11
  537.3 0.7 slice_bitcast_fusion.3
  538.0 1.5 slice_bitcast_fusion
  539.4 11.0 %all-to-all-done.1 = bf16[2,8,3,128,128]{4,3,0,2,1:T(8,128)(2,1)S(1)} async-done(((bf16[2,8,3,128,128]{4,3,0,2,1:T(8,128)(2,1)}), bf16[2,8,3,128,128]{4,3,0,2,1:T(8,128)(2,1)S(1)}, u32[]{:S(2)}, u32[]{:S(2)}) %all-to-all-start.1) | async-done | bytes 1572896 | tf_op jit(solution)/shard_map/all_to_all | solution.py:1156
  550.8 0.2 copy.88
  551.1 2.5 copy.91
  553.7 0.2 copy.86
  554.0 2.5 copy.90
  556.9 2.5 copy.89
  559.4 1.0 copy.111
  (55 shorter events, 1.7 us)
Async XLA Ops:
  7.2 1.8 copy-start.1
  7.2 2.3 copy-start.2
  7.2 116.8 %all-gather.5.cloned.1.call-start = ((), (), s32[]{:S(2)}) async-start(), calls=%async_computation.6 | async-start | bytes 3932160 | tf_op jit(solution)/shard_map/all_gather | solution.py:69
  11.9 14.4 %copy-start.6 = (bf16[128,2,128]{2,1,0:T(2,128)(2,1)S(1)}, bf16[128,2,128]{2,1,0:T(2,128)(2,1)}, u32[]{:S(2)}) copy-start(bf16[128,2,128]{2,1,0:T(2,128)(2,1)} %param.18) | copy-start | bytes 196612
  11.9 14.5 %copy-start.8 = (bf16[128,256]{1,0:T(8,128)(2,1)S(1)}, bf16[128,256]{1,0:T(8,128)(2,1)}, u32[]{:S(2)}) copy-start(bf16[128,256]{1,0:T(8,128)(2,1)} %param.19) | copy-start | bytes 196612
  11.9 14.5 %copy-start.9 = (bf16[128,256]{1,0:T(8,128)(2,1)S(1)}, bf16[128,256]{1,0:T(8,128)(2,1)}, u32[]{:S(2)}) copy-start(bf16[128,256]{1,0:T(8,128)(2,1)} %param.17) | copy-start | bytes 196612
  26.2 205.7 %all-gather.7.cloned.1.call-start = ((), (), s32[]{:S(2)}) async-start(), calls=%async_computation.7 | async-start | bytes 7864320 | tf_op jit(solution)/shard_map/all_gather | solution.py:69
  27.1 67.3 %copy-start.11 = (bf16[512,1024]{1,0:T(8,128)(2,1)S(1)}, bf16[512,1024]{1,0:T(8,128)(2,1)}, u32[]{:S(2)}) copy-start(bf16[512,1024]{1,0:T(8,128)(2,1)} %refs_12_.1) | copy-start | bytes 3145732
  27.1 69.5 %copy-start.10 = (s32[2]{0:T(128)S(1)}, s32[2]{0:T(128)}, u32[]{:S(2)}) copy-start(s32[2]{0:T(128)} %lengths.1) | copy-start | bytes 28
  27.1 70.2 %copy-start.5 = (bf16[1024,32]{0,1:T(8,128)(2,1)S(1)}, bf16[1024,32]{0,1:T(8,128)(2,1)}, u32[]{:S(2)}) copy-start(bf16[1024,32]{0,1:T(8,128)(2,1)} %param.21) | copy-start | bytes 196612
  93.8 351.1 %reduce-scatter.3.cloned.1.call-start = ((), (), s32[]{:S(2)}) async-start(), calls=%async_computation.4 | async-start | bytes 7864320 | tf_op jit(solution)/shard_map/reduce_scatter | solution.py:1134
  94.3 29.6 %collective-permute-start.1 = (bf16[512,1024]{1,0:T(8,128)(2,1)S(1)}, bf16[512,1024]{1,0:T(8,128)(2,1)S(1)}, u32[]{:S(2)}, u32[]{:S(2)}) collective-permute-start(bf16[512,1024]{1,0:T(8,128)(2,1)S(1)} %copy-done.11), channel_id=1, source_target_pairs={{0,4},{1,5},{2,6},{3,7},{4,0},{5,1},{6,2},{7,3},{8,12},{9,13},{10,... | collective-permute-start | bytes 3145736 | tf_op jit(solution)/shard_map/ppermute | solution.py:49
  95.3 28.7 %collective-permute-start = (bf16[512,1024]{1,0:T(8,128)(2,1)S(1)}, bf16[512,1024]{1,0:T(8,128)(2,1)}, u32[]{:S(2)}, u32[]{:S(2)}) collective-permute-start(bf16[512,1024]{1,0:T(8,128)(2,1)S(1)} %copy-done.11), channel_id=1, source_target_pairs={{0,2},{1,3},{2,0},{3,1},{4,6},{5,7},{6,4},{7,5},{8,10},{9,11},{10,... | collective-permute-start | bytes 3145736 | tf_op jit(solution)/shard_map/ppermute | solution.py:49
  124.0 1.0 copy-start.12
  253.1 270.7 %reduce-scatter.5.cloned.1.call-start = ((), (), s32[]{:S(2)}) async-start(), calls=%async_computation.5 | async-start | bytes 7864320 | tf_op jit(solution)/shard_map/reduce_scatter | solution.py:1134
  391.9 53.0 %all-to-all-start = ((bf16[4,512,1024]{2,1,0:T(8,128)(2,1)}), bf16[4,512,1024]{2,1,0:T(8,128)(2,1)}, u32[]{:S(2)}, u32[]{:S(2)}) async-start(bf16[4,512,1024]{2,1,0:T(8,128)(2,1)} %get-tuple-element.102), calls=%async_computation | async-start | bytes 8388608 | tf_op jit(solution)/shard_map/all_to_all | solution.py:1113
  526.6 23.9 %all-to-all-start.1 = ((bf16[2,8,3,128,128]{4,3,0,2,1:T(8,128)(2,1)}), bf16[2,8,3,128,128]{4,3,0,2,1:T(8,128)(2,1)S(1)}, u32[]{:S(2)}, u32[]{:S(2)}) async-start(bf16[2,8,3,128,128]{4,3,0,2,1:T(8,128)(2,1)} %copy.82), calls=%async_computation.3 | async-start | bytes 3145728 | tf_op jit(solution)/shard_map/all_to_all | solution.py:1156
  530.4 3.5 copy-start
  533.9 1.3 copy-start.4
  533.9 2.8 copy-start.7
  556.9 2.5 copy-start.3
Sparse Core Ops, SparseCore 0:
  26.3 75.2 all-gather.4
  103.2 127.0 all-gather.6
  253.2 121.4 reduce-scatter.2
  376.9 110.9 reduce-scatter.4

commit v4 on v3

--- a/solution.py
+++ b/solution.py
@@ -3,6 +3,7 @@
 
 import jax
 import jax.numpy as jnp
+import numpy as np
 from jax import lax
 from jax.experimental import pallas as pl
 from jax.experimental.pallas import tpu as pltpu
@@ -107,10 +108,11 @@
 
 
 def attend_kernel(
-    where_ref, rows, w, cos, sin,
+    lengths, rows, w, cos, sin,
     q_ref, k_ref, v_ref, ctx_ref, lse_ref, keep_ref, send_ref,
 ):
-    core, length = where_ref[0], where_ref[1]
+    core = lax.axis_index("tensor") % 2
+    length = lengths[lax.axis_index("tensor") // 2]
     seq, width = rows.shape
     half = seq // 2
     kw = k_ref.shape[1] // 2
@@ -157,11 +159,12 @@
 
 
 def attend_back_kernel(
-    where_ref, rows, gb_ref, w, cos, sin, q_ref, k_ref, v_ref, ctx_ref, lse_ref,
+    lengths, rows, gb_ref, w, cos, sin, q_ref, k_ref, v_ref, ctx_ref, lse_ref,
     dw_ref, keep_ref, send_ref,
     gc_ref, dqkv_ref, dk_ref, dv_ref,
 ):
-    core, length = where_ref[0], where_ref[1]
+    core = lax.axis_index("tensor") % 2
+    length = lengths[lax.axis_index("tensor") // 2]
     seq, width = rows.shape
     half = seq // 2
     kw = k_ref.shape[1] // 2
@@ -251,16 +254,35 @@
     return copies
 
 
-def deal_kernel(w_send, *refs):
-    dealt, (send_sem, recv_sem) = refs[:-2], refs[-2:]
+def deal_kernel(w_send, w_mine, *refs):
+    dealt, (line_ref, send_sem, recv_sem, line_send, line_recv) = refs[:-5], refs[-5:]
+    d, t = lax.axis_index("dp"), lax.axis_index("tensor")
+    planes = line_ref.shape[0]
+    z, x = d // 2, d % 2
     p = own_place()
     peers = plane_devices()
-    barrier = pltpu.get_barrier_semaphore()
-    for peer in peers[1:]:
-        pl.semaphore_signal(barrier, inc=1, device_id=peer, device_id_type=pl.DeviceIdType.MESH)
-    pl.semaphore_wait(barrier, 7)
-    for copy in deal_out(p, peers, w_send, range(len(dealt)), dealt, send_sem, recv_sem):
+    z_peers = [{"dp": lax.rem(z + k, planes) * 2 + x, "tensor": t} for k in range(1, planes)]
+    greet((*peers[1:], *z_peers))
+    copies = deal_out(p, peers, w_send, range(len(dealt)), dealt, send_sem, recv_sem)
+    lines = []
+    for k, peer in enumerate(z_peers):
+        copy = remote(w_mine, line_ref.at[z], line_send.at[k], line_recv.at[z], peer)
+        copy.start()
+        lines.append(copy)
+    line_ref[z] = w_mine[...]
+    for copy in copies:
         copy.wait()
+    for k in range(1, planes):
+        lines[k - 1].wait_send()
+        at = lax.rem(z + k, planes)
+        remote(line_ref.at[at], line_ref.at[at], line_send.at[0], line_recv.at[at], peers[1]).wait_recv()
+
+
+def group_rows_of(experts):
+    local = experts // 8
+    row = lax.broadcasted_iota(jnp.int32, (64, experts), 0)
+    expert = lax.broadcasted_iota(jnp.int32, (64, experts), 1)
+    return ((row % 8 < local) & (row // 8 * local + row % 8 == expert)).astype(f32).astype(bf16)
 
 
 def rank_rows(lengths, routes_t, block, ranks_ref):
@@ -283,87 +305,54 @@
         ranks_ref[0, b] = jnp.where(hit, earlier, -1.0).astype(bf16)
 
 
-def gather_kernel(later, lengths, tokens, gain, routes_t, w_mine, w_send, rows_ref, w_ref, ranks_ref, *refs):
-    dealt, (send_sem, recv_sem, row_sem, deal_send, deal_recv) = refs[:-5], refs[-5:]
-    d, t = lax.axis_index("dp"), lax.axis_index("tensor")
-    planes = w_ref.shape[1] // 2
+def gather_kernel(
+    later, lengths, tokens, gain, routes_t, router, line, w_send, rows_ref, w_ref, ranks_ref, router_ref, *refs
+):
+    (pair, last), (send_sem, recv_sem, row_sem, deal_send, deal_recv) = refs[:-5], refs[-5:]
+    planes = line.shape[0]
     half = tokens.shape[0]
-    z, x, core = d // 2, d % 2, t % 2
-
-    def device(dp, tensor):
-        return {"dp": dp, "tensor": tensor}
-
-    def plane(dz):
-        return lax.rem(z + dz, planes)
-
-    x_peer, y_peer = device(z * 2 + 1 - x, t), device(d, (t + 2) % 4)
-    core_peer = device(d, t + 1 - 2 * core)
-    z_peers = [device(plane(dz) * 2 + x, t) for dz in range(1, planes)]
-    barrier = pltpu.get_barrier_semaphore()
-    p = own_place()
-    plane_peers = plane_devices()
-    for peer in [*z_peers, x_peer, *plane_peers[1:4], *plane_peers[5:]]:
-        pl.semaphore_signal(barrier, inc=1, device_id=peer, device_id_type=pl.DeviceIdType.MESH)
-    pl.semaphore_wait(barrier, planes + 6)
-
+    x, core = lax.axis_index("dp") % 2, lax.axis_index("tensor") % 2
+    p, plane_peers = own_place(), plane_devices()
+    x_peer, y_peer, core_peer = neighbours()
+    greet(plane_peers[1:])
     copies = []
 
     def push(source, side, dp, peer):
-        copy = pltpu.make_async_remote_copy(
-            src_ref=source, dst_ref=w_ref.at[side, dp], send_sem=send_sem.at[len(copies)],
-            recv_sem=recv_sem.at[side, dp], device_id=peer, device_id_type=pl.DeviceIdType.MESH,
-        )
+        copy = remote(source, w_ref.at[side, dp], send_sem.at[len(copies)], recv_sem.at[side, dp], peer)
         copy.start()
         copies.append(copy)
 
     def arrive(side, dp):
         slot = w_ref.at[side, dp]
-        pltpu.make_async_remote_copy(
-            src_ref=slot, dst_ref=slot, send_sem=send_sem.at[0], recv_sem=recv_sem.at[side, dp],
-            device_id=x_peer, device_id_type=pl.DeviceIdType.MESH,
-        ).wait_recv()
-
-    for peer in z_peers:
-        push(w_mine, 0, d, peer)
-    push(w_mine, 0, d, x_peer)
-    push(w_mine, 1, d, y_peer)
-    pair, last = dealt
+        remote(slot, slot, send_sem.at[0], recv_sem.at[side, dp], x_peer).wait_recv()
+
+    near = [k * 2 + x for k in range(planes)]
+    over = [k * 2 + 1 - x for k in range(planes)]
+    for k in range(planes):
+        push(line.at[k], 0, near[k], x_peer)
+        push(line.at[k], 1, near[k], y_peer)
     deals = deal_out(p, plane_peers, w_send, later, (pair.at[0], pair.at[1], last), deal_send, deal_recv)
     values = tokens[...].astype(f32)
     inverse = lax.rsqrt(jnp.mean(values * values, axis=1, keepdims=True) + epsilon)
     at = pl.ds(pl.multiple_of(core * half, half), half)
     rows_ref[at] = (values * inverse * gain[...]).astype(bf16)
-    row_copy = pltpu.make_async_remote_copy(
-        src_ref=rows_ref.at[at], dst_ref=rows_ref.at[at], send_sem=row_sem.at[0], recv_sem=row_sem.at[1],
-        device_id=core_peer, device_id_type=pl.DeviceIdType.MESH,
-    )
+    row_copy = remote(rows_ref.at[at], rows_ref.at[at], row_sem.at[0], row_sem.at[1], core_peer)
     row_copy.start()
-    w_ref[0, d] = w_mine[...]
     rank_rows(lengths, routes_t, half, ranks_ref)
-    rank_copy = pltpu.make_async_remote_copy(
-        src_ref=ranks_ref.at[0], dst_ref=ranks_ref.at[1], send_sem=row_sem.at[2], recv_sem=row_sem.at[3],
-        device_id=plane_peers[4], device_id_type=pl.DeviceIdType.MESH,
-    )
+    rank_copy = remote(ranks_ref.at[0], ranks_ref.at[1], row_sem.at[2], row_sem.at[3], x_peer)
     rank_copy.start()
-    near = [plane(dz) * 2 + x for dz in range(planes)]
-    over = [plane(dz) * 2 + 1 - x for dz in range(planes)]
-
-    def turn(dz):
-        arrive(0, over[dz])
-        if dz < planes // 2:
-            push(w_ref.at[0, over[dz]], 1, over[dz], y_peer)
-        arrive(1, near[dz])
-        if dz >= planes // 2:
-            push(w_ref.at[1, near[dz]], 1, near[dz], x_peer)
-
-    for dz in range(1, planes):
-        arrive(0, near[dz])
-        push(w_ref.at[0, near[dz]], 0, near[dz], x_peer)
-        push(w_ref.at[0, near[dz]], 1, near[dz], y_peer)
-        turn(dz - 1)
-    turn(planes - 1)
-    for dz in range(planes):
-        arrive(1, over[dz])
+    router_ref[...] = dot(group_rows_of(router.shape[1]), router[...], 1, 1).astype(bf16)
+    for k in range(planes):
+        w_ref[0, near[k]] = line[k]
+    for k in range(planes):
+        arrive(0, over[k])
+        if k < planes // 2:
+            push(w_ref.at[0, over[k]], 1, over[k], y_peer)
+        arrive(1, near[k])
+        if k >= planes // 2:
+            push(w_ref.at[1, near[k]], 1, near[k], x_peer)
+    for k in range(planes):
+        arrive(1, over[k])
     for copy in copies:
         copy.wait_send()
     row_copy.wait()
@@ -403,6 +392,39 @@
     )
 
 
+def live_rows(lengths, rows):
+    first = lax.axis_index("tensor") * rows
+    seq_len = 4 * rows // lengths.shape[0]
+    position = lax.rem(first, seq_len) + lax.broadcasted_iota(jnp.int32, (rows, 1), 0)
+    return (position < lengths[first // seq_len]).astype(f32)
+
+
+def z_steps(step, up_from, down_from, up_to, down_to, sem):
+    d, t = lax.axis_index("dp"), lax.axis_index("tensor")
+    planes = lax.axis_size("dp") // 2
+    z = d // 2
+    above = {"dp": lax.rem(z + 1, planes) * 2 + d % 2, "tensor": t}
+    below = {"dp": lax.rem(z + planes - 1, planes) * 2 + d % 2, "tensor": t}
+    up = remote(up_from, up_to, sem.at[0], sem.at[1], above)
+    down = remote(down_from, down_to, sem.at[2], sem.at[3], below)
+    steps = (
+        (up, (z >= step - 1) & (z < planes - 1), z >= step),
+        (down, (z > 0) & (z <= planes - step), z < planes - step),
+    )
+    return steps, above, below
+
+
+def start_steps(steps):
+    for copy, sends, _ in steps:
+        pl.when(sends)(copy.start)
+
+
+def settle_steps(steps):
+    for copy, sends, receives in steps:
+        pl.when(sends)(copy.wait_send)
+        pl.when(receives)(copy.wait_recv)
+
+
 def block_ranks(ranks, j):
     return ranks[j // 4, lax.axis_index("tensor") ^ (j % 4)].astype(f32)
 
@@ -417,13 +439,22 @@
 
 
 def mix_kernel(
-    local, cap, tokens, keep, send, live, gain, out_own, out_y, out_x, ranks, router_t,
-    hidden_ref, normed_ref, inv_ref, gates_ref, x_hbm, g_hbm,
-    normed_buf, out_buf, got_ref, stage_ref, ranks_ref, shares_ref,
-    send_sem, recv_sem, core_sem, stage_sem,
+    local, cap, carry, lengths, tokens, keep, send, gain, out_own, out_y, out_x, ranks, router_t, *refs
 ):
+    if carry:
+        moving, refs = refs[0], refs[1:]
+        (up_to, down_to), refs = refs[6:8], refs[:6] + refs[8:]
+    (
+        hidden_ref, normed_ref, inv_ref, gates_ref, x_hbm, g_hbm,
+        normed_buf, out_buf, got_ref, stage_ref, ranks_ref, shares_ref,
+        send_sem, recv_sem, core_sem, stage_sem, z_sem,
+    ) = refs
     x_peer, y_peer, core_peer = neighbours()
-    greet((x_peer, y_peer, core_peer))
+    if carry:
+        steps, above, below = z_steps(carry, moving, moving, up_to, down_to, z_sem)
+        greet((x_peer, y_peer, core_peer, above, below))
+    else:
+        greet((x_peer, y_peer, core_peer))
     rows = tokens.shape[0]
     low, high = pl.ds(0, rows // 2), pl.ds(rows // 2, rows // 2)
     sent = []
@@ -438,6 +469,8 @@
 
     core_copy = remote(send, got_ref, core_sem.at[0], core_sem.at[1], core_peer)
     core_copy.start()
+    if carry:
+        start_steps(steps)
     push(1, out_y.at[low], out_buf.at[6, low], 6, x_peer)
     push(1, out_x.at[high], out_buf.at[6, high], 8, y_peer)
     push(1, out_own, out_buf.at[1], 1, core_peer)
@@ -445,7 +478,7 @@
     push(1, out_x, out_buf.at[5], 5, core_peer)
     core_copy.wait()
     branch = keep[...].astype(f32) + got_ref[...].astype(f32)
-    hidden = tokens[...].astype(f32) + live[...] * branch
+    hidden = tokens[...].astype(f32) + live_rows(lengths, rows) * branch
     inverse = lax.rsqrt(jnp.mean(hidden * hidden, axis=1, keepdims=True) + epsilon)
     hidden_ref[...] = hidden
     inv_ref[...] = inverse
@@ -517,12 +550,14 @@
         copy.wait_send()
     for copy in staged[-2:]:
         copy.wait()
+    if carry:
+        settle_steps(steps)
 
 
 def return_kernel(local, cap, *refs):
     dxs, ys, refs = refs[:local], refs[local:2 * local], refs[2 * local:]
     (
-        ranks, normed, hidden_in, inv, out_grad, router, hits, live, gain,
+        lengths, ranks, normed, hidden_in, inv, out_grad, router, gain,
         grad_hidden_ref, branch_ref, router_grad_ref, gain_grad_ref, y_ref,
         load_ref, part_ref, core_ref, total_ref, diag_ref, last_ref, y_part, y_core, ranks_ref,
         load_sem, send_sem, recv_sem, y_send, y_recv, branch_sem,
@@ -625,7 +660,9 @@
         y_copies[3 - k].wait()
         y_ref[k ^ (own_place() // 2)] = (mine + y_core[k].astype(f32)).astype(bf16)
 
-    hit = hits[...] > 0.0
+    experts = router.shape[1]
+    hit_rows = (block_ranks(ranks, 0) >= 0.0).astype(f32).astype(bf16)
+    hit = dot(hit_rows, group_rows_of(experts), 0, 0) > 0.0
     shares = masked_shares(dot(normed[...], router[...], 1, 0), hit, 1)
     arrive(last_ref.at[0, low], 6)
     arrive(last_ref.at[1, high], 7)
@@ -640,7 +677,7 @@
             total_ref[3, :, cols].astype(f32) + last_ref[0, :, cols].astype(f32) + last_ref[1, :, cols].astype(f32)
         )
 
-    grad_shares = jnp.where(hit, summed(width, wide), 0.0)
+    grad_shares = jnp.where(hit, summed(width, wide)[:, :experts], 0.0)
     grad_chosen = shares * (grad_shares - jnp.sum(shares * grad_shares, axis=1, keepdims=True))
     top, rest = split16(grad_chosen)
     hidden, inverse = hidden_in[...], inv[...]
@@ -650,12 +687,11 @@
     grad_hidden = out_grad[...].astype(f32) + inverse * weighted - hidden * (inverse * inverse * inverse * centre)
     grad_hidden_ref[...] = grad_hidden
     at = pl.ds(pl.multiple_of(core * rows, rows), rows)
-    branch_ref[at] = (live[...] * grad_hidden).astype(bf16)
+    branch_ref[at] = (live_rows(lengths, rows) * grad_hidden).astype(bf16)
     branch_copy = remote(branch_ref.at[at], branch_ref.at[at], branch_sem.at[0], branch_sem.at[1], core_peer)
     branch_copy.start()
     gain_grad_ref[...] = jnp.sum(grad_mix * hidden * inverse, axis=0, keepdims=True)
-    experts = router_grad_ref.shape[0]
-    router_grad_ref[...] = (dot(top, normed[...], 0, 0) + dot(rest, normed[...], 0, 0))[:experts]
+    router_grad_ref[...] = dot(top, normed[...], 0, 0) + dot(rest, normed[...], 0, 0)
     branch_copy.wait()
 
 
@@ -673,36 +709,9 @@
     blocks = [(dp // 2, dp % 2 * 4) for dp in range(2 * members)]
     z = d // 2
     if carry:
-        above = {"dp": lax.rem(z + 1, members) * 2 + d % 2, "tensor": t}
-        below = {"dp": lax.rem(z + members - 1, members) * 2 + d % 2, "tensor": t}
+        steps_out, above, below = z_steps(carry, up_from, down_from, up_to, down_to, z_sem)
         greet((above, below))
-        up = remote(up_from, up_to, z_sem.at[0], z_sem.at[1], above)
-        down = remote(down_from, down_to, z_sem.at[2], z_sem.at[3], below)
-
-        @pl.when((z >= carry - 1) & (z < members - 1))
-        def _():
-            up.start()
-
-        @pl.when((z > 0) & (z <= members - carry))
-        def _():
-            down.start()
-
-    def settle():
-        @pl.when((z >= carry - 1) & (z < members - 1))
-        def _():
-            up.wait_send()
-
-        @pl.when(z >= carry)
-        def _():
-            up.wait_recv()
-
-        @pl.when((z > 0) & (z <= members - carry))
-        def _():
-            down.wait_send()
-
-        @pl.when(z < members - carry)
-        def _():
-            down.wait_recv()
+        start_steps(steps_out)
 
     def fetch(act):
         if not chained:
@@ -775,7 +784,7 @@
     for copy in outs:
         copy.wait()
     if carry:
-        settle()
+        settle_steps(steps_out)
 
 
 def all_peers(d, t, planes):
@@ -787,21 +796,43 @@
     return peers
 
 
+def push_back(p, plane_peers, sums, back_ref, send_sem, recv_sem):
+    copies = []
+    for e in range(2):
+        for j in (6, 7, 2, 4, 3, 5, 1):
+            copies.append(
+                remote(sums.at[e, p ^ j], back_ref.at[e, p], send_sem.at[e, j], recv_sem.at[e, j], plane_peers[j])
+            )
+        copies.append(pltpu.make_async_copy(sums.at[e, p], back_ref.at[e, p], send_sem.at[e, 0]))
+    for copy in copies:
+        copy.start()
+    return copies
+
+
+def settle_back(p, plane_peers, copies, back_ref, send_sem, recv_sem):
+    for e in range(2):
+        for n, j in enumerate((6, 7, 2, 4, 3, 5, 1)):
+            copies[8 * e + n].wait_send()
+            slot = back_ref.at[e, p ^ j]
+            remote(slot, slot, send_sem.at[e, j], recv_sem.at[e, j], plane_peers[1]).wait_recv()
+        copies[8 * e + 7].wait()
+
+
 def tail_kernel(
     tokens, keep, send, grad_hidden, gain, router_grad, gain_mix_grad, dw, sums,
-    out_ref, small_ref, grad_ref, back_ref,
-    got_ref, first_ref, second_ref, diag_ref, own_ref, far_ref, small_buf,
-    core_sem, send_sem, recv_sem, far_send, far_recv, small_send, small_recv, back_send, back_recv,
+    out_ref, router_ref, gains_ref, plane_ref, back_ref,
+    got_ref, first_ref, second_ref, diag_ref, own_ref, small_ref, small_buf, part_ref, part_buf, parts_ref,
+    core_sem, send_sem, recv_sem, small_send, small_recv, back_send, back_recv,
+    part_send, part_recv, parts_send, parts_recv,
 ):
     d, t = lax.axis_index("dp"), lax.axis_index("tensor")
     planes = dw.shape[1] // 2
     half = planes // 2
-    z, x = d // 2, d % 2
+    x = d % 2
     doubling = all_peers(d, t, planes)
     core_peer, y_peer, x_peer = doubling[:3]
-    z_peers = [{"dp": lax.rem(z + k, planes) * 2 + x, "tensor": t} for k in range(1, planes)]
     p, plane_peers = own_place(), plane_devices()
-    greet((*plane_peers[1:], *z_peers))
+    greet((*plane_peers[1:], *doubling[3:]))
     experts = router_grad.shape[0]
     sent = []
 
@@ -823,42 +854,31 @@
     for k in range(half):
         push(dw.at[0, over[k]], first_ref.at[k], 0, k, x_peer)
         push(dw.at[1, near[half + k]], second_ref.at[half + k], 1, half + k, y_peer)
-    backs = []
-    for e in range(2):
-        for j in (6, 7, 2, 4, 3, 5, 1):
-            backs.append(
-                remote(sums.at[e, p ^ j], back_ref.at[e, p], back_send.at[e, j], back_recv.at[e, j], plane_peers[j])
-            )
-        backs.append(pltpu.make_async_copy(sums.at[e, p], back_ref.at[e, p], back_send.at[e, 0]))
-    for copy in backs:
-        copy.start()
-
     core_copy.wait()
     source = tokens[...].astype(f32)
     inverse = lax.rsqrt(jnp.mean(source * source, axis=1, keepdims=True) + epsilon)
     grad = keep[...].astype(f32) + got_ref[...].astype(f32)
+    gain_grad = jnp.sum(grad * source * inverse, axis=0, keepdims=True)
     small_ref[:experts] = router_grad[...]
-    small_ref[experts:experts + 1] = gain_mix_grad[...]
-    small_ref[experts + 1:experts + 2] = jnp.sum(grad * source * inverse, axis=0, keepdims=True)
-    small_ref[experts + 2:] = jnp.zeros_like(small_ref[experts + 2:])
-    small_copies = []
+    row = lax.broadcasted_iota(jnp.int32, (8, small_ref.shape[1]), 0)
+    small_ref[experts:] = jnp.where(row == 0, gain_mix_grad[...], jnp.where(row == 1, gain_grad, 0.0))
 
     def small_start(n):
         copy = remote(small_ref, small_buf.at[n], small_send.at[n], small_recv.at[n], doubling[n])
         copy.start()
-        small_copies.append(copy)
-
-    def small_end(n):
-        small_copies[n].wait()
+        return copy
+
+    def small_end(n, copy):
+        copy.wait()
         small_ref[...] = small_ref[...] + small_buf[n]
 
-    small_start(0)
+    running = small_start(0)
     weighted = grad * gain[...]
     centre = jnp.mean(source * weighted, axis=1, keepdims=True)
     total = grad_hidden[...] + inverse * weighted - source * (inverse * inverse * inverse * centre)
     out_ref[...] = total.astype(bf16)
-    small_end(0)
-    small_start(1)
+    small_end(0, running)
+    running = small_start(1)
     for k in range(half):
         arrive(diag_ref.at[k], 2, k)
         own_ref[k] = (dw[1, near[k]].astype(f32) + diag_ref[k].astype(f32)).astype(bf16)
@@ -866,38 +886,89 @@
         arrive(diag_ref.at[half + k], 2, half + k)
         own_ref[half + k] = (dw[0, over[half + k]].astype(f32) + diag_ref[half + k].astype(f32)).astype(bf16)
         push(own_ref.at[half + k], first_ref.at[half + k], 0, half + k, x_peer)
-    small_end(1)
-    small_start(2)
+    small_end(1, running)
+    running = small_start(2)
+    backs = push_back(p, plane_peers, sums, back_ref, back_send, back_recv)
     for copy in sent:
         copy.wait_send()
     for k in range(planes):
         arrive(first_ref.at[k], 0, k)
         arrive(second_ref.at[k], 1, k)
-        own_ref[k] = (
+        plane_ref[k] = (
             dw[0, near[k]].astype(f32) + first_ref[k].astype(f32) + second_ref[k].astype(f32)
         ).astype(bf16)
+    small_end(2, running)
+    cols = small_ref.shape[1] // 8
+    part_ref[...] = small_ref[:, pl.ds(pl.multiple_of(p * cols, cols), cols)]
+    for n, peer in enumerate(doubling[3:]):
+        copy = remote(part_ref, part_buf.at[n], part_send.at[n], part_recv.at[n], peer)
+        copy.start()
+        copy.wait()
+        part_ref[...] = part_ref[...] + part_buf[n]
+    spread = []
+    for j in range(1, 8):
+        copy = remote(part_ref, parts_ref.at[p], parts_send.at[j], parts_recv.at[j], plane_peers[j])
+        copy.start()
+        spread.append(copy)
+    parts_ref[p] = part_ref[...]
+    settle_back(p, plane_peers, backs, back_ref, back_send, back_recv)
+    for j in range(1, 8):
+        spread[j - 1].wait_send()
+        slot = parts_ref.at[p ^ j]
+        remote(slot, slot, parts_send.at[j], parts_recv.at[j], plane_peers[1]).wait_recv()
+    for q in range(8):
+        router_ref[q * cols:(q + 1) * cols] = parts_ref[q, :experts].T
+        gains_ref[:, q * cols:(q + 1) * cols] = parts_ref[q, experts:]
+
+
+def last_kernel(
+    plane, back_first, sums, query_ref, keyval_ref, wo_ref, gate_ref, up_ref, down_ref,
+    back_ref, far_ref, far_send, far_recv, back_send, back_recv,
+):
+    d, t = lax.axis_index("dp"), lax.axis_index("tensor")
+    planes = plane.shape[0]
+    z, x = d // 2, d % 2
+    z_peers = [{"dp": lax.rem(z + k, planes) * 2 + x, "tensor": t} for k in range(1, planes)]
+    p, plane_peers = own_place(), plane_devices()
+    greet((*plane_peers[1:], *z_peers))
     far = []
     for k, peer in enumerate(z_peers):
-        copy = remote(
-            own_ref.at[lax.rem(z + k + 1, planes)], far_ref.at[k], far_send.at[k], far_recv.at[k], peer
-        )
+        copy = remote(plane.at[lax.rem(z + k + 1, planes)], far_ref.at[k], far_send.at[k], far_recv.at[k], peer)
         copy.start()
         far.append(copy)
-    small_end(2)
-    for n in range(3, len(doubling)):
-        small_start(n)
-        small_end(n)
-    mine = own_ref[z].astype(f32)
+    backs = push_back(p, plane_peers, sums, back_ref, back_send, back_recv)
+    outs = (gate_ref, up_ref, down_ref)
+    deep = back_first.shape[3]
+    experts = gate_ref.shape[0] // deep
+
+    def assemble(source, first, e, q):
+        rows = pl.ds(q * (experts // 8) + first + e, deep, stride=experts)
+        for which, out in enumerate(outs):
+            out[rows, :] = source[e, q, which].astype(f32)
+
+    for q in range(8):
+        for e in range(2):
+            assemble(back_first, 0, e, q)
+    for e in range(2):
+        backs[8 * e + 7].wait()
+        assemble(back_ref, 2, e, p)
+    for j in (1, 2, 4, 3, 5, 6, 7):
+        for e in range(2):
+            slot = back_ref.at[e, p ^ j]
+            remote(slot, slot, back_send.at[e, j], back_recv.at[e, j], plane_peers[1]).wait_recv()
+            assemble(back_ref, 2, e, p ^ j)
+    for e in range(2):
+        for n in range(7):
+            backs[8 * e + n].wait_send()
+    mine = plane[z].astype(f32)
     for k, copy in enumerate(far):
         copy.wait()
         mine += far_ref[k].astype(f32)
-    grad_ref[...] = mine
-    for e in range(2):
-        for n, j in enumerate((6, 7, 2, 4, 3, 5, 1)):
-            backs[8 * e + n].wait_send()
-            slot = back_ref.at[e, p ^ j]
-            remote(slot, slot, back_send.at[e, j], back_recv.at[e, j], x_peer).wait_recv()
-        backs[8 * e + 7].wait()
+    qw, kvw = query_ref.shape[1], keyval_ref.shape[2]
+    query_ref[...] = mine[:, :qw]
+    keyval_ref[:, 0] = mine[:, qw:qw + kvw]
+    keyval_ref[:, 1] = mine[:, qw + kvw:qw + 2 * kvw]
+    wo_ref[...] = mine[:, qw + 2 * kvw:]
 
 
 def shards(
@@ -945,28 +1016,30 @@
     q_cols, kv_cols = w_query.shape[1], w_keyvalue.shape[2]
     cut = q_cols + 2 * kv_cols
     w_mine = jnp.concatenate([w_query, w_keyvalue[:, 0], w_keyvalue[:, 1], w_out], axis=1)
-    pushes = 3 * planes + 2 * (planes - 1)
+    pushes = 3 * planes
     hbm = pl.BlockSpec(memory_space=pl.ANY)
     dealt_shape = sds((8, 3, deep, quarter), bf16)
-    early = 1
-    dealt_early = pl.pallas_call(
+    dma = pltpu.SemaphoreType.DMA
+    line_shape = sds((planes, deep, cut + q_cols), bf16)
+    dealt_first, line = pl.pallas_call(
         deal_kernel,
-        out_shape=[dealt_shape] * early,
-        in_specs=[hbm], out_specs=[hbm] * early,
-        scratch_shapes=[pltpu.SemaphoreType.DMA((early, 8)), pltpu.SemaphoreType.DMA((early, 8))],
+        out_shape=[dealt_shape, line_shape],
+        in_specs=[hbm, VM], out_specs=[hbm, VM],
+        scratch_shapes=[dma((1, 8)), dma((1, 8)), dma((planes,)), dma((planes,))],
         compiler_params=pltpu.CompilerParams(
             vmem_limit_bytes=VMEM_LIMIT, collective_id=1, has_side_effects=True
         ),
         cost_estimate=pl.CostEstimate(flops=10**6, bytes_accessed=20 * 2**20, transcendentals=0),
-    )(w_send)
-    later = tuple(range(early, local))
-    normed_rows, w_attn, ranks, dealt_pair, dealt_last = pl.pallas_call(
+    )(w_send, w_mine)
+    later = tuple(range(1, local))
+    normed_rows, w_attn, ranks, router_t, dealt_pair, dealt_last = pl.pallas_call(
         functools.partial(gather_kernel, later),
         out_shape=[
             sds((2 * rows, width), bf16), sds((2, nd, deep, cut + q_cols), bf16), sds((2, nt, 64, rows), bf16),
+            sds((64, width), bf16),
         ]
         + [sds((2,) + dealt_shape.shape, bf16), dealt_shape],
-        in_specs=[SM] + [VM] * 4 + [hbm], out_specs=[VM] * 3 + [hbm] * 2,
+        in_specs=[SM] + [VM] * 5 + [hbm], out_specs=[VM] * 4 + [hbm] * 2,
         scratch_shapes=[
             pltpu.SemaphoreType.DMA((pushes,)), pltpu.SemaphoreType.DMA((2, nd)), pltpu.SemaphoreType.DMA((4,)),
             pltpu.SemaphoreType.DMA((len(later), 8)), pltpu.SemaphoreType.DMA((len(later), 8)),
@@ -975,32 +1048,18 @@
             vmem_limit_bytes=VMEM_LIMIT, collective_id=0, has_side_effects=True
         ),
         cost_estimate=pl.CostEstimate(flops=10**7, bytes_accessed=100 * 2**20, transcendentals=0),
-    )(lengths, tokens, gain_attn[None, :], routes.T, after(w_mine, *dealt_early), w_send)
-
-    w_first = gather_weights(dealt_early[0], with_place)
+    )(lengths, tokens, gain_attn[None, :], routes.T, w_router, line, w_send)
+
+    w_first = gather_weights(dealt_first, with_place)
     w_pair = gather_weights(dealt_pair, with_place)
     by_steps = members == local == 4
     w_last = dealt_last if by_steps else gather_weights(dealt_last, with_place)
 
-    positions = jnp.arange(group_rows, dtype=jnp.int32) % seq_len
-    live = positions < jnp.repeat(lengths, seq_len)
-    own_start = t_id * rows
-    live_own = lax.dynamic_slice_in_dim(live, own_start, rows, 0).astype(f32)[:, None]
-    routes_own = lax.dynamic_slice_in_dim(routes, own_start, rows, 0)
-    lane_ids = jnp.arange(LANES, dtype=jnp.int32)
-    hits_own = jnp.any(routes_own[:, :, None] == lane_ids[None, None, :], axis=1).astype(f32) * live_own
-    router = jnp.pad(w_router, ((0, 0), (0, LANES - experts)))
-    router_t = jnp.pad(w_router.T.reshape(8, local, width), ((0, 0), (0, 8 - local), (0, 0))).reshape(64, width)
-
-    half_head = HD // 2
-    exponent = 2.0 * jnp.arange(half_head, dtype=f32) / HD
-    angles = jnp.arange(seq_len, dtype=f32)[:, None] * jnp.exp(-math.log(rope_base) * exponent)[None, :]
-    cosine, sine = jnp.cos(angles), jnp.sin(angles)
-    cos_table = jnp.concatenate([cosine] * 4, axis=1)
-    sin_table = jnp.concatenate([-sine, sine] * 2, axis=1)
-
-    length = lax.dynamic_slice_in_dim(lengths, own_start // seq_len, 1, 0)[0]
-    where_attn = jnp.stack([core, length]).astype(jnp.int32)
+    exponent = 2.0 * np.arange(HD // 2) / HD
+    angles = np.arange(seq_len)[:, None] * np.exp(-math.log(rope_base) * exponent)[None, :]
+    cosine, sine = np.cos(angles).astype(np.float32), np.sin(angles).astype(np.float32)
+    cos_table = jnp.asarray(np.concatenate([cosine] * 4, axis=1))
+    sin_table = jnp.asarray(np.concatenate([-sine, sine] * 2, axis=1))
 
     out_late = after(out_grad, w_attn)
     out_y, out_x = hop_y(out_late), hop_x(out_late)
@@ -1015,7 +1074,7 @@
         ],
         12 * 10**9, 16 * 2**20,
         in_specs=[SM] + [VM] * 4, out_specs=[VM] * 7,
-    )(where_attn, normed_rows, w_attn, cos_table, sin_table)
+    )(lengths, normed_rows, w_attn, cos_table, sin_table)
 
     def remote_call(kernel, number, out_shape, flops, nbytes, **kw):
         return pl.pallas_call(
@@ -1027,31 +1086,30 @@
             **kw,
         )
 
-    dma = pltpu.SemaphoreType.DMA
     slots_shape = (local, 8, cap, width)
-    hidden_own, normed_mix, inverse_mix, gates_in, rows_in, grads_in = remote_call(
-        functools.partial(mix_kernel, local, cap), 2,
+    hidden_own, normed_mix, inverse_mix, gates_in, rows_in, grads_in, *moving = remote_call(
+        functools.partial(mix_kernel, local, cap, int(by_steps)), 2,
         [
             sds((rows, width), f32), sds((rows, width), bf16), sds((rows, 1), f32),
             sds((local, 8, cap, 1), f32), sds(slots_shape, bf16), sds(slots_shape, bf16),
-        ],
+        ] + [dealt_shape] * (2 * by_steps),
         10**10, 100 * 2**20,
-        in_specs=[VM] * 10, out_specs=[VM] * 4 + [hbm] * 2,
+        in_specs=[SM] + [VM] * 9 + [hbm] * by_steps, out_specs=[VM] * 4 + [hbm] * (2 + 2 * by_steps),
         scratch_shapes=[
             pltpu.VMEM((8, rows, width), bf16), pltpu.VMEM((8, rows, width), bf16), pltpu.VMEM((rows, width), bf16),
             pltpu.VMEM((2, local, cap, width), bf16), pltpu.VMEM((64, rows), f32), pltpu.VMEM((64, rows), f32),
-            dma((2, 9)), dma((2, 9)), dma((2,)), dma((2,)),
+            dma((2, 9)), dma((2, 9)), dma((2,)), dma((2,)), dma((4,)),
         ],
     )(
-        tokens, after(keep, w_first), send, live_own, gain_mixer[None, :], out_grad, out_y, out_x, ranks, router_t
+        lengths, tokens, after(keep, w_first), send, gain_mixer[None, :], out_grad, out_y, out_x, ranks, router_t,
+        *([dealt_last] if by_steps else []),
     )
     ys, dxs, dw_pairs = [], [], []
-    moving = (dealt_last, dealt_last)
-    arrived = (w_last,)
+    arrived = (w_last, *moving)
     pair_shape = sds((members, 2, 8, 3, deep, quarter), bf16)
     before = []
     for e in range(local):
-        step = e + 1 if by_steps and e < local - 1 else 0
+        step = e + 2 if by_steps and e + 2 < members else 0
         sources = ((w_first,), (w_pair,), (w_pair,), arrived)[e]
         inputs = [after(rows_in, *before), grads_in, gates_in, *sources, *(moving if step else ())]
         aliases = {}
@@ -1094,7 +1152,7 @@
             sds((4, rows, width), bf16),
         ],
         10**10, 100 * 2**20,
-        in_specs=[hbm] * (2 * local) + [VM] * 9, out_specs=[VM] * 5,
+        in_specs=[hbm] * (2 * local) + [SM] + [VM] * 7, out_specs=[VM] * 5,
         scratch_shapes=[
             pltpu.VMEM((3, local * cap, wide), bf16),
             pltpu.VMEM((4, rows, wide), bf16), pltpu.VMEM((4, rows, wide), bf16), pltpu.VMEM((4, rows, wide), bf16),
@@ -1103,8 +1161,7 @@
             dma((3, local)), dma((10,)), dma((10,)), dma((4,)), dma((4,)), dma((2,)),
         ],
     )(
-        *dxs, *ys, ranks, normed_mix, hidden_own, inverse_mix, out_grad, router, hits_own, live_own,
-        gain_mixer[None, :],
+        *dxs, *ys, lengths, ranks, normed_mix, hidden_own, inverse_mix, out_grad, w_router, gain_mixer[None, :],
     )
     chip_groups = [
         [with_place[side][a] * nt + y * 2 + c for side in range(2) for y in range(2)]
@@ -1125,57 +1182,65 @@
             pltpu.VMEM((seq_len, LANES), f32), pltpu.VMEM((seq_len, LANES), f32),
         ],
     )(
-        where_attn, normed_rows, grad_branch, w_attn, cos_table, sin_table,
+        lengths, normed_rows, grad_branch, w_attn, cos_table, sin_table,
         q, k, v, ctx, lse,
     )
-    doublings = 2 + (nd - 1).bit_length()
     per_dp = (deep, cut + q_cols)
     sums = [
         lax.psum_scatter(dw, "dp", scatter_dimension=0, axis_index_groups=with_place) for dw in dw_pairs
     ]
-    grad_tokens, small, attn_grad, back_first = remote_call(
+    back_shape = sds((2, 8, 3, deep, quarter), bf16)
+    doublings = (nd - 1).bit_length() - 1
+    small_rows, part = experts + 8, width // 8
+    grad_tokens, grad_router, gains, plane_grad, back_first = remote_call(
         tail_kernel, 8,
         [
-            sds((rows, width), bf16), sds((experts + 8, width), f32), sds(per_dp, f32),
-            sds((2, 8, 3, deep, quarter), bf16),
+            sds((rows, width), bf16), sds((width, experts), f32), sds((8, width), f32),
+            sds((planes,) + per_dp, bf16), back_shape,
         ],
         10**8, 30 * 2**20,
-        in_specs=[VM] * 8 + [hbm], out_specs=[VM] * 3 + [hbm],
+        in_specs=[VM] * 8 + [hbm], out_specs=[VM] * 4 + [hbm],
         scratch_shapes=[pltpu.VMEM((rows, width), bf16)]
         + [pltpu.VMEM((planes,) + per_dp, bf16)] * 4
         + [
-            pltpu.VMEM((planes - 1,) + per_dp, bf16), pltpu.VMEM((doublings, experts + 8, width), f32),
-            dma((2,)), dma((3, planes)), dma((3, planes)), dma((planes - 1,)), dma((planes - 1,)),
-            dma((doublings,)), dma((doublings,)), dma((2, 8)), dma((2, 8)),
+            pltpu.VMEM((small_rows, width), f32), pltpu.VMEM((3, small_rows, width), f32),
+            pltpu.VMEM((small_rows, part), f32), pltpu.VMEM((doublings, small_rows, part), f32),
+            pltpu.VMEM((8, small_rows, part), f32),
+            dma((2,)), dma((3, planes)), dma((3, planes)), dma((3,)), dma((3,)), dma((2, 8)), dma((2, 8)),
+            dma((doublings,)), dma((doublings,)), dma((8,)), dma((8,)),
         ],
     )(
         after(tokens, y_terms), keep_back, send_back, grad_hidden, gain_attn[None, :], router_grad, gain_mix_grad,
         dw_attn, sums[0],
     )
-
-    back_last = lax.all_to_all(
-        after(sums[1], grad_tokens), BOTH, 1, 1, tiled=True, axis_index_groups=plane_groups
-    )
-
-    def to_owner(which):
-        parts = jnp.concatenate([back_first[:, :, which], back_last[:, :, which]], axis=0).astype(f32)
-        return jnp.transpose(parts, (2, 1, 0, 3)).reshape(deep, experts, quarter)
-
-    grad_query = attn_grad[:, :q_cols]
-    grad_keyval = attn_grad[:, q_cols:cut].reshape(deep, 2, kv_cols)
-    grad_out = attn_grad[:, cut:]
+    expert_grad = sds((deep * experts, quarter), f32)
+    grad_query, grad_keyval, grad_out, *expert_grads = remote_call(
+        last_kernel, 9,
+        [
+            sds((deep, q_cols), f32), sds((deep, 2, kv_cols), f32), sds((deep, q_cols), f32),
+            expert_grad, expert_grad, expert_grad,
+        ],
+        10**8, 30 * 2**20,
+        in_specs=[VM] * 2 + [hbm], out_specs=[VM] * 6,
+        scratch_shapes=[
+            pltpu.VMEM((2, 8, 3, deep, quarter), bf16), pltpu.VMEM((planes - 1,) + per_dp, bf16),
+            dma((planes - 1,)), dma((planes - 1,)), dma((2, 8)), dma((2, 8)),
+        ],
+    )(plane_grad, back_first, sums[1])
+    grad_gate, grad_up, grad_down = (g.reshape(deep, experts, quarter) for g in expert_grads)
+
     return (
         mixed,
         grad_tokens,
-        small[experts + 1],
+        gains[1],
         grad_query,
         grad_keyval,
         grad_out,
-        small[experts],
-        small[:experts].T,
-        to_owner(0),
-        to_owner(1),
-        to_owner(2),
+        gains[0],
+        grad_router,
+        grad_gate,
+        grad_up,
+        grad_down,
     )
 
 

time: 571 us -> 546 us (0.956)
  Pallas kernels: 471 us -> 455 us
  other arithmetic: 17.3 us -> 7.78 us
  waiting for transfers between devices: 28.6 us -> 37.7 us
    pallas_call x4, Pallas kernels: 145 us -> 108 us  [shards(): pl.pallas_call(functools.partial(expert_kernel, e, local, len(sources), s...]
    pallas_call x3 -> x4, Pallas kernels: 151 us -> 174 us  [the longest x1 63.3 us: shards(): remote_call(functools.partial(mix_kernel, local, cap, int(by_steps)), 2,...]
    all_to_all x1 -> x0, waiting for transfers between devices: 11 us -> none  [shards(): lax.all_to_all(after(sums[1], grad_tokens), BOTH, 1, 1, tiled=True, axis_...]
    reduce_scatter x2, waiting for transfers between devices: 0.02 us -> 9.36 us  [shards(): lax.psum_scatter(dw, 'dp', scatter_dimension=0, axis_index_groups=with_pl...]
    all_gather x2, waiting for transfers between devices: 0.02 us -> 7.39 us  [gather_weights(): return lax.all_gather(x, 'dp', axis_index_groups=weight_groups)]
    unnamed x39 -> x40, local copies, waits for them, and re-layouts: 12.5 us -> 16.2 us
  transfers between devices with their start and end apart: 8 -> 7, of which waited for: 2 -> 5; matrix products, arithmetic and copies ran while one was open for 4% -> 2% of each run, Pallas kernels for 77% -> 71%
where the time goes in v4:
time: 546 us; the launch traced here: 542 us
  Pallas kernels  455 us (83%)
  waiting for transfers between devices  37.7 us (7%)
  local copies, waits for them, and re-layouts  18.7 us (3%)
  between operations  14.5 us (3%)
  starting transfers between devices  7.94 us (1%)
  other arithmetic  7.78 us (1%)
    pallas_call x4, Pallas kernels, shards(): pl.pallas_call(functools.partial(expert_kernel, e, local, len(sources), s...  108 us
    pallas_call x1, Pallas kernels, shards(): pl.pallas_call(functools.partial(gather_kernel, later), out_shape=[sds((2...  64.5 us
    pallas_call x1, Pallas kernels, shards(): remote_call(functools.partial(mix_kernel, local, cap, int(by_steps)), 2,...  63.3 us
    pallas_call x1, Pallas kernels, shards(): remote_call(tail_kernel, 8, [sds((rows, width), bf16), sds((width, expert...  59.7 us
    pallas_call x1, Pallas kernels, shards(): remote_call(functools.partial(return_kernel, local, cap), 3, [sds((rows,...  58.5 us
    pallas_call x1, Pallas kernels, shards(): call(attend_back_kernel, [sds((2, nd, deep, cut + q_cols), bf16), sds((ro...  30.6 us
    pallas_call x1, Pallas kernels, shards(): remote_call(last_kernel, 9, [sds((deep, q_cols), f32), sds((deep, 2, kv_c...  28 us
    pallas_call x1, Pallas kernels, shards(): pl.pallas_call(deal_kernel, out_shape=[dealt_shape, line_shape], in_specs...  22.7 us
  transfers between devices with their start and end apart: 7, of which 5 were waited for; matrix products, arithmetic and copies ran while one was open for 2% of the time, Pallas kernels for 71%

profile of v4, /device:TPU:0, one launch (start us, length us, event | category | flops | bytes accessed | tf_op | source)
XLA Modules:
  0.0 542.0 jit_solution(4580459534173688337)
XLA Ops:
  7.2 0.0 all-gather.5.cloned.1.call-start
  7.2 1.1 fusion
  8.4 1.6 copy.36
  10.0 0.4 copy.37
  10.4 0.4 copy.38
  10.9 2.0 pad_maximum_fusion.w_send
  12.9 0.7 pad_maximum_fusion.1.w_mine
  13.6 22.7 %shard_map.230 = (bf16[8,3,128,128]{3,2,1,0:T(8,128)(2,1)}, bf16[4,128,768]{2,1,0:T(8,128)(2,1)}) custom-call(bf16[8,4,3,128,128]{4,3,2,1,0:T(8,128)(2,1)} %pad_maximum_fusion.w_send, bf16[128,768]{1,0:T(8,128)(2,1)} %pad_maximum_fusion.1.w_mine), custom_call_target="tpu_custom_call" | custom-call | flops 1000000 | bytes 20971520 | tf_op jit(solution)/shard_map/pallas_call | solution.py:1024
  36.3 0.0 all-gather.5.cloned.1.call-update
  36.3 0.0 all-gather.7.cloned.1.call-start
  36.4 0.8 copy.41.router.refs_14_
  37.2 64.5 %shard_map.231 = (bf16[1024,1024]{1,0:T(8,128)(2,1)}, bf16[2,8,128,768]{3,2,1,0:T(8,128)(2,1)}, bf16[2,4,64,512]{3,2,1,0:T(8,128)(2,1)}, bf16[64,1024]{1,0:T(8,1...) custom-call(s32[2]{0:T(128)} %lengths.7, bf16[512,1024]{1,0:T(8,128)(2,1)} %tokens.4, ...), custom_call_target="tpu_custom_call" | custom-call | flops 10000000 | bytes 104857600 | tf_op jit(solution)/shard_map/pallas_call | solution.py:1035
  101.8 0.0 all-gather.7.cloned.1.call-update
  101.8 0.5 reduce-scatter.3.cloned.1.call-start
  102.3 1.1 collective-permute-start.1
  103.5 0.9 collective-permute-start
  104.4 19.9 %shard_map.232 = (bf16[1024,512]{1,0:T(8,128)(2,1)}, bf16[1024,256]{1,0:T(8,128)(2,1)}, bf16[1024,256]{1,0:T(8,128)(2,1)}, bf16[1024,512]{1,0:T(8,128)(2,1)}, f3...) custom-call(s32[2]{0:T(128)} %lengths.7, bf16[1024,1024]{1,0:T(8,128)(2,1)} %get-tuple-element.76.rows, ...), custom_call_target="tpu_custom_call" | custom-call | flops 12000000000 | bytes 16777216 | tf_op jit(solution)/shard_map/pallas_call | solution.py:1068
  124.3 2.9 collective-permute-done.1.out_x
  127.2 0.8 collective-permute-done.out_y
  128.0 0.2 copy-done.12
  128.2 0.8 copy-done.13
  129.0 63.3 %shard_map.233 = (f32[512,1024]{1,0:T(8,128)}, bf16[512,1024]{1,0:T(8,128)(2,1)}, f32[512,1]{1,0:T(8,128)}, f32[4,8,144,1]{3,2,1,0:T(8,128)}, bf16[4,8,144,1024]...) custom-call(s32[2]{0:T(128)} %lengths.7, ...), custom_call_target="tpu_custom_call" | custom-call | flops 10000000000 | bytes 104857600 | tf_op jit(solution)/shard_map/pallas_call | solution.py:1090
  192.3 53.0 %shard_map.234 = (bf16[8,144,1024]{2,1,0:T(8,128)(2,1)}, bf16[8,144,1152]{2,1,0:T(8,128)(2,1)}, bf16[4,2,8,3,128,128]{5,4,3,2,1,0:T(8,128)(2,1)}, bf16[8,3,128,1...) custom-call(bf16[4,8,144,1024]{3,2,1,0:T(8,128)(2,1)} %get-tuple-element.104.x_hbm, ...), custom_call_target="tpu_custom_call" | custom-call | flops 10000000000 | bytes 20971520 | tf_op jit(solution)/shard_map/pallas_call | solution.py:1119
  245.4 7.4 %all-gather.7.cloned.1.call-done = bf16[8,8,3,128,128]{4,3,2,1,0:T(8,128)(2,1)} async-done(((bf16[2,8,3,128,128]{4,3,2,1,0:T(8,128)(2,1)}), bf16[8,8,3,128,128]{4,3,2,1,0:T(8,128)(2,1)}) %all-gather.7.cloned.1.call-update) | async-done | bytes 6291472 | tf_op jit(solution)/shard_map/all_gather | solution.py:70
  252.7 19.9 %shard_map.235 = (bf16[8,144,1024]{2,1,0:T(8,128)(2,1)}, bf16[8,144,1152]{2,1,0:T(8,128)(2,1)}, bf16[4,2,8,3,128,128]{5,4,3,2,1,0:T(8,128)(2,1)}, bf16[8,3,128,1...) custom-call(bf16[4,8,144,1024]{3,2,1,0:T(8,128)(2,1)} %get-tuple-element.104.x_hbm, ...), custom_call_target="tpu_custom_call", output_to_operand_aliasing={{2}: (6, {})} | custom-call | flops 10000000000 | bytes 20971520 | tf_op jit(solution)/shard_map/pallas_call | solution.py:1119
  272.7 0.0 reduce-scatter.3.cloned.1.call-update
  272.7 0.2 reduce-scatter.5.cloned.1.call-start
  272.9 17.4 %shard_map.236 = (bf16[8,144,1024]{2,1,0:T(8,128)(2,1)}, bf16[8,144,1152]{2,1,0:T(8,128)(2,1)}, bf16[4,2,8,3,128,128]{5,4,3,2,1,0:T(8,128)(2,1)}) custom-call(bf16[4,8,144,1024]{3,2,1,0:T(8,128)(2,1)} %get-tuple-element.104.x_hbm, bf16[4,8,144,1024]{3,2,1,0:T(8,128)(2,1)} %get-tuple-element.88.g_hbm, f32[4,8,144,1]{3,2,1,0:T(8,128)} %get-tuple-element.89.gates_hbm, ...), custom_call_target="tpu_custom_call" | custom-call | flops 10000000000 | bytes 20971520 | tf_op jit(solution)/shard_map/pallas_call | solution.py:1119
  290.3 17.8 %shard_map.237 = (bf16[8,144,1024]{2,1,0:T(8,128)(2,1)}, bf16[8,144,1152]{2,1,0:T(8,128)(2,1)}, bf16[4,2,8,3,128,128]{5,4,3,2,1,0:T(8,128)(2,1)}) custom-call(bf16[4,8,144,1024]{3,2,1,0:T(8,128)(2,1)} %get-tuple-element.104.x_hbm, bf16[4,8,144,1024]{3,2,1,0:T(8,128)(2,1)} %get-tuple-element.88.g_hbm, ...), custom_call_target="tpu_custom_call", output_to_operand_aliasing={{2}: (10, {})} | custom-call | flops 10000000000 | bytes 20971520 | tf_op jit(solution)/shard_map/pallas_call | solution.py:1119
  308.1 58.5 %shard_map.238 = (f32[512,1024]{1,0:T(8,128)}, bf16[1024,1024]{1,0:T(8,128)(2,1)}, f32[32,1024]{1,0:T(8,128)}, f32[1,1024]{1,0:T(1,128)}, bf16[4,512,1024]{2,1,0:T(8,128)(2,1)}) custom-call(bf16[8,144,1152]{2,1,0:T(8,128)(2,1)} %get-tuple-element.92.refs_0_, bf16[8,144,1152]{2,1,0:T(8,128)(2,1)} %get-tuple-element.99.refs_1_, ...), custom_call_target="tpu_custom_call" | custom-call | flops 10000000000 | bytes 104857600 | tf_op jit(solution)/shard_map/pallas_call | solution.py:1148
  366.6 5.1 all-to-all-start
  371.7 30.6 %shard_map.239 = (bf16[2,8,128,768]{3,2,1,0:T(8,128)(2,1)}, bf16[512,1024]{1,0:T(8,128)(2,1)}, bf16[512,1024]{1,0:T(8,128)(2,1)}) custom-call(s32[2]{0:T(128)} %lengths.7, bf16[1024,1024]{1,0:T(8,128)(2,1)} %get-tuple-element.76.rows, bf16[1024,1024]{1,0:T(8,128)(2,1)} %get-tuple-element.114.gb_ref, bf16[2,8,128,768]{3,2,1,0:T(8,128)(2,1)} %get-tuple-element.77.w, ...), custom_call_target="tpu_custom_call" | custom-call | flops 24999999488 | bytes 25165824 | tf_op jit(solution)/shard_map/pallas_call | solution.py:1173
  402.3 17.2 %all-to-all-done = bf16[4,512,1024]{2,1,0:T(8,128)(2,1)} async-done(((bf16[4,512,1024]{2,1,0:T(8,128)(2,1)}), bf16[4,512,1024]{2,1,0:T(8,128)(2,1)}, u32[]{:S(2)}, u32[]{:S(2)}) %all-to-all-start) | async-done | bytes 4194336 | tf_op jit(solution)/shard_map/all_to_all | solution.py:1170
  419.5 3.8 convert_reduce_fusion
  423.3 1.3 add_convert_fusion
  424.6 59.7 %shard_map.240 = (bf16[512,1024]{1,0:T(8,128)(2,1)}, f32[1024,32]{1,0:T(8,128)}, f32[8,1024]{1,0:T(8,128)}, bf16[4,128,768]{2,1,0:T(8,128)(2,1)}, bf16[2,8,3,128,128]{4,3,2,1,0:T(8,128)(2,1)}) custom-call(bf16[512,1024]{1,0:T(8,128)(2,1)} %tokens.4, bf16[512,1024]{1,0:T(8,128)(2,1)} %get-tuple-element.120.keep, bf16[512,1024]{1,0:T(8,128)(2,1)} %get-tuple-element.121.send, ...), custom_call_target="tpu_custom_call" | custom-call | flops 100000000 | bytes 31457280 | tf_op jit(solution)/shard_map/pallas_call | solution.py:1195
  484.3 2.0 copy.43
  486.3 1.4 fusion.1
  487.7 9.4 %reduce-scatter.5.cloned.1.call-done = bf16[1,2,8,3,128,128]{5,4,3,2,1,0:T(8,128)(2,1)} async-done(((bf16[4,2,8,3,128,128]{5,4,3,2,1,0:T(8,128)(2,1)}), bf16[1,2,8,3,128,128]{5,4,3,2,1,0:T(8,128)(2,1)}) %reduce-scatter.5.cloned.1.call-update) | async-done | bytes 1572880 | tf_op jit(solution)/shard_map/reduce_scatter | solution.py:1190
  497.1 28.0 %shard_map.241 = (f32[128,256]{1,0:T(8,128)}, f32[128,2,128]{2,1,0:T(2,128)}, f32[128,256]{1,0:T(8,128)}, f32[4096,128]{1,0:T(8,128)}, f32[4096,128]{1,0:T(8,128)}, /*index=5*/f32[4096,128]{1,0:T(8,128)}) custom-call(bf16[4,128,768]{2,1,0:T(8,128)(2,1)} %get-tuple-element.129.plane, bf16[2,8,3,128,128]{4,3,2,1,0:T(8,128)(2,1)} %get-tuple-element.130.back_first, ...), custom_call_target="tpu_custom_call" | custom-call | flops 100000000 | bytes 31457280 | tf_op jit(solution)/shard_map/pallas_call | solution.py:1217
  525.1 1.0 copy.57
  526.1 1.7 copy.58
  527.8 1.6 copy.59
  529.3 0.7 copy.60
  530.0 1.3 copy.61
  531.3 1.3 copy.62
  532.6 1.0 copy-done.1
  533.7 1.3 copy.63
  (29 shorter events, 0.1 us)
Async XLA Ops:
  7.2 2.8 copy-start.4
  7.2 3.3 copy-start.5
  7.2 117.1 %all-gather.5.cloned.1.call-start = ((), (), s32[]{:S(2)}) async-start(), calls=%async_computation.5 | async-start | bytes 3932160 | tf_op jit(solution)/shard_map/all_gather | solution.py:70
  10.9 2.0 copy-start.9
  10.9 2.0 copy-start.10
  12.9 23.5 %copy-start.8 = (bf16[1024,32]{0,1:T(8,128)(2,1)S(1)}, bf16[1024,32]{0,1:T(8,128)(2,1)}, u32[]{:S(2)}) copy-start(bf16[1024,32]{0,1:T(8,128)(2,1)} %param.23) | copy-start | bytes 196612
  36.3 216.4 %all-gather.7.cloned.1.call-start = ((), (), s32[]{:S(2)}) async-start(), calls=%async_computation.6 | async-start | bytes 7864320 | tf_op jit(solution)/shard_map/all_gather | solution.py:70
  37.2 65.1 %copy-start.11 = (bf16[512,1024]{1,0:T(8,128)(2,1)S(1)}, bf16[512,1024]{1,0:T(8,128)(2,1)}, u32[]{:S(2)}) copy-start(bf16[512,1024]{1,0:T(8,128)(2,1)} %refs_13_.1) | copy-start | bytes 3145732
  101.8 322.8 %reduce-scatter.3.cloned.1.call-start = ((), (), s32[]{:S(2)}) async-start(), calls=%async_computation.3 | async-start | bytes 7864320 | tf_op jit(solution)/shard_map/reduce_scatter | solution.py:1190
  102.3 24.9 %collective-permute-start.1 = (bf16[512,1024]{1,0:T(8,128)(2,1)S(1)}, bf16[512,1024]{1,0:T(8,128)(2,1)S(1)}, u32[]{:S(2)}, u32[]{:S(2)}) collective-permute-start(bf16[512,1024]{1,0:T(8,128)(2,1)S(1)} %copy-done.11), channel_id=1, source_target_pairs={{0,4},{1,5},{2,6},{3,7},{4,0},{5,1},{6,2},{7,3},{8,12},{9,13},{10,... | collective-permute-start | bytes 3145736 | tf_op jit(solution)/shard_map/ppermute | solution.py:50
  103.5 24.5 %collective-permute-start = (bf16[512,1024]{1,0:T(8,128)(2,1)S(1)}, bf16[512,1024]{1,0:T(8,128)(2,1)S(1)}, u32[]{:S(2)}, u32[]{:S(2)}) collective-permute-start(bf16[512,1024]{1,0:T(8,128)(2,1)S(1)} %copy-done.11), channel_id=1, source_target_pairs={{0,2},{1,3},{2,0},{3,1},{4,6},{5,7},{6,4},{7,5},{8,10},{9,11},{10,... | collective-permute-start | bytes 3145736 | tf_op jit(solution)/shard_map/ppermute | solution.py:50
  127.2 1.0 copy-start.12
  128.0 1.0 copy-start.13
  272.7 224.4 %reduce-scatter.5.cloned.1.call-start = ((), (), s32[]{:S(2)}) async-start(), calls=%async_computation.4 | async-start | bytes 7864320 | tf_op jit(solution)/shard_map/reduce_scatter | solution.py:1190
  366.6 52.9 %all-to-all-start = ((bf16[4,512,1024]{2,1,0:T(8,128)(2,1)}), bf16[4,512,1024]{2,1,0:T(8,128)(2,1)}, u32[]{:S(2)}, u32[]{:S(2)}) async-start(bf16[4,512,1024]{2,1,0:T(8,128)(2,1)} %get-tuple-element.112), calls=%async_computation | async-start | bytes 8388608 | tf_op jit(solution)/shard_map/all_to_all | solution.py:1170
  402.3 21.0 %copy-start = (f32[512,1024]{1,0:T(8,128)S(1)}, f32[512,1024]{1,0:T(8,128)}, u32[]{:S(2)}) copy-start(f32[512,1024]{1,0:T(8,128)} %get-tuple-element.86.refs_11_) | copy-start | bytes 6291460
  484.3 40.8 %copy-start.6 = (bf16[512,1024]{1,0:T(8,128)(2,1)S(1)}, bf16[512,1024]{1,0:T(8,128)(2,1)}, u32[]{:S(2)}) copy-start(bf16[512,1024]{1,0:T(8,128)(2,1)} %get-tuple-element.179) | copy-start | bytes 3145732
  525.0 4.3 copy-start.7
  525.1 4.9 copy-start.3
  526.1 5.3 copy-start.2
  531.3 2.3 copy-start.1
Sparse Core Ops, SparseCore 0:
  36.4 65.7 all-gather.4
  103.8 148.9 all-gather.6
  272.8 109.8 reduce-scatter.2
  384.9 112.1 reduce-scatter.4

commit v5 on v4

--- a/solution.py
+++ b/solution.py
@@ -255,7 +255,7 @@
 
 
 def deal_kernel(w_send, w_mine, *refs):
-    dealt, (line_ref, send_sem, recv_sem, line_send, line_recv) = refs[:-5], refs[-5:]
+    pair, line_ref, send_sem, recv_sem, line_send, line_recv = refs
     d, t = lax.axis_index("dp"), lax.axis_index("tensor")
     planes = line_ref.shape[0]
     z, x = d // 2, d % 2
@@ -263,12 +263,12 @@
     peers = plane_devices()
     z_peers = [{"dp": lax.rem(z + k, planes) * 2 + x, "tensor": t} for k in range(1, planes)]
     greet((*peers[1:], *z_peers))
-    copies = deal_out(p, peers, w_send, range(len(dealt)), dealt, send_sem, recv_sem)
     lines = []
     for k, peer in enumerate(z_peers):
         copy = remote(w_mine, line_ref.at[z], line_send.at[k], line_recv.at[z], peer)
         copy.start()
         lines.append(copy)
+    copies = deal_out(p, peers, w_send, (0, 1), (pair.at[0], pair.at[1]), send_sem, recv_sem)
     line_ref[z] = w_mine[...]
     for copy in copies:
         copy.wait()
@@ -308,7 +308,7 @@
 def gather_kernel(
     later, lengths, tokens, gain, routes_t, router, line, w_send, rows_ref, w_ref, ranks_ref, router_ref, *refs
 ):
-    (pair, last), (send_sem, recv_sem, row_sem, deal_send, deal_recv) = refs[:-5], refs[-5:]
+    dealt, (send_sem, recv_sem, row_sem, deal_send, deal_recv) = refs[:-5], refs[-5:]
     planes = line.shape[0]
     half = tokens.shape[0]
     x, core = lax.axis_index("dp") % 2, lax.axis_index("tensor") % 2
@@ -331,7 +331,7 @@
     for k in range(planes):
         push(line.at[k], 0, near[k], x_peer)
         push(line.at[k], 1, near[k], y_peer)
-    deals = deal_out(p, plane_peers, w_send, later, (pair.at[0], pair.at[1], last), deal_send, deal_recv)
+    deals = deal_out(p, plane_peers, w_send, later, dealt, deal_send, deal_recv)
     values = tokens[...].astype(f32)
     inverse = lax.rsqrt(jnp.mean(values * values, axis=1, keepdims=True) + epsilon)
     at = pl.ds(pl.multiple_of(core * half, half), half)
@@ -715,7 +715,7 @@
 
     def fetch(act):
         if not chained:
-            source = sources[0] if expert in (0, local - 1) else sources[0].at[:, expert - 1]
+            source = sources[0].at[:, expert] if expert < 2 else sources[0]
             act(pltpu.make_async_copy(source, w_buf, w_sem.at[0]))
             return
         act(pltpu.make_async_copy(sources[0], w_buf.at[z], w_sem.at[0]))
@@ -1021,24 +1021,24 @@
     dealt_shape = sds((8, 3, deep, quarter), bf16)
     dma = pltpu.SemaphoreType.DMA
     line_shape = sds((planes, deep, cut + q_cols), bf16)
-    dealt_first, line = pl.pallas_call(
+    dealt_pair, line = pl.pallas_call(
         deal_kernel,
-        out_shape=[dealt_shape, line_shape],
+        out_shape=[sds((2,) + dealt_shape.shape, bf16), line_shape],
         in_specs=[hbm, VM], out_specs=[hbm, VM],
-        scratch_shapes=[dma((1, 8)), dma((1, 8)), dma((planes,)), dma((planes,))],
+        scratch_shapes=[dma((2, 8)), dma((2, 8)), dma((planes,)), dma((planes,))],
         compiler_params=pltpu.CompilerParams(
             vmem_limit_bytes=VMEM_LIMIT, collective_id=1, has_side_effects=True
         ),
         cost_estimate=pl.CostEstimate(flops=10**6, bytes_accessed=20 * 2**20, transcendentals=0),
     )(w_send, w_mine)
-    later = tuple(range(1, local))
-    normed_rows, w_attn, ranks, router_t, dealt_pair, dealt_last = pl.pallas_call(
+    later = tuple(range(2, local))
+    normed_rows, w_attn, ranks, router_t, dealt_third, dealt_last = pl.pallas_call(
         functools.partial(gather_kernel, later),
         out_shape=[
             sds((2 * rows, width), bf16), sds((2, nd, deep, cut + q_cols), bf16), sds((2, nt, 64, rows), bf16),
             sds((64, width), bf16),
         ]
-        + [sds((2,) + dealt_shape.shape, bf16), dealt_shape],
+        + [dealt_shape] * 2,
         in_specs=[SM] + [VM] * 5 + [hbm], out_specs=[VM] * 4 + [hbm] * 2,
         scratch_shapes=[
             pltpu.SemaphoreType.DMA((pushes,)), pltpu.SemaphoreType.DMA((2, nd)), pltpu.SemaphoreType.DMA((4,)),
@@ -1050,8 +1050,8 @@
         cost_estimate=pl.CostEstimate(flops=10**7, bytes_accessed=100 * 2**20, transcendentals=0),
     )(lengths, tokens, gain_attn[None, :], routes.T, w_router, line, w_send)
 
-    w_first = gather_weights(dealt_first, with_place)
     w_pair = gather_weights(dealt_pair, with_place)
+    w_third = gather_weights(dealt_third, with_place)
     by_steps = members == local == 4
     w_last = dealt_last if by_steps else gather_weights(dealt_last, with_place)
 
@@ -1101,7 +1101,7 @@
             dma((2, 9)), dma((2, 9)), dma((2,)), dma((2,)), dma((4,)),
         ],
     )(
-        lengths, tokens, after(keep, w_first), send, gain_mixer[None, :], out_grad, out_y, out_x, ranks, router_t,
+        lengths, tokens, keep, send, gain_mixer[None, :], out_grad, out_y, out_x, ranks, router_t,
         *([dealt_last] if by_steps else []),
     )
     ys, dxs, dw_pairs = [], [], []
@@ -1110,7 +1110,7 @@
     before = []
     for e in range(local):
         step = e + 2 if by_steps and e + 2 < members else 0
-        sources = ((w_first,), (w_pair,), (w_pair,), arrived)[e]
+        sources = ((w_pair,), (w_pair,), (w_third,), arrived)[e]
         inputs = [after(rows_in, *before), grads_in, gates_in, *sources, *(moving if step else ())]
         aliases = {}
         if e % 2:

time: 546 us -> 540 us (0.989)
  waiting for transfers between devices: 37.7 us -> 29.9 us
    pallas_call x4, Pallas kernels: 108 us -> 121 us  [shards(): pl.pallas_call(functools.partial(expert_kernel, e, local, len(sources), s...]
    all_gather x2, waiting for transfers between devices: 7.39 us -> 0.04 us  [gather_weights(): return lax.all_gather(x, 'dp', axis_index_groups=weight_groups)]
    pallas_call x1, Pallas kernels: 64.5 us -> 57.3 us  [shards(): pl.pallas_call(functools.partial(gather_kernel, later), out_shape=[sds((2...]
    pallas_call x1, Pallas kernels: 63.3 us -> 57.2 us  [shards(): remote_call(functools.partial(mix_kernel, local, cap, int(by_steps)), 2,...]
  transfers between devices with their start and end apart: 7 -> 7, of which waited for: 5 -> 4; matrix products, arithmetic and copies ran while one was open for 2% -> 2% of each run, Pallas kernels for 71% -> 75%
where the time goes in v5:
time: 540 us; the launch traced here: 536 us
  Pallas kernels  457 us (85%)
  waiting for transfers between devices  29.9 us (6%)
  local copies, waits for them, and re-layouts  18.7 us (3%)
  between operations  14.5 us (3%)
  starting transfers between devices  8.37 us (2%)
  other arithmetic  7.61 us (1%)
    pallas_call x4, Pallas kernels, shards(): pl.pallas_call(functools.partial(expert_kernel, e, local, len(sources), s...  121 us
    pallas_call x1, Pallas kernels, shards(): remote_call(functools.partial(return_kernel, local, cap), 3, [sds((rows,...  59.2 us
    pallas_call x1, Pallas kernels, shards(): remote_call(tail_kernel, 8, [sds((rows, width), bf16), sds((width, expert...  58.4 us
    pallas_call x1, Pallas kernels, shards(): pl.pallas_call(functools.partial(gather_kernel, later), out_shape=[sds((2...  57.3 us
    pallas_call x1, Pallas kernels, shards(): remote_call(functools.partial(mix_kernel, local, cap, int(by_steps)), 2,...  57.2 us
    pallas_call x1, Pallas kernels, shards(): call(attend_back_kernel, [sds((2, nd, deep, cut + q_cols), bf16), sds((ro...  30.6 us
    pallas_call x1, Pallas kernels, shards(): remote_call(last_kernel, 9, [sds((deep, q_cols), f32), sds((deep, 2, kv_c...  28 us
    pallas_call x1, Pallas kernels, shards(): pl.pallas_call(deal_kernel, out_shape=[sds((2,) + dealt_shape.shape, bf16...  25.3 us
  transfers between devices with their start and end apart: 7, of which 4 were waited for; matrix products, arithmetic and copies ran while one was open for 2% of the time, Pallas kernels for 75%

profile of v5, /device:TPU:0, one launch (start us, length us, event | category | flops | bytes accessed | tf_op | source)
XLA Modules:
  0.0 536.1 jit_solution(2076569287467869000)
XLA Ops:
  7.2 0.0 all-gather.5.cloned.1.call-start
  7.2 1.1 fusion
  8.4 1.6 copy.36
  10.0 0.4 copy.37
  10.4 0.4 copy.38
  10.9 2.0 pad_maximum_fusion.w_send
  12.9 0.7 pad_maximum_fusion.1.w_mine
  13.6 25.3 %shard_map.230 = (bf16[2,8,3,128,128]{4,3,2,1,0:T(8,128)(2,1)}, bf16[4,128,768]{2,1,0:T(8,128)(2,1)}) custom-call(bf16[8,4,3,128,128]{4,3,2,1,0:T(8,128)(2,1)} %pad_maximum_fusion.w_send, bf16[128,768]{1,0:T(8,128)(2,1)} %pad_maximum_fusion.1.w_mine), custom_call_target="tpu_custom_call" | custom-call | flops 1000000 | bytes 20971520 | tf_op jit(solution)/shard_map/pallas_call | solution.py:1024
  38.9 0.0 all-gather.5.cloned.1.call-update
  38.9 0.0 all-gather.7.cloned.1.call-start
  39.0 0.8 copy.41.router.refs_14_
  39.8 57.3 %shard_map.231 = (bf16[1024,1024]{1,0:T(8,128)(2,1)}, bf16[2,8,128,768]{3,2,1,0:T(8,128)(2,1)}, bf16[2,4,64,512]{3,2,1,0:T(8,128)(2,1)}, bf16[64,1024]{1,0:T(8,1...) custom-call(s32[2]{0:T(128)} %lengths.7, bf16[512,1024]{1,0:T(8,128)(2,1)} %tokens.4, ...), custom_call_target="tpu_custom_call" | custom-call | flops 10000000 | bytes 104857600 | tf_op jit(solution)/shard_map/pallas_call | solution.py:1035
  97.2 0.5 reduce-scatter.3.cloned.1.call-start
  97.7 1.0 collective-permute-start.1
  98.7 1.5 collective-permute-start
  100.2 19.9 %shard_map.232 = (bf16[1024,512]{1,0:T(8,128)(2,1)}, bf16[1024,256]{1,0:T(8,128)(2,1)}, bf16[1024,256]{1,0:T(8,128)(2,1)}, bf16[1024,512]{1,0:T(8,128)(2,1)}, f3...) custom-call(s32[2]{0:T(128)} %lengths.7, bf16[1024,1024]{1,0:T(8,128)(2,1)} %get-tuple-element.75.rows, ...), custom_call_target="tpu_custom_call" | custom-call | flops 12000000000 | bytes 16777216 | tf_op jit(solution)/shard_map/pallas_call | solution.py:1068
  120.1 2.4 collective-permute-done.1.out_x
  122.5 0.7 collective-permute-done.out_y
  123.3 0.2 copy-done.12
  123.5 0.7 copy-done.13
  124.2 57.2 %shard_map.233 = (f32[512,1024]{1,0:T(8,128)}, bf16[512,1024]{1,0:T(8,128)(2,1)}, f32[512,1]{1,0:T(8,128)}, f32[4,8,144,1]{3,2,1,0:T(8,128)}, bf16[4,8,144,1024]...) custom-call(s32[2]{0:T(128)} %lengths.7, ...), custom_call_target="tpu_custom_call" | custom-call | flops 10000000000 | bytes 104857600 | tf_op jit(solution)/shard_map/pallas_call | solution.py:1090
  181.4 0.0 all-gather.5.cloned.1.call-done
  181.4 50.4 %shard_map.234 = (bf16[8,144,1024]{2,1,0:T(8,128)(2,1)}, bf16[8,144,1152]{2,1,0:T(8,128)(2,1)}, bf16[4,2,8,3,128,128]{5,4,3,2,1,0:T(8,128)(2,1)}, bf16[8,3,128,1...) custom-call(bf16[4,8,144,1024]{3,2,1,0:T(8,128)(2,1)} %get-tuple-element.102.x_hbm, ...), custom_call_target="tpu_custom_call" | custom-call | flops 10000000000 | bytes 20971520 | tf_op jit(solution)/shard_map/pallas_call | solution.py:1119
  231.8 35.5 %shard_map.235 = (bf16[8,144,1024]{2,1,0:T(8,128)(2,1)}, bf16[8,144,1152]{2,1,0:T(8,128)(2,1)}, bf16[4,2,8,3,128,128]{5,4,3,2,1,0:T(8,128)(2,1)}, bf16[8,3,128,1...) custom-call(bf16[4,8,144,1024]{3,2,1,0:T(8,128)(2,1)} %get-tuple-element.102.x_hbm, ...), custom_call_target="tpu_custom_call", output_to_operand_aliasing={{2}: (6, {})} | custom-call | flops 10000000000 | bytes 20971520 | tf_op jit(solution)/shard_map/pallas_call | solution.py:1119
  267.4 0.2 reduce-scatter.5.cloned.1.call-start
  267.6 0.0 all-gather.7.cloned.1.call-done
  267.6 17.4 %shard_map.236 = (bf16[8,144,1024]{2,1,0:T(8,128)(2,1)}, bf16[8,144,1152]{2,1,0:T(8,128)(2,1)}, bf16[4,2,8,3,128,128]{5,4,3,2,1,0:T(8,128)(2,1)}) custom-call(bf16[4,8,144,1024]{3,2,1,0:T(8,128)(2,1)} %get-tuple-element.102.x_hbm, bf16[4,8,144,1024]{3,2,1,0:T(8,128)(2,1)} %get-tuple-element.85.g_hbm, f32[4,8,144,1]{3,2,1,0:T(8,128)} %get-tuple-element.86.gates_hbm, ...), custom_call_target="tpu_custom_call" | custom-call | flops 10000000000 | bytes 20971520 | tf_op jit(solution)/shard_map/pallas_call | solution.py:1119
  285.0 17.8 %shard_map.237 = (bf16[8,144,1024]{2,1,0:T(8,128)(2,1)}, bf16[8,144,1152]{2,1,0:T(8,128)(2,1)}, bf16[4,2,8,3,128,128]{5,4,3,2,1,0:T(8,128)(2,1)}) custom-call(bf16[4,8,144,1024]{3,2,1,0:T(8,128)(2,1)} %get-tuple-element.102.x_hbm, bf16[4,8,144,1024]{3,2,1,0:T(8,128)(2,1)} %get-tuple-element.85.g_hbm, ...), custom_call_target="tpu_custom_call", output_to_operand_aliasing={{2}: (10, {})} | custom-call | flops 10000000000 | bytes 20971520 | tf_op jit(solution)/shard_map/pallas_call | solution.py:1119
  302.8 0.0 reduce-scatter.5.cloned.1.call-update
  302.8 59.2 %shard_map.238 = (f32[512,1024]{1,0:T(8,128)}, bf16[1024,1024]{1,0:T(8,128)(2,1)}, f32[32,1024]{1,0:T(8,128)}, f32[1,1024]{1,0:T(1,128)}, bf16[4,512,1024]{2,1,0:T(8,128)(2,1)}) custom-call(bf16[8,144,1152]{2,1,0:T(8,128)(2,1)} %get-tuple-element.90.refs_0_, bf16[8,144,1152]{2,1,0:T(8,128)(2,1)} %get-tuple-element.96.refs_1_, ...), custom_call_target="tpu_custom_call" | custom-call | flops 10000000000 | bytes 104857600 | tf_op jit(solution)/shard_map/pallas_call | solution.py:1148
  362.0 5.1 all-to-all-start
  367.1 30.6 %shard_map.239 = (bf16[2,8,128,768]{3,2,1,0:T(8,128)(2,1)}, bf16[512,1024]{1,0:T(8,128)(2,1)}, bf16[512,1024]{1,0:T(8,128)(2,1)}) custom-call(s32[2]{0:T(128)} %lengths.7, bf16[1024,1024]{1,0:T(8,128)(2,1)} %get-tuple-element.75.rows, bf16[1024,1024]{1,0:T(8,128)(2,1)} %get-tuple-element.112.gb_ref, bf16[2,8,128,768]{3,2,1,0:T(8,128)(2,1)} %get-tuple-element.76.w, ...), custom_call_target="tpu_custom_call" | custom-call | flops 24999999488 | bytes 25165824 | tf_op jit(solution)/shard_map/pallas_call | solution.py:1173
  397.7 17.3 %all-to-all-done = bf16[4,512,1024]{2,1,0:T(8,128)(2,1)} async-done(((bf16[4,512,1024]{2,1,0:T(8,128)(2,1)}), bf16[4,512,1024]{2,1,0:T(8,128)(2,1)}, u32[]{:S(2)}, u32[]{:S(2)}) %all-to-all-start) | async-done | bytes 4194336 | tf_op jit(solution)/shard_map/all_to_all | solution.py:1170
  415.0 3.7 convert_reduce_fusion
  418.6 1.3 add_convert_fusion
  420.0 58.4 %shard_map.240 = (bf16[512,1024]{1,0:T(8,128)(2,1)}, f32[1024,32]{1,0:T(8,128)}, f32[8,1024]{1,0:T(8,128)}, bf16[4,128,768]{2,1,0:T(8,128)(2,1)}, bf16[2,8,3,128,128]{4,3,2,1,0:T(8,128)(2,1)}) custom-call(bf16[512,1024]{1,0:T(8,128)(2,1)} %tokens.4, bf16[512,1024]{1,0:T(8,128)(2,1)} %get-tuple-element.118.keep, bf16[512,1024]{1,0:T(8,128)(2,1)} %get-tuple-element.119.send, ...), custom_call_target="tpu_custom_call" | custom-call | flops 100000000 | bytes 31457280 | tf_op jit(solution)/shard_map/pallas_call | solution.py:1195
  478.4 2.0 copy.43
  480.4 1.4 fusion.1
  481.8 9.4 %reduce-scatter.5.cloned.1.call-done = bf16[1,2,8,3,128,128]{5,4,3,2,1,0:T(8,128)(2,1)} async-done(((bf16[4,2,8,3,128,128]{5,4,3,2,1,0:T(8,128)(2,1)}), bf16[1,2,8,3,128,128]{5,4,3,2,1,0:T(8,128)(2,1)}) %reduce-scatter.5.cloned.1.call-update) | async-done | bytes 1572880 | tf_op jit(solution)/shard_map/reduce_scatter | solution.py:1190
  491.2 28.0 %shard_map.241 = (f32[128,256]{1,0:T(8,128)}, f32[128,2,128]{2,1,0:T(2,128)}, f32[128,256]{1,0:T(8,128)}, f32[4096,128]{1,0:T(8,128)}, f32[4096,128]{1,0:T(8,128)}, /*index=5*/f32[4096,128]{1,0:T(8,128)}) custom-call(bf16[4,128,768]{2,1,0:T(8,128)(2,1)} %get-tuple-element.127.plane, bf16[2,8,3,128,128]{4,3,2,1,0:T(8,128)(2,1)} %get-tuple-element.128.back_first, ...), custom_call_target="tpu_custom_call" | custom-call | flops 100000000 | bytes 31457280 | tf_op jit(solution)/shard_map/pallas_call | solution.py:1217
  519.2 1.0 copy.57
  520.1 1.7 copy.58
  521.9 1.6 copy.59
  523.4 0.7 copy.60
  524.1 1.3 copy.61
  525.4 1.3 copy.62
  526.7 1.0 copy-done.1
  527.8 1.3 copy.63
  (29 shorter events, 0.1 us)
Async XLA Ops:
  7.2 2.8 copy-start.4
  7.2 3.3 copy-start.5
  7.2 174.2 %all-gather.5.cloned.1.call-start = ((), (), s32[]{:S(2)}) async-start(), calls=%async_computation.5 | async-start | bytes 7864320 | tf_op jit(solution)/shard_map/all_gather | solution.py:70
  10.9 2.0 copy-start.9
  10.9 2.0 copy-start.10
  12.9 26.1 %copy-start.8 = (bf16[1024,32]{0,1:T(8,128)(2,1)S(1)}, bf16[1024,32]{0,1:T(8,128)(2,1)}, u32[]{:S(2)}) copy-start(bf16[1024,32]{0,1:T(8,128)(2,1)} %param.23) | copy-start | bytes 196612
  38.9 228.7 %all-gather.7.cloned.1.call-start = ((), (), s32[]{:S(2)}) async-start(), calls=%async_computation.6 | async-start | bytes 3932160 | tf_op jit(solution)/shard_map/all_gather | solution.py:70
  39.8 57.9 %copy-start.11 = (bf16[512,1024]{1,0:T(8,128)(2,1)S(1)}, bf16[512,1024]{1,0:T(8,128)(2,1)}, u32[]{:S(2)}) copy-start(bf16[512,1024]{1,0:T(8,128)(2,1)} %refs_13_.1) | copy-start | bytes 3145732
  97.2 322.8 %reduce-scatter.3.cloned.1.call-start = ((), (), s32[]{:S(2)}) async-start(), calls=%async_computation.3 | async-start | bytes 7864320 | tf_op jit(solution)/shard_map/reduce_scatter | solution.py:1190
  97.7 24.8 %collective-permute-start.1 = (bf16[512,1024]{1,0:T(8,128)(2,1)S(1)}, bf16[512,1024]{1,0:T(8,128)(2,1)S(1)}, u32[]{:S(2)}, u32[]{:S(2)}) collective-permute-start(bf16[512,1024]{1,0:T(8,128)(2,1)S(1)} %copy-done.11), channel_id=1, source_target_pairs={{0,4},{1,5},{2,6},{3,7},{4,0},{5,1},{6,2},{7,3},{8,12},{9,13},{10,... | collective-permute-start | bytes 3145736 | tf_op jit(solution)/shard_map/ppermute | solution.py:50
  98.7 24.5 %collective-permute-start = (bf16[512,1024]{1,0:T(8,128)(2,1)S(1)}, bf16[512,1024]{1,0:T(8,128)(2,1)S(1)}, u32[]{:S(2)}, u32[]{:S(2)}) collective-permute-start(bf16[512,1024]{1,0:T(8,128)(2,1)S(1)} %copy-done.11), channel_id=1, source_target_pairs={{0,2},{1,3},{2,0},{3,1},{4,6},{5,7},{6,4},{7,5},{8,10},{9,11},{10,... | collective-permute-start | bytes 3145736 | tf_op jit(solution)/shard_map/ppermute | solution.py:50
  122.5 1.0 copy-start.12
  123.2 1.0 copy-start.13
  267.4 223.8 %reduce-scatter.5.cloned.1.call-start = ((), (), s32[]{:S(2)}) async-start(), calls=%async_computation.4 | async-start | bytes 7864320 | tf_op jit(solution)/shard_map/reduce_scatter | solution.py:1190
  362.0 53.0 %all-to-all-start = ((bf16[4,512,1024]{2,1,0:T(8,128)(2,1)}), bf16[4,512,1024]{2,1,0:T(8,128)(2,1)}, u32[]{:S(2)}, u32[]{:S(2)}) async-start(bf16[4,512,1024]{2,1,0:T(8,128)(2,1)} %get-tuple-element.110), calls=%async_computation | async-start | bytes 8388608 | tf_op jit(solution)/shard_map/all_to_all | solution.py:1170
  397.7 21.0 %copy-start = (f32[512,1024]{1,0:T(8,128)S(1)}, f32[512,1024]{1,0:T(8,128)}, u32[]{:S(2)}) copy-start(f32[512,1024]{1,0:T(8,128)} %get-tuple-element.83.refs_11_) | copy-start | bytes 6291460
  478.4 40.8 %copy-start.6 = (bf16[512,1024]{1,0:T(8,128)(2,1)S(1)}, bf16[512,1024]{1,0:T(8,128)(2,1)}, u32[]{:S(2)}) copy-start(bf16[512,1024]{1,0:T(8,128)(2,1)} %get-tuple-element.177) | copy-start | bytes 3145732
  519.1 4.3 copy-start.7
  519.2 4.9 copy-start.3
  520.1 5.3 copy-start.2
  525.4 2.3 copy-start.1
Sparse Core Ops, SparseCore 0:
  39.1 127.6 all-gather.4
  168.3 82.2 all-gather.6
  267.5 109.3 reduce-scatter.2
  379.0 112.1 reduce-scatter.4

commit v6 on v5

--- a/solution.py
+++ b/solution.py
@@ -1009,10 +1009,13 @@
 
     quarter = hidden // nt
 
-    def for_plane(w):
-        return jnp.transpose(w.reshape(deep, 8, local, quarter), (1, 2, 0, 3))
-
-    w_send = jnp.stack([for_plane(w_gate), for_plane(w_up), for_plane(w_down)], axis=2)
+    def for_plane(weights, first):
+        parts = [
+            jnp.transpose(w.reshape(deep, 8, local, quarter)[:, :, first:first + 2], (1, 2, 0, 3)) for w in weights
+        ]
+        return jnp.stack(parts, axis=2)
+
+    w_send = for_plane((w_gate, w_up, w_down), 0)
     q_cols, kv_cols = w_query.shape[1], w_keyvalue.shape[2]
     cut = q_cols + 2 * kv_cols
     w_mine = jnp.concatenate([w_query, w_keyvalue[:, 0], w_keyvalue[:, 1], w_out], axis=1)
@@ -1031,7 +1034,8 @@
         ),
         cost_estimate=pl.CostEstimate(flops=10**6, bytes_accessed=20 * 2**20, transcendentals=0),
     )(w_send, w_mine)
-    later = tuple(range(2, local))
+    later = (0, 1)
+    w_late = for_plane([after(w, line) for w in (w_gate, w_up, w_down)], 2)
     normed_rows, w_attn, ranks, router_t, dealt_third, dealt_last = pl.pallas_call(
         functools.partial(gather_kernel, later),
         out_shape=[
@@ -1048,7 +1052,7 @@
             vmem_limit_bytes=VMEM_LIMIT, collective_id=0, has_side_effects=True
         ),
         cost_estimate=pl.CostEstimate(flops=10**7, bytes_accessed=100 * 2**20, transcendentals=0),
-    )(lengths, tokens, gain_attn[None, :], routes.T, w_router, line, w_send)
+    )(lengths, tokens, gain_attn[None, :], routes.T, w_router, line, w_late)
 
     w_pair = gather_weights(dealt_pair, with_place)
     w_third = gather_weights(dealt_third, with_place)

time: 540 us -> 541 us (level)
    unnamed x40 -> x44, local copies, waits for them, and re-layouts: 16.2 us -> 16.9 us
where the time goes in v6:
time: 541 us; the launch traced here: 536 us
  Pallas kernels  454 us (84%)
  waiting for transfers between devices  30 us (6%)
  local copies, waits for them, and re-layouts  20.9 us (4%)
  between operations  14.5 us (3%)
  starting transfers between devices  8.35 us (2%)
  other arithmetic  8.27 us (2%)
    pallas_call x4, Pallas kernels, shards(): pl.pallas_call(functools.partial(expert_kernel, e, local, len(sources), s...  118 us
    pallas_call x1, Pallas kernels, shards(): remote_call(functools.partial(return_kernel, local, cap), 3, [sds((rows,...  59.2 us
    pallas_call x1, Pallas kernels, shards(): remote_call(tail_kernel, 8, [sds((rows, width), bf16), sds((width, expert...  58.5 us
    pallas_call x1, Pallas kernels, shards(): pl.pallas_call(functools.partial(gather_kernel, later), out_shape=[sds((2...  57.2 us
    pallas_call x1, Pallas kernels, shards(): remote_call(functools.partial(mix_kernel, local, cap, int(by_steps)), 2,...  57.1 us
    pallas_call x1, Pallas kernels, shards(): call(attend_back_kernel, [sds((2, nd, deep, cut + q_cols), bf16), sds((ro...  30.6 us
    pallas_call x1, Pallas kernels, shards(): remote_call(last_kernel, 9, [sds((deep, q_cols), f32), sds((deep, 2, kv_c...  27.9 us
    pallas_call x1, Pallas kernels, shards(): pl.pallas_call(deal_kernel, out_shape=[sds((2,) + dealt_shape.shape, bf16...  25.4 us
  transfers between devices with their start and end apart: 7, of which 4 were waited for; matrix products, arithmetic and copies ran while one was open for 2% of the time, Pallas kernels for 75%

profile of v6, /device:TPU:0, one launch (start us, length us, event | category | flops | bytes accessed | tf_op | source)
XLA Modules:
  0.0 536.3 jit_solution(14422690709030737454)
XLA Ops:
  7.2 1.1 fusion
  8.3 1.6 copy.39
  10.0 0.4 copy.40
  10.4 0.7 copy-done.2
  11.2 0.4 copy.41
  11.7 1.3 pad_maximum_fusion.w_send
  13.1 0.7 pad_maximum_fusion.2.w_mine
  13.7 25.4 %shard_map.230 = (bf16[2,8,3,128,128]{4,3,2,1,0:T(8,128)(2,1)}, bf16[4,128,768]{2,1,0:T(8,128)(2,1)}) custom-call(bf16[8,2,3,128,128]{4,3,2,1,0:T(8,128)(2,1)} %pad_maximum_fusion.w_send, bf16[128,768]{1,0:T(8,128)(2,1)} %pad_maximum_fusion.2.w_mine), custom_call_target="tpu_custom_call" | custom-call | flops 1000000 | bytes 20971520 | tf_op jit(solution)/shard_map/pallas_call | solution.py:1027
  39.2 0.8 copy.47.router.refs_14_
  40.0 0.4 copy.44
  40.5 0.4 copy.45
  40.9 0.4 copy.46
  41.4 1.3 pad_maximum_fusion.1.w_send
  42.7 57.2 %shard_map.231 = (bf16[1024,1024]{1,0:T(8,128)(2,1)}, bf16[2,8,128,768]{3,2,1,0:T(8,128)(2,1)}, bf16[2,4,64,512]{3,2,1,0:T(8,128)(2,1)}, bf16[64,1024]{1,0:T(8,1...) custom-call(s32[2]{0:T(128)} %lengths.7, bf16[512,1024]{1,0:T(8,128)(2,1)} %tokens.4, ...), custom_call_target="tpu_custom_call" | custom-call | flops 10000000 | bytes 104857600 | tf_op jit(solution)/shard_map/pallas_call | solution.py:1039
  100.0 0.5 reduce-scatter.3.cloned.1.call-start
  100.5 1.0 collective-permute-start.1
  101.5 1.5 collective-permute-start
  103.0 19.9 %shard_map.232 = (bf16[1024,512]{1,0:T(8,128)(2,1)}, bf16[1024,256]{1,0:T(8,128)(2,1)}, bf16[1024,256]{1,0:T(8,128)(2,1)}, bf16[1024,512]{1,0:T(8,128)(2,1)}, f3...) custom-call(s32[2]{0:T(128)} %lengths.7, bf16[1024,1024]{1,0:T(8,128)(2,1)} %get-tuple-element.81.rows, ...), custom_call_target="tpu_custom_call" | custom-call | flops 12000000000 | bytes 16777216 | tf_op jit(solution)/shard_map/pallas_call | solution.py:1072
  122.9 2.4 collective-permute-done.1.out_x
  125.3 0.7 collective-permute-done.out_y
  126.1 0.2 copy-done.14
  126.3 0.7 copy-done.15
  127.0 57.1 %shard_map.233 = (f32[512,1024]{1,0:T(8,128)}, bf16[512,1024]{1,0:T(8,128)(2,1)}, f32[512,1]{1,0:T(8,128)}, f32[4,8,144,1]{3,2,1,0:T(8,128)}, bf16[4,8,144,1024]...) custom-call(s32[2]{0:T(128)} %lengths.7, ...), custom_call_target="tpu_custom_call" | custom-call | flops 10000000000 | bytes 104857600 | tf_op jit(solution)/shard_map/pallas_call | solution.py:1094
  184.2 50.3 %shard_map.234 = (bf16[8,144,1024]{2,1,0:T(8,128)(2,1)}, bf16[8,144,1152]{2,1,0:T(8,128)(2,1)}, bf16[4,2,8,3,128,128]{5,4,3,2,1,0:T(8,128)(2,1)}, bf16[8,3,128,1...) custom-call(bf16[4,8,144,1024]{3,2,1,0:T(8,128)(2,1)} %get-tuple-element.108.x_hbm, ...), custom_call_target="tpu_custom_call" | custom-call | flops 10000000000 | bytes 20971520 | tf_op jit(solution)/shard_map/pallas_call | solution.py:1123
  234.5 33.0 %shard_map.235 = (bf16[8,144,1024]{2,1,0:T(8,128)(2,1)}, bf16[8,144,1152]{2,1,0:T(8,128)(2,1)}, bf16[4,2,8,3,128,128]{5,4,3,2,1,0:T(8,128)(2,1)}, bf16[8,3,128,1...) custom-call(bf16[4,8,144,1024]{3,2,1,0:T(8,128)(2,1)} %get-tuple-element.108.x_hbm, ...), custom_call_target="tpu_custom_call", output_to_operand_aliasing={{2}: (6, {})} | custom-call | flops 10000000000 | bytes 20971520 | tf_op jit(solution)/shard_map/pallas_call | solution.py:1123
  267.6 0.2 reduce-scatter.5.cloned.1.call-start
  267.8 17.3 %shard_map.236 = (bf16[8,144,1024]{2,1,0:T(8,128)(2,1)}, bf16[8,144,1152]{2,1,0:T(8,128)(2,1)}, bf16[4,2,8,3,128,128]{5,4,3,2,1,0:T(8,128)(2,1)}) custom-call(bf16[4,8,144,1024]{3,2,1,0:T(8,128)(2,1)} %get-tuple-element.108.x_hbm, bf16[4,8,144,1024]{3,2,1,0:T(8,128)(2,1)} %get-tuple-element.91.g_hbm, f32[4,8,144,1]{3,2,1,0:T(8,128)} %get-tuple-element.92.gates_hbm, ...), custom_call_target="tpu_custom_call" | custom-call | flops 10000000000 | bytes 20971520 | tf_op jit(solution)/shard_map/pallas_call | solution.py:1123
  285.2 17.7 %shard_map.237 = (bf16[8,144,1024]{2,1,0:T(8,128)(2,1)}, bf16[8,144,1152]{2,1,0:T(8,128)(2,1)}, bf16[4,2,8,3,128,128]{5,4,3,2,1,0:T(8,128)(2,1)}) custom-call(bf16[4,8,144,1024]{3,2,1,0:T(8,128)(2,1)} %get-tuple-element.108.x_hbm, bf16[4,8,144,1024]{3,2,1,0:T(8,128)(2,1)} %get-tuple-element.91.g_hbm, ...), custom_call_target="tpu_custom_call", output_to_operand_aliasing={{2}: (10, {})} | custom-call | flops 10000000000 | bytes 20971520 | tf_op jit(solution)/shard_map/pallas_call | solution.py:1123
  302.9 59.2 %shard_map.238 = (f32[512,1024]{1,0:T(8,128)}, bf16[1024,1024]{1,0:T(8,128)(2,1)}, f32[32,1024]{1,0:T(8,128)}, f32[1,1024]{1,0:T(1,128)}, bf16[4,512,1024]{2,1,0:T(8,128)(2,1)}) custom-call(bf16[8,144,1152]{2,1,0:T(8,128)(2,1)} %get-tuple-element.96.refs_0_, bf16[8,144,1152]{2,1,0:T(8,128)(2,1)} %get-tuple-element.102.refs_1_, ...), custom_call_target="tpu_custom_call" | custom-call | flops 10000000000 | bytes 104857600 | tf_op jit(solution)/shard_map/pallas_call | solution.py:1152
  362.1 5.1 all-to-all-start
  367.2 30.6 %shard_map.239 = (bf16[2,8,128,768]{3,2,1,0:T(8,128)(2,1)}, bf16[512,1024]{1,0:T(8,128)(2,1)}, bf16[512,1024]{1,0:T(8,128)(2,1)}) custom-call(s32[2]{0:T(128)} %lengths.7, bf16[1024,1024]{1,0:T(8,128)(2,1)} %get-tuple-element.81.rows, bf16[1024,1024]{1,0:T(8,128)(2,1)} %get-tuple-element.118.gb_ref, bf16[2,8,128,768]{3,2,1,0:T(8,128)(2,1)} %get-tuple-element.82.w, ...), custom_call_target="tpu_custom_call" | custom-call | flops 24999999488 | bytes 25165824 | tf_op jit(solution)/shard_map/pallas_call | solution.py:1177
  397.8 17.3 %all-to-all-done = bf16[4,512,1024]{2,1,0:T(8,128)(2,1)} async-done(((bf16[4,512,1024]{2,1,0:T(8,128)(2,1)}), bf16[4,512,1024]{2,1,0:T(8,128)(2,1)}, u32[]{:S(2)}, u32[]{:S(2)}) %all-to-all-start) | async-done | bytes 4194336 | tf_op jit(solution)/shard_map/all_to_all | solution.py:1174
  415.1 3.7 convert_reduce_fusion
  418.8 1.3 add_convert_fusion
  420.1 58.5 %shard_map.240 = (bf16[512,1024]{1,0:T(8,128)(2,1)}, f32[1024,32]{1,0:T(8,128)}, f32[8,1024]{1,0:T(8,128)}, bf16[4,128,768]{2,1,0:T(8,128)(2,1)}, bf16[2,8,3,128,128]{4,3,2,1,0:T(8,128)(2,1)}) custom-call(bf16[512,1024]{1,0:T(8,128)(2,1)} %tokens.4, bf16[512,1024]{1,0:T(8,128)(2,1)} %get-tuple-element.124.keep, bf16[512,1024]{1,0:T(8,128)(2,1)} %get-tuple-element.125.send, ...), custom_call_target="tpu_custom_call" | custom-call | flops 100000000 | bytes 31457280 | tf_op jit(solution)/shard_map/pallas_call | solution.py:1199
  478.6 1.9 copy.49
  480.4 1.5 fusion.1
  481.9 9.5 %reduce-scatter.5.cloned.1.call-done = bf16[1,2,8,3,128,128]{5,4,3,2,1,0:T(8,128)(2,1)} async-done(((bf16[4,2,8,3,128,128]{5,4,3,2,1,0:T(8,128)(2,1)}), bf16[1,2,8,3,128,128]{5,4,3,2,1,0:T(8,128)(2,1)}) %reduce-scatter.5.cloned.1.call-update) | async-done | bytes 1572880 | tf_op jit(solution)/shard_map/reduce_scatter | solution.py:1194
  491.4 27.9 %shard_map.241 = (f32[128,256]{1,0:T(8,128)}, f32[128,2,128]{2,1,0:T(2,128)}, f32[128,256]{1,0:T(8,128)}, f32[4096,128]{1,0:T(8,128)}, f32[4096,128]{1,0:T(8,128)}, /*index=5*/f32[4096,128]{1,0:T(8,128)}) custom-call(bf16[4,128,768]{2,1,0:T(8,128)(2,1)} %get-tuple-element.133.plane, bf16[2,8,3,128,128]{4,3,2,1,0:T(8,128)(2,1)} %get-tuple-element.134.back_first, ...), custom_call_target="tpu_custom_call" | custom-call | flops 100000000 | bytes 31457280 | tf_op jit(solution)/shard_map/pallas_call | solution.py:1221
  519.4 1.0 copy.63
  520.3 1.7 copy.64
  522.0 0.7 copy.65
  522.7 0.7 copy.66
  523.3 1.3 copy.67
  524.7 1.0 copy-done.5
  525.7 1.3 copy.68
  527.0 1.0 copy-done.4
  528.0 1.3 copy.69
  (42 shorter events, 0.5 us)
Async XLA Ops:
  7.2 2.8 copy-start.1
  7.2 177.0 %all-gather.5.cloned.1.call-start = ((), (), s32[]{:S(2)}) async-start(), calls=%async_computation.5 | async-start | bytes 7864320 | tf_op jit(solution)/shard_map/all_gather | solution.py:70
  9.9 1.2 copy-start.2
  11.7 1.3 copy-start.11
  11.7 1.3 copy-start.12
  13.0 26.2 %copy-start.10 = (bf16[1024,32]{0,1:T(8,128)(2,1)S(1)}, bf16[1024,32]{0,1:T(8,128)(2,1)}, u32[]{:S(2)}) copy-start(bf16[1024,32]{0,1:T(8,128)(2,1)} %param.23) | copy-start | bytes 196612
  13.0 27.0 %copy-start = (bf16[128,32,128]{2,1,0:T(8,128)(2,1)S(1)}, bf16[128,32,128]{2,1,0:T(8,128)(2,1)}, u32[]{:S(2)}) copy-start(bf16[128,32,128]{2,1,0:T(8,128)(2,1)} %param.24) | copy-start | bytes 3145732
  39.1 228.7 %all-gather.7.cloned.1.call-start = ((), (), s32[]{:S(2)}) async-start(), calls=%async_computation.6 | async-start | bytes 3932160 | tf_op jit(solution)/shard_map/all_gather | solution.py:70
  42.7 57.8 %copy-start.13 = (bf16[512,1024]{1,0:T(8,128)(2,1)S(1)}, bf16[512,1024]{1,0:T(8,128)(2,1)}, u32[]{:S(2)}) copy-start(bf16[512,1024]{1,0:T(8,128)(2,1)} %refs_13_.1) | copy-start | bytes 3145732
  100.0 320.1 %reduce-scatter.3.cloned.1.call-start = ((), (), s32[]{:S(2)}) async-start(), calls=%async_computation.3 | async-start | bytes 7864320 | tf_op jit(solution)/shard_map/reduce_scatter | solution.py:1194
  100.5 24.8 %collective-permute-start.1 = (bf16[512,1024]{1,0:T(8,128)(2,1)S(1)}, bf16[512,1024]{1,0:T(8,128)(2,1)S(1)}, u32[]{:S(2)}, u32[]{:S(2)}) collective-permute-start(bf16[512,1024]{1,0:T(8,128)(2,1)S(1)} %copy-done.13), channel_id=1, source_target_pairs={{0,4},{1,5},{2,6},{3,7},{4,0},{5,1},{6,2},{7,3},{8,12},{9,13},{10,... | collective-permute-start | bytes 3145736 | tf_op jit(solution)/shard_map/ppermute | solution.py:50
  101.5 24.5 %collective-permute-start = (bf16[512,1024]{1,0:T(8,128)(2,1)S(1)}, bf16[512,1024]{1,0:T(8,128)(2,1)S(1)}, u32[]{:S(2)}, u32[]{:S(2)}) collective-permute-start(bf16[512,1024]{1,0:T(8,128)(2,1)S(1)} %copy-done.13), channel_id=1, source_target_pairs={{0,2},{1,3},{2,0},{3,1},{4,6},{5,7},{6,4},{7,5},{8,10},{9,11},{10,... | collective-permute-start | bytes 3145736 | tf_op jit(solution)/shard_map/ppermute | solution.py:50
  125.3 1.0 copy-start.14
  126.1 1.0 copy-start.15
  267.6 223.8 %reduce-scatter.5.cloned.1.call-start = ((), (), s32[]{:S(2)}) async-start(), calls=%async_computation.4 | async-start | bytes 7864320 | tf_op jit(solution)/shard_map/reduce_scatter | solution.py:1194
  362.1 53.0 %all-to-all-start = ((bf16[4,512,1024]{2,1,0:T(8,128)(2,1)}), bf16[4,512,1024]{2,1,0:T(8,128)(2,1)}, u32[]{:S(2)}, u32[]{:S(2)}) async-start(bf16[4,512,1024]{2,1,0:T(8,128)(2,1)} %get-tuple-element.116), calls=%async_computation | async-start | bytes 8388608 | tf_op jit(solution)/shard_map/all_to_all | solution.py:1174
  397.8 21.0 %copy-start.3 = (f32[512,1024]{1,0:T(8,128)S(1)}, f32[512,1024]{1,0:T(8,128)}, u32[]{:S(2)}) copy-start(f32[512,1024]{1,0:T(8,128)} %get-tuple-element.89.refs_11_) | copy-start | bytes 6291460
  480.4 38.9 %copy-start.7 = (bf16[512,1024]{1,0:T(8,128)(2,1)S(1)}, bf16[512,1024]{1,0:T(8,128)(2,1)}, u32[]{:S(2)}) copy-start(bf16[512,1024]{1,0:T(8,128)(2,1)} %get-tuple-element.185) | copy-start | bytes 3145732
  519.3 2.7 copy-start.9
  519.3 3.4 copy-start.8
  519.3 4.0 copy-start.6
  523.3 2.3 copy-start.5
  525.7 2.3 copy-start.4
Sparse Core Ops, SparseCore 0:
  39.3 127.6 all-gather.4
  168.5 82.3 all-gather.6
  267.7 109.2 reduce-scatter.2
  379.2 112.1 reduce-scatter.4
